TPU v7x, 512 devices: a whole 4x8x8 slice. The times are simulated.
512 devices in a mesh: col: 8 (over z_hi, core), row: 64 (over z_lo, y, x).
Axes of the slice: x: 4, y: 8, z: 8 (z_hi: 4, z_lo: 2; z = z_hi * 2 + z_lo), core: 2. Of those that a mesh axis runs over, the one named last changes fastest.
Arguments:
- matrix: float32 [16384, 4096], P('row', 'col'), may hold values from -100 to 100
- seats: int32 [16], replicated, may hold values from 0 to 15, each once
Outputs:
- rotated: float32 [16384, 4096], P('row', 'col')
- mean_squares: float32 [4096], P('col')
All inputs are finite; a program needn't handle non-finite values.
Results may differ from a plain program's by a relative error of at most 0.0003.
Values sent between devices are 32-bit elements; how exact they have to be, the bound alone decides.
No kernel may reach another device: no remote copies, remote signals or barrier semaphores. Data moves between devices by JAX's collectives and lax.ppermute only.
A program may use at most 64 MiB of HBM per device.

v0:
```python
import jax
import jax.numpy as jnp
from jax import lax
from jax.sharding import PartitionSpec as P

HIGH = lax.Precision.HIGHEST


def passed_along(block, axis, distance):
    devices = range(lax.axis_size(axis))
    route = [((i - distance) % len(devices), i) for i in devices]
    return lax.ppermute(block, axis, route)


def mat(a, b):
    return jnp.dot(a, b, precision=HIGH, preferred_element_type=jnp.float32)


def inner(a, b):
    return lax.dot_general(
        a, b, (((0,), (0,)), ((), ())), precision=HIGH, preferred_element_type=jnp.float32
    )


def batch_inner(a, b):
    return lax.dot_general(
        a, b, (((1,), (1,)), ((0,), (0,))), precision=HIGH, preferred_element_type=jnp.float32
    )


def root_poly(square):
    eye = jnp.eye(square.shape[0], dtype=jnp.float32)
    first = 1.5 * eye - 0.5 * square
    ystep = mat(square, first)
    second = 1.5 * eye - 0.5 * mat(first, ystep)
    return mat(second, first)


def couplings(lefts, rights, total_rows):
    cross, sum_left, sum_right = lax.psum(
        (
            batch_inner(lefts, rights),
            jnp.sum(lefts * lefts, axis=1),
            jnp.sum(rights * rights, axis=1),
        ),
        "row",
    )
    mean_left = sum_left / total_rows
    mean_right = sum_right / total_rows
    return (
        0.5
        * (cross / total_rows)
        / jnp.sqrt((mean_left[:, :, None] + 1e-06) * (mean_right[:, None, :] + 1e-06))
    )


def left_part(left, right, coupling):
    eye = jnp.eye(coupling.shape[0], dtype=jnp.float32)
    zleft = root_poly(eye + mat(coupling, coupling.T))
    return mat(
        left
        - lax.dot_general(
            right,
            coupling,
            (((1,), (1,)), ((), ())),
            precision=HIGH,
            preferred_element_type=jnp.float32,
        ),
        zleft,
    )


def right_part(left, right, coupling):
    eye = jnp.eye(coupling.shape[0], dtype=jnp.float32)
    zright = root_poly(eye + inner(coupling, coupling))
    return mat(right + mat(left, coupling), zright)


def pair_update(left, right, total_rows):
    coupling = couplings(left[None], right[None], total_rows)[0]
    return (left_part(left, right, coupling), right_part(left, right, coupling))


def on_device(matrix, seats):
    width = matrix.shape[1] // 2
    total_rows = matrix.shape[0] * lax.axis_size("row")
    top = matrix[:, :width]
    bottom = matrix[:, width:]
    top, bottom = pair_update(top, bottom, total_rows)
    top = passed_along(top, "col", 1)
    bottom = passed_along(bottom, "col", -1)
    top, bottom = pair_update(top, bottom, total_rows)
    top = passed_along(top, "col", -1)
    bottom = passed_along(bottom, "col", 1)
    final = jnp.concatenate([top, bottom], axis=1)
    totals = lax.psum(jnp.sum(final * final, axis=0), "row") / total_rows
    table = lax.all_gather(totals.reshape(2, width), "col", axis=0, tiled=True)
    wanted = 2 * lax.axis_index("col") + jnp.arange(2, dtype=jnp.int32)
    select = (seats[None, :] == wanted[:, None]).astype(jnp.float32)
    picked = mat(select, table)
    return (final, picked.reshape(2 * width))


def solution(mesh):
    placed = (P("row", "col"), P())
    return jax.shard_map(
        on_device,
        mesh=mesh,
        in_specs=placed,
        out_specs=(P("row", "col"), P("col")),
        check_vma=False,
    )
```

profile of v0, /device:TPU:1, one launch (start us, length us, event | category | flops | bytes accessed | tf_op | source)
XLA Modules:
  0.0 1350.2 jit_solution(11622088123836080981)
XLA Ops:
  7.2 0.0 copy-start
  7.2 0.0 all-reduce.5.cloned.1.call-start
  7.2 2.4 convolution_bitcast_fusion.3
  9.6 0.0 all-reduce.5.cloned.1.call-update
  9.6 0.0 all-reduce.7.cloned.1.call-start
  9.7 0.0 copy-done
  9.7 0.1 multiply_reduce_fusion.4
  9.7 134.9 %all-reduce.1 = (f32[1,256]{1,0:T(1,128)S(1)}, f32[1,256]{1,0:T(1,128)S(1)}) all-reduce(f32[1,256]{1,0:T(1,128)S(1)} %bitcast.83, f32[1,256]{1,0:T(1,128)S(1)} %bitcast.82), channel_id=1, replica_groups=mesh['col'=8,'row'=64] {'row'}, use_global_device_ids=true, to_apply=%region_4.0 | all-reduce | flops 512 | bytes 4096 | tf_op jit(solution)/shard_map/psum | solution.py:40
  144.7 399.6 %all-reduce.5.cloned.1.call-done = f32[1,256,256]{2,1,0:T(8,128)} async-done(((f32[1,256,256]{2,1,0:T(8,128)}), f32[1,256,256]{2,1,0:T(8,128)}) %all-reduce.5.cloned.1.call-update) | async-done | bytes 262160 | tf_op jit(solution)/shard_map/psum | solution.py:40
  544.3 1.7 convolution_add_fusion.3
  546.1 0.4 fusion.19
  546.5 0.4 fusion.2
  546.9 0.0 copy-start.1
  546.9 0.4 fusion.18
  547.3 0.5 copy-done.1
  547.8 0.5 fusion.3
  548.4 0.4 fusion.102
  548.7 30.6 %collective-permute-start.1 = (f32[256,256]{1,0:T(8,128)S(1)}, f32[256,256]{1,0:T(8,128)S(1)}, u32[]{:S(2)}, u32[]{:S(2)}) collective-permute-start(f32[256,256]{1,0:T(8,128)S(1)} %fusion.102), channel_id=1, source_target_pairs={{64,0},{128,64},{192,128},{256,192},{320,256},{384,320},{448,384},... | collective-permute-start | bytes 786440 | tf_op jit(solution)/shard_map/ppermute | solution.py:12
  579.3 0.5 convolution_add_fusion.4
  579.8 0.4 fusion.21
  580.2 0.4 fusion.4
  580.7 0.4 fusion.20
  581.1 0.5 fusion.5
  581.6 0.4 fusion.101
  582.0 4.2 collective-permute-start
  586.2 1.5 collective-permute-done.1
  587.7 1.9 collective-permute-done
  589.6 1.3 convolution_bitcast_fusion
  590.9 0.0 all-reduce.7.cloned.1.call-update
  590.9 0.1 multiply_reduce_fusion.1
  591.0 0.1 multiply_reduce_fusion.2
  591.0 130.9 %all-reduce = (f32[1,256]{1,0:T(1,128)S(1)}, f32[1,256]{1,0:T(1,128)S(1)}) all-reduce(f32[1,256]{1,0:T(1,128)S(1)} %bitcast.84, f32[1,256]{1,0:T(1,128)S(1)} %bitcast.85), channel_id=1, replica_groups=mesh['col'=8,'row'=64] {'row'}, use_global_device_ids=true, to_apply=%region_9.0 | all-reduce | flops 512 | bytes 4096 | tf_op jit(solution)/shard_map/psum | solution.py:40
  722.0 397.1 %all-reduce.7.cloned.1.call-done = f32[1,256,256]{2,1,0:T(8,128)} async-done(((f32[1,256,256]{2,1,0:T(8,128)}), f32[1,256,256]{2,1,0:T(8,128)}) %all-reduce.7.cloned.1.call-update) | async-done | bytes 262160 | tf_op jit(solution)/shard_map/psum | solution.py:40
  1119.1 1.7 convolution_add_fusion
  1120.8 0.4 fusion.15
  1121.2 0.4 fusion
  1121.6 0.0 copy-start.2
  1121.7 0.4 fusion.14
  1122.1 0.5 copy-done.2
  1122.6 0.5 convolution_add_fusion.2
  1123.1 0.4 fusion.17
  1123.5 0.4 fusion.1
  1123.9 0.4 fusion.16
  1124.3 0.5 convolution_subtract_fusion
  1124.8 0.4 fusion.103
  1125.2 30.6 %collective-permute-start.2 = (f32[256,256]{1,0:T(8,128)S(1)}, f32[256,256]{1,0:T(8,128)S(1)}, u32[]{:S(2)}, u32[]{:S(2)}) collective-permute-start(f32[256,256]{1,0:T(8,128)S(1)} %fusion.103), channel_id=1, source_target_pairs={{64,0},{128,64},{192,128},{256,192},{320,256},{384,320},{448,384},... | collective-permute-start | bytes 786440 | tf_op jit(solution)/shard_map/ppermute | solution.py:12
  1155.8 0.5 convolution_add_fusion.1
  1156.3 0.4 fusion.104
  1156.7 4.2 collective-permute-start.3
  1160.9 3.6 collective-permute-done.2
  1164.5 0.0 collective-permute-done.3
  1164.6 0.0 copy-start.3
  1164.6 0.1 multiply_reduce_fusion
  1164.7 129.0 %psum.55 = f32[512]{0:T(512)S(1)} all-reduce(f32[512]{0:T(512)S(1)} %multiply_reduce_fusion), channel_id=1, replica_groups=mesh['col'=8,'row'=64] {'row'}, use_global_device_ids=true, to_apply=%region_11.0 | all-reduce | flops 512 | bytes 4096 | tf_op jit(solution)/shard_map/psum | solution.py:96
  1293.7 48.3 %all-gather = f32[8,2,256]{2,1,0:T(2,128)S(1)} all-gather(f32[1,2,256]{2,1,0:T(2,128)S(1)} %reshape.175), channel_id=1, replica_groups=mesh['col'=8,'row'=64] {'col'}, dimensions={0}, use_global_device_ids=true | all-gather | bytes 18432 | tf_op jit(solution)/shard_map/all_gather | solution.py:97
  1341.9 0.0 copy-start.4
  1341.9 0.6 copy-done.4
  1342.6 0.2 convolution_bitcast_fusion.4
  1342.8 0.6 copy.4
  1343.4 0.0 copy-done.3
  (9 shorter events, 0.1 us)
Async XLA Ops:
  7.2 2.5 copy-start
  7.2 537.2 %all-reduce.5.cloned.1.call-start = ((), (), s32[]{:S(2)}) async-start(), calls=%async_computation | async-start | bytes 524288 | tf_op jit(solution)/shard_map/psum | solution.py:40
  9.6 1109.5 %all-reduce.7.cloned.1.call-start = ((), (), s32[]{:S(2)}) async-start(), calls=%async_computation.1 | async-start | bytes 524288 | tf_op jit(solution)/shard_map/psum | solution.py:40
  546.9 1.0 copy-start.1
  548.7 39.0 %collective-permute-start.1 = (f32[256,256]{1,0:T(8,128)S(1)}, f32[256,256]{1,0:T(8,128)S(1)}, u32[]{:S(2)}, u32[]{:S(2)}) collective-permute-start(f32[256,256]{1,0:T(8,128)S(1)} %fusion.102), channel_id=1, source_target_pairs={{64,0},{128,64},{192,128},{256,192},{320,256},{384,320},{448,384},... | collective-permute-start | bytes 786440 | tf_op jit(solution)/shard_map/ppermute | solution.py:12
  582.0 7.6 collective-permute-start
  1121.6 1.0 copy-start.2
  1125.2 39.3 %collective-permute-start.2 = (f32[256,256]{1,0:T(8,128)S(1)}, f32[256,256]{1,0:T(8,128)S(1)}, u32[]{:S(2)}, u32[]{:S(2)}) collective-permute-start(f32[256,256]{1,0:T(8,128)S(1)} %fusion.103), channel_id=1, source_target_pairs={{64,0},{128,64},{192,128},{256,192},{320,256},{384,320},{448,384},... | collective-permute-start | bytes 786440 | tf_op jit(solution)/shard_map/ppermute | solution.py:12
  1156.7 7.9 collective-permute-start.3
  1164.6 178.8 %copy-start.3 = (f32[256,512]{1,0:T(8,128)}, f32[256,512]{1,0:T(8,128)S(1)}, u32[]{:S(2)}) copy-start(f32[256,512]{1,0:T(8,128)S(1)} %constant_dynamic-update-slice_fusion) | copy-start | bytes 1572868
  1341.9 0.7 copy-start.4
Sparse Core Ops, SparseCore 0:
  11.5 532.8 all-reduce.4
  591.0 527.9 all-reduce.6
where the time goes:
time: 1350 us
  waiting for transfers between devices  804 us (60%)
  blocking collectives  443 us (33%)
  starting transfers between devices  69.6 us (5%)
  matrix products  16.7 us (1%)
  between operations  14.3 us (1%)
    psum x2, waiting for transfers between devices, couplings(): lax.psum((batch_inner(lefts, rights), jnp.sum(lefts * lefts, axis=1), jnp...  797 us
    psum x2, blocking collectives, couplings(): lax.psum((batch_inner(lefts, rights), jnp.sum(lefts * lefts, axis=1), jnp...  266 us
    psum x1, blocking collectives, on_device(): totals = lax.psum(jnp.sum(final * final, axis=0), 'row') / total_rows  129 us
    ppermute x4, starting transfers between devices, passed_along(): return lax.ppermute(block, axis, route)  69.5 us
    all_gather x1, blocking collectives, on_device(): table = lax.all_gather(totals.reshape(2, width), 'col', axis=0, tiled=True)  48.3 us
  transfers between devices with their start and end apart: 6, of which 5 were waited for; matrix products, arithmetic and copies ran while one was open for 0% of the time, Pallas kernels for 0%

commit v1 on v0

v1 whole, which is shorter than its diff:
```python
import jax
import jax.numpy as jnp
from jax import lax
from jax.sharding import PartitionSpec as P

PREC = lax.Precision.HIGH


def passed_along(block, axis, distance):
    devices = range(lax.axis_size(axis))
    route = [((i - distance) % len(devices), i) for i in devices]
    return lax.ppermute(block, axis, route)


def product(a, b, ca, cb):
    return lax.dot_general(
        a, b, (((ca,), (cb,)), ((), ())), precision=PREC, preferred_element_type=jnp.float32
    )


def exchange(pieces, axis):
    return lax.all_to_all(pieces, axis, 0, 0, tiled=True)


def root(s):
    eye = jnp.eye(s.shape[0], dtype=jnp.float32)
    s2 = product(s, s, 1, 0)
    return (eye - 0.5 * s + 0.375 * s2) + product(s2, 0.0625 * s2 - 0.3125 * s, 1, 0)


def couplings(left, right, total_rows):
    n = lax.axis_size("row")
    width = left.shape[1]
    cross = product(left, right, 0, 0)
    sum_left = jnp.sum(left * left, axis=0).reshape(2, 128)
    sum_right = jnp.sum(right * right, axis=0).reshape(2, 128)
    tiles = jnp.concatenate([cross[:, :128], cross[:, 128:]], axis=0).reshape(n, 1024)
    norm_left = jnp.tile(jnp.repeat(sum_left, n // 4, axis=0), (2, 1))
    norm_right = jnp.repeat(sum_right, n // 2, axis=0)
    payload = jnp.concatenate([tiles, norm_left, norm_right], axis=1)
    got = jnp.sum(exchange(payload.reshape(n, 1, 1280), "row"), axis=0).reshape(1280)
    tile = got[:1024].reshape(8, 128)
    start = 8 * (lax.axis_index("row") % 16)
    mean_left = lax.dynamic_slice(got[1024:1152], (start,), (8,)) / total_rows
    mean_right = got[1152:] / total_rows
    part = (
        0.5
        * (tile / total_rows)
        / jnp.sqrt((mean_left[:, None] + 1e-06) * (mean_right[None, :] + 1e-06))
    )
    whole = exchange(jnp.broadcast_to(part[None], (n, 8, 128)), "row").reshape(2 * width, 128)
    return jnp.concatenate([whole[:width], whole[width:]], axis=1)


def pair_update(left, right, total_rows):
    x = couplings(left, right, total_rows)
    new_left = product(
        left - product(right, x, 1, 1), root(product(x, x, 1, 1)), 1, 0
    )
    new_right = product(
        right + product(left, x, 1, 0), root(product(x, x, 0, 0)), 1, 0
    )
    return new_left, new_right


def on_device(matrix, seats):
    width = matrix.shape[1] // 2
    n, cols = lax.axis_size("row"), lax.axis_size("col")
    total_rows = matrix.shape[0] * n
    top = matrix[:, :width]
    bottom = matrix[:, width:]
    top, bottom = pair_update(top, bottom, total_rows)
    top = passed_along(top, "col", 1)
    bottom = passed_along(bottom, "col", -1)
    top, bottom = pair_update(top, bottom, total_rows)
    sums = jnp.concatenate([jnp.sum(top * top, axis=0), jnp.sum(bottom * bottom, axis=0)])
    top = passed_along(top, "col", -1)
    bottom = passed_along(bottom, "col", 1)
    final = jnp.concatenate([top, bottom], axis=1)
    sums = exchange(jnp.broadcast_to(sums.reshape(1, 4, 128), (n, 4, 128)), "row")
    means = jnp.sum(sums, axis=0) / total_rows
    table = exchange(jnp.broadcast_to(means[None], (cols, 4, 128)), "col")
    tops = jnp.roll(table[:, :2].reshape(cols, width), -1, axis=0)
    bottoms = jnp.roll(table[:, 2:].reshape(cols, width), 1, axis=0)
    by_seat = jnp.stack([tops, bottoms], axis=1).reshape(2 * cols, width)
    wanted = 2 * lax.axis_index("col") + jnp.arange(2, dtype=jnp.int32)
    hit = seats[None, :] == wanted[:, None]
    picked = jnp.sum(jnp.where(hit[:, :, None], by_seat[None], 0.0), axis=1)
    return (final, picked.reshape(2 * width))


def solution(mesh):
    placed = (P("row", "col"), P())
    return jax.shard_map(
        on_device,
        mesh=mesh,
        in_specs=placed,
        out_specs=(P("row", "col"), P("col")),
        check_vma=False,
    )
```

time: 1350 us -> 147 us (0.11)
  waiting for transfers between devices: 804 us -> 41.1 us
  blocking collectives: 443 us -> 35.2 us
  starting transfers between devices: 69.6 us -> 53.7 us
    psum x2 -> x0, waiting for transfers between devices: 797 us -> none  [couplings(): lax.psum((batch_inner(lefts, rights), jnp.sum(lefts * lefts, axis=1), jnp...]
    psum x3 -> x0, blocking collectives: 395 us -> none  [the longest x2 266 us: couplings(): lax.psum((batch_inner(lefts, rights), jnp.sum(lefts * lefts, axis=1), jnp...]
    ppermute x4, starting transfers between devices: 69.5 us -> 17.6 us  [passed_along(): return lax.ppermute(block, axis, route)]
    all_gather x1 -> x0, blocking collectives: 48.3 us -> none  [on_device(): table = lax.all_gather(totals.reshape(2, width), 'col', axis=0, tiled=True)]
    all_to_all x0 -> x4, starting transfers between devices: none -> 36.1 us  [exchange(): return lax.all_to_all(pieces, axis, 0, 0, tiled=True)]
    all_to_all x0 -> x2, blocking collectives: none -> 35.2 us  [exchange(): return lax.all_to_all(pieces, axis, 0, 0, tiled=True)]
    all_to_all x0 -> x4, waiting for transfers between devices: none -> 31.9 us  [exchange(): return lax.all_to_all(pieces, axis, 0, 0, tiled=True)]
  transfers between devices with their start and end apart: 6 -> 8, of which waited for: 5 -> 6; matrix products, arithmetic and copies ran while one was open for 0% -> 1% of each run, Pallas kernels for 0% -> 0%
where the time goes in v1:
time: 147 us; the launch traced here: 146 us
  starting transfers between devices  53.7 us (37%)
  waiting for transfers between devices  41.1 us (28%)
  blocking collectives  35.2 us (24%)
  matrix products  8.27 us (6%)
  local copies, waits for them, and re-layouts  4.34 us (3%)
  other arithmetic  2.34 us (2%)
    all_to_all x4, starting transfers between devices, exchange(): return lax.all_to_all(pieces, axis, 0, 0, tiled=True)  36.1 us
    all_to_all x2, blocking collectives, exchange(): return lax.all_to_all(pieces, axis, 0, 0, tiled=True)  35.2 us
    all_to_all x4, waiting for transfers between devices, exchange(): return lax.all_to_all(pieces, axis, 0, 0, tiled=True)  31.9 us
    ppermute x4, starting transfers between devices, passed_along(): return lax.ppermute(block, axis, route)  17.6 us
    ppermute x4, waiting for transfers between devices, passed_along(): return lax.ppermute(block, axis, route)  9.23 us
    dot_general x22, matrix products, product(): lax.dot_general(a, b, (((ca,), (cb,)), ((), ())), precision=PREC, preferr...  8.27 us
  transfers between devices with their start and end apart: 8, of which 6 were waited for; matrix products, arithmetic and copies ran while one was open for 1% of the time, Pallas kernels for 0%

profile of v1, /device:TPU:1, one launch (start us, length us, event | category | flops | bytes accessed | tf_op | source)
XLA Modules:
  0.0 146.1 jit_solution(14829721683740504984)
XLA Ops:
  0.6 1.5 %fusion.51 = f32[256,256]{1,0:T(8,128)S(1)} fusion(f32[256,512]{1,0:T(8,128)} %param.2), kind=kOutput, calls=%fused_computation.101 | convolution fusion | flops 100663296 | bytes 786432 | tf_op jit(solution)/shard_map/dot_general | solution.py:16
  2.3 0.1 copy.10
  2.4 0.1 multiply_reduce_fusion.5
  2.5 0.1 copy.11
  2.7 0.1 multiply_reduce_fusion.4
  2.9 0.9 reshape.215
  3.8 12.9 %all-to-all-start = ((f32[64,1,1280]{2,1,0:T(1,128)}), f32[64,1,1280]{2,1,0:T(1,128)S(1)}, u32[]{:S(2)}, u32[]{:S(2)}) async-start(f32[64,1,1280]{2,1,0:T(1,128)} %reshape.215), calls=%async_computation | async-start | bytes 655360 | tf_op jit(solution)/shard_map/all_to_all | solution.py:22
  16.8 11.7 %all-to-all-done = f32[64,1,1280]{2,1,0:T(1,128)S(1)} async-done(((f32[64,1,1280]{2,1,0:T(1,128)}), f32[64,1,1280]{2,1,0:T(1,128)S(1)}, u32[]{:S(2)}, u32[]{:S(2)}) %all-to-all-start) | async-done | bytes 327712 | tf_op jit(solution)/shard_map/all_to_all | solution.py:22
  28.5 0.2 reduce_sum.96
  28.7 0.1 add_bitcast_fusion.1
  28.8 0.1 rsqrt_multiply_fusion.1
  28.9 17.4 %all_to_all.30 = f32[64,8,128]{2,1,0:T(8,128)S(1)} all-to-all(f32[64,8,128]{2,1,0:T(8,128)S(1)} %broadcast_in_dim.66), channel_id=1, replica_groups=mesh['col'=8,'row'=64] {'row'}, dimensions={0} | all-to-all | bytes 524288 | tf_op jit(solution)/shard_map/all_to_all | solution.py:22
  46.4 0.4 fusion
  46.8 0.3 fusion.1
  47.1 0.3 fusion.29
  47.5 0.4 fusion.28
  47.9 0.3 fusion.63
  48.2 0.3 convolution_add_fusion.3
  48.4 0.3 fusion.61
  48.7 0.3 convolution_add_fusion.4
  49.0 0.4 fusion.62
  49.4 9.3 %collective-permute-start = (f32[256,256]{1,0:T(8,128)S(1)}, f32[256,256]{1,0:T(8,128)S(1)}, u32[]{:S(2)}, u32[]{:S(2)}) collective-permute-start(f32[256,256]{1,0:T(8,128)S(1)} %fusion.62), channel_id=1, source_target_pairs={{448,0},{0,64},{64,128},{128,192},{192,256},{256,320},{320,384},{3... | collective-permute-start | bytes 786440 | tf_op jit(solution)/shard_map/ppermute | solution.py:12
  58.7 0.4 fusion.64
  59.1 1.9 %collective-permute-start.1 = (f32[256,256]{1,0:T(8,128)S(1)}, f32[256,256]{1,0:T(8,128)S(1)}, u32[]{:S(2)}, u32[]{:S(2)}) collective-permute-start(f32[256,256]{1,0:T(8,128)S(1)} %fusion.64), channel_id=1, source_target_pairs={{64,0},{128,64},{192,128},{256,192},{320,256},{384,320},{448,384},... | collective-permute-start | bytes 786440 | tf_op jit(solution)/shard_map/ppermute | solution.py:12
  61.0 1.3 collective-permute-done
  62.4 7.9 %collective-permute-done.1 = f32[256,256]{1,0:T(8,128)S(1)} collective-permute-done((f32[256,256]{1,0:T(8,128)S(1)}, f32[256,256]{1,0:T(8,128)S(1)}, u32[]{:S(2)}, u32[]{:S(2)}) %collective-permute-start.1) | collective-permute-done | bytes 262176 | tf_op jit(solution)/shard_map/ppermute | solution.py:12
  70.2 0.4 fusion.65
  70.7 0.1 multiply_reduce_fusion.3
  70.8 0.1 multiply_reduce_fusion.2
  70.9 0.2 reshape.220
  71.1 17.7 %all_to_all.31 = f32[64,1,1280]{2,1,0:T(1,128)S(1)} all-to-all(f32[64,1,1280]{2,1,0:T(1,128)S(1)} %reshape.220), channel_id=1, replica_groups=mesh['col'=8,'row'=64] {'row'}, dimensions={0} | all-to-all | bytes 655360 | tf_op jit(solution)/shard_map/all_to_all | solution.py:22
  88.9 0.2 reduce_sum.100
  89.1 0.1 add_bitcast_fusion
  89.2 0.1 rsqrt_multiply_fusion
  89.3 0.7 broadcast_in_dim.69
  90.0 5.9 %all-to-all-start.3 = ((f32[64,8,128]{2,1,0:T(8,128)}), f32[64,8,128]{2,1,0:T(8,128)S(1)}, u32[]{:S(2)}, u32[]{:S(2)}) async-start(f32[64,8,128]{2,1,0:T(8,128)} %broadcast_in_dim.69), calls=%async_computation.3 | async-start | bytes 524288 | tf_op jit(solution)/shard_map/all_to_all | solution.py:22
  95.9 10.5 %all-to-all-done.3 = f32[64,8,128]{2,1,0:T(8,128)S(1)} async-done(((f32[64,8,128]{2,1,0:T(8,128)}), f32[64,8,128]{2,1,0:T(8,128)S(1)}, u32[]{:S(2)}, u32[]{:S(2)}) %all-to-all-start.3) | async-done | bytes 262176 | tf_op jit(solution)/shard_map/all_to_all | solution.py:22
  106.5 0.3 fusion.27
  106.8 0.4 fusion.26
  107.2 0.3 fusion.67
  107.5 0.3 convolution_add_fusion
  107.8 0.3 fusion.66
  108.1 0.3 convolution_add_fusion.2
  108.4 0.3 convolution_subtract_fusion
  108.7 0.3 multiply_reduce_fusion.1
  109.0 0.3 convolution_add_fusion.1
  109.3 0.3 multiply_reduce_fusion
  109.6 0.7 broadcast_in_dim.71
  110.3 6.4 %all-to-all-start.4 = ((f32[64,4,128]{2,1,0:T(4,128)}), f32[64,4,128]{2,1,0:T(4,128)S(1)}, u32[]{:S(2)}, u32[]{:S(2)}) async-start(f32[64,4,128]{2,1,0:T(4,128)} %broadcast_in_dim.71), calls=%async_computation.4 | async-start | bytes 262144 | tf_op jit(solution)/shard_map/all_to_all | solution.py:22
  116.7 0.0 copy-start.1
  116.8 3.7 %collective-permute-start.2 = (f32[256,256]{1,0:T(8,128)S(1)}, f32[256,256]{1,0:T(8,128)S(1)}, u32[]{:S(2)}, u32[]{:S(2)}) collective-permute-start(f32[256,256]{1,0:T(8,128)S(1)} %get-tuple-element.23), channel_id=1, source_target_pairs={{64,0},{128,64},{192,128},{256,192},{320,256},{384,320},{448,384},... | collective-permute-start | bytes 786440 | tf_op jit(solution)/shard_map/ppermute | solution.py:12
  120.5 2.7 %collective-permute-start.3 = (f32[256,256]{1,0:T(8,128)S(1)}, f32[256,256]{1,0:T(8,128)S(1)}, u32[]{:S(2)}, u32[]{:S(2)}) collective-permute-start(f32[256,256]{1,0:T(8,128)S(1)} %get-tuple-element.21), channel_id=1, source_target_pairs={{448,0},{0,64},{64,128},{128,192},{192,256},{256,320},{320,384},{3... | collective-permute-start | bytes 786440 | tf_op jit(solution)/shard_map/ppermute | solution.py:12
  123.2 0.0 copy-done.1
  123.2 0.1 broadcast_compare_fusion
  123.3 3.4 %all-to-all-done.4 = f32[64,4,128]{2,1,0:T(4,128)S(1)} async-done(((f32[64,4,128]{2,1,0:T(4,128)}), f32[64,4,128]{2,1,0:T(4,128)S(1)}, u32[]{:S(2)}, u32[]{:S(2)}) %all-to-all-start.4) | async-done | bytes 131104 | tf_op jit(solution)/shard_map/all_to_all | solution.py:22
  126.7 0.1 reduce_sum.104
  126.8 0.6 broadcast_in_dim.72
  127.4 10.8 %all-to-all-start.5 = ((f32[8,4,128]{2,1,0:T(4,128)}), f32[8,4,128]{2,1,0:T(4,128)S(1)}, u32[]{:S(2)}, u32[]{:S(2)}) async-start(f32[8,4,128]{2,1,0:T(4,128)} %broadcast_in_dim.72), calls=%async_computation.5 | async-start | bytes 32768 | tf_op jit(solution)/shard_map/all_to_all | solution.py:22
  138.2 0.0 collective-permute-done.2
  138.2 0.0 collective-permute-done.3
  138.2 0.9 pad_maximum_fusion
  139.1 6.2 %all-to-all-done.5 = f32[8,4,128]{2,1,0:T(4,128)S(1)} async-done(((f32[8,4,128]{2,1,0:T(4,128)}), f32[8,4,128]{2,1,0:T(4,128)S(1)}, u32[]{:S(2)}, u32[]{:S(2)}) %all-to-all-start.5) | async-done | bytes 16416 | tf_op jit(solution)/shard_map/all_to_all | solution.py:22
  145.4 0.1 select_reduce_fusion
  145.5 0.6 copy.14
  (38 shorter events, 0.5 us)
Async XLA Ops:
  0.6 1.5 %copy-start = (f32[256,512]{1,0:T(8,128)S(1)}, f32[256,512]{1,0:T(8,128)}, u32[]{:S(2)}) copy-start(f32[256,512]{1,0:T(8,128)} %param.2) | copy-start | bytes 1572868
  3.8 24.7 %all-to-all-start = ((f32[64,1,1280]{2,1,0:T(1,128)}), f32[64,1,1280]{2,1,0:T(1,128)S(1)}, u32[]{:S(2)}, u32[]{:S(2)}) async-start(f32[64,1,1280]{2,1,0:T(1,128)} %reshape.215), calls=%async_computation | async-start | bytes 655360 | tf_op jit(solution)/shard_map/all_to_all | solution.py:22
  49.4 12.9 %collective-permute-start = (f32[256,256]{1,0:T(8,128)S(1)}, f32[256,256]{1,0:T(8,128)S(1)}, u32[]{:S(2)}, u32[]{:S(2)}) collective-permute-start(f32[256,256]{1,0:T(8,128)S(1)} %fusion.62), channel_id=1, source_target_pairs={{448,0},{0,64},{64,128},{128,192},{192,256},{256,320},{320,384},{3... | collective-permute-start | bytes 786440 | tf_op jit(solution)/shard_map/ppermute | solution.py:12
  59.1 11.2 %collective-permute-start.1 = (f32[256,256]{1,0:T(8,128)S(1)}, f32[256,256]{1,0:T(8,128)S(1)}, u32[]{:S(2)}, u32[]{:S(2)}) collective-permute-start(f32[256,256]{1,0:T(8,128)S(1)} %fusion.64), channel_id=1, source_target_pairs={{64,0},{128,64},{192,128},{256,192},{320,256},{384,320},{448,384},... | collective-permute-start | bytes 786440 | tf_op jit(solution)/shard_map/ppermute | solution.py:12
  90.0 16.5 %all-to-all-start.3 = ((f32[64,8,128]{2,1,0:T(8,128)}), f32[64,8,128]{2,1,0:T(8,128)S(1)}, u32[]{:S(2)}, u32[]{:S(2)}) async-start(f32[64,8,128]{2,1,0:T(8,128)} %broadcast_in_dim.69), calls=%async_computation.3 | async-start | bytes 524288 | tf_op jit(solution)/shard_map/all_to_all | solution.py:22
  110.3 16.4 %all-to-all-start.4 = ((f32[64,4,128]{2,1,0:T(4,128)}), f32[64,4,128]{2,1,0:T(4,128)S(1)}, u32[]{:S(2)}, u32[]{:S(2)}) async-start(f32[64,4,128]{2,1,0:T(4,128)} %broadcast_in_dim.71), calls=%async_computation.4 | async-start | bytes 262144 | tf_op jit(solution)/shard_map/all_to_all | solution.py:22
  116.7 6.5 %copy-start.1 = (s32[16]{0:T(128)S(1)}, s32[16]{0:T(128)}, u32[]{:S(2)}) copy-start(s32[16]{0:T(128)} %param.3) | copy-start | bytes 196
  116.8 21.5 %collective-permute-start.2 = (f32[256,256]{1,0:T(8,128)S(1)}, f32[256,256]{1,0:T(8,128)S(1)}, u32[]{:S(2)}, u32[]{:S(2)}) collective-permute-start(f32[256,256]{1,0:T(8,128)S(1)} %get-tuple-element.23), channel_id=1, source_target_pairs={{64,0},{128,64},{192,128},{256,192},{320,256},{384,320},{448,384},... | collective-permute-start | bytes 786440 | tf_op jit(solution)/shard_map/ppermute | solution.py:12
  120.5 17.7 %collective-permute-start.3 = (f32[256,256]{1,0:T(8,128)S(1)}, f32[256,256]{1,0:T(8,128)S(1)}, u32[]{:S(2)}, u32[]{:S(2)}) collective-permute-start(f32[256,256]{1,0:T(8,128)S(1)} %get-tuple-element.21), channel_id=1, source_target_pairs={{448,0},{0,64},{64,128},{128,192},{192,256},{256,320},{320,384},{3... | collective-permute-start | bytes 786440 | tf_op jit(solution)/shard_map/ppermute | solution.py:12
  127.4 17.9 %all-to-all-start.5 = ((f32[8,4,128]{2,1,0:T(4,128)}), f32[8,4,128]{2,1,0:T(4,128)S(1)}, u32[]{:S(2)}, u32[]{:S(2)}) async-start(f32[8,4,128]{2,1,0:T(4,128)} %broadcast_in_dim.72), calls=%async_computation.5 | async-start | bytes 32768 | tf_op jit(solution)/shard_map/all_to_all | solution.py:22

commit v2 on v1

--- a/solution.py
+++ b/solution.py
@@ -6,10 +6,18 @@
 PREC = lax.Precision.HIGH
 
 
-def passed_along(block, axis, distance):
-    devices = range(lax.axis_size(axis))
-    route = [((i - distance) % len(devices), i) for i in devices]
-    return lax.ppermute(block, axis, route)
+def swapped(block):
+    cols = lax.axis_size("col")
+    return lax.ppermute(
+        block, "col", [(c, (c + (2 if c % 2 else -2)) % cols) for c in range(cols)]
+    )
+
+
+def swapped_back(block):
+    cols = lax.axis_size("col")
+    return lax.ppermute(
+        block, "col", [(c, (c + (-2 if c % 2 else 2)) % cols) for c in range(cols)]
+    )
 
 
 def product(a, b, ca, cb):
@@ -28,7 +36,7 @@
     return (eye - 0.5 * s + 0.375 * s2) + product(s2, 0.0625 * s2 - 0.3125 * s, 1, 0)
 
 
-def couplings(left, right, total_rows):
+def couplings(left, right, sign, total_rows):
     n = lax.axis_size("row")
     width = left.shape[1]
     cross = product(left, right, 0, 0)
@@ -44,7 +52,7 @@
     mean_left = lax.dynamic_slice(got[1024:1152], (start,), (8,)) / total_rows
     mean_right = got[1152:] / total_rows
     part = (
-        0.5
+        (0.5 * sign)
         * (tile / total_rows)
         / jnp.sqrt((mean_left[:, None] + 1e-06) * (mean_right[None, :] + 1e-06))
     )
@@ -52,8 +60,8 @@
     return jnp.concatenate([whole[:width], whole[width:]], axis=1)
 
 
-def pair_update(left, right, total_rows):
-    x = couplings(left, right, total_rows)
+def pair_update(left, right, sign, total_rows):
+    x = couplings(left, right, sign, total_rows)
     new_left = product(
         left - product(right, x, 1, 1), root(product(x, x, 1, 1)), 1, 0
     )
@@ -67,22 +75,27 @@
     width = matrix.shape[1] // 2
     n, cols = lax.axis_size("row"), lax.axis_size("col")
     total_rows = matrix.shape[0] * n
-    top = matrix[:, :width]
-    bottom = matrix[:, width:]
-    top, bottom = pair_update(top, bottom, total_rows)
-    top = passed_along(top, "col", 1)
-    bottom = passed_along(bottom, "col", -1)
-    top, bottom = pair_update(top, bottom, total_rows)
-    sums = jnp.concatenate([jnp.sum(top * top, axis=0), jnp.sum(bottom * bottom, axis=0)])
-    top = passed_along(top, "col", -1)
-    bottom = passed_along(bottom, "col", 1)
-    final = jnp.concatenate([top, bottom], axis=1)
+    odd = lax.axis_index("col") % 2 == 1
+    keep = jnp.where(odd, matrix[:, width:], matrix[:, :width])
+    move = jnp.where(odd, matrix[:, :width], matrix[:, width:])
+    sign = jnp.where(odd, -1.0, 1.0).astype(jnp.float32)
+    keep, move = pair_update(keep, move, sign, total_rows)
+    keep, guest = pair_update(keep, swapped(move), sign, total_rows)
+    sums = jnp.concatenate([jnp.sum(keep * keep, axis=0), jnp.sum(guest * guest, axis=0)])
+    back = swapped_back(guest)
+    final = jnp.concatenate(
+        [jnp.where(odd, back, keep), jnp.where(odd, keep, back)], axis=1
+    )
     sums = exchange(jnp.broadcast_to(sums.reshape(1, 4, 128), (n, 4, 128)), "row")
     means = jnp.sum(sums, axis=0) / total_rows
     table = exchange(jnp.broadcast_to(means[None], (cols, 4, 128)), "col")
-    tops = jnp.roll(table[:, :2].reshape(cols, width), -1, axis=0)
-    bottoms = jnp.roll(table[:, 2:].reshape(cols, width), 1, axis=0)
-    by_seat = jnp.stack([tops, bottoms], axis=1).reshape(2 * cols, width)
+    kept = table[:, :2].reshape(cols, width)
+    guests = table[:, 2:].reshape(cols, width)
+    rows = []
+    for c in range(cols):
+        rows.append(guests[(c + 2) % cols] if c % 2 else kept[c])
+        rows.append(kept[c] if c % 2 else guests[(c - 2) % cols])
+    by_seat = jnp.stack(rows)
     wanted = 2 * lax.axis_index("col") + jnp.arange(2, dtype=jnp.int32)
     hit = seats[None, :] == wanted[:, None]
     picked = jnp.sum(jnp.where(hit[:, :, None], by_seat[None], 0.0), axis=1)

time: 147 us -> 151 us (1.027)
  waiting for transfers between devices: 41.1 us -> 53.8 us
  starting transfers between devices: 53.7 us -> 46.4 us
    ppermute x4 -> x2, starting transfers between devices: 17.6 us -> 9.79 us  [the longest x1 5.8 us: swapped(): lax.ppermute(block, 'col', [(c, (c + (2 if c % 2 else -2)) % cols) for c...]
    ppermute x4 -> x2, waiting for transfers between devices: 9.23 us -> 16 us  [the longest x1 9.9 us: swapped(): lax.ppermute(block, 'col', [(c, (c + (2 if c % 2 else -2)) % cols) for c...]
    all_to_all x4, waiting for transfers between devices: 31.9 us -> 37.9 us  [exchange(): return lax.all_to_all(pieces, axis, 0, 0, tiled=True)]
  transfers between devices with their start and end apart: 8 -> 6, of which waited for: 6 -> 6; matrix products, arithmetic and copies ran while one was open for 1% -> 1% of each run, Pallas kernels for 0% -> 0%
where the time goes in v2:
time: 151 us; the launch traced here: 150 us
  waiting for transfers between devices  53.8 us (36%)
  starting transfers between devices  46.4 us (31%)
  blocking collectives  34.2 us (23%)
  matrix products  6.85 us (5%)
  local copies, waits for them, and re-layouts  4.68 us (3%)
  other arithmetic  3.14 us (2%)
    all_to_all x4, waiting for transfers between devices, exchange(): return lax.all_to_all(pieces, axis, 0, 0, tiled=True)  37.9 us
    all_to_all x4, starting transfers between devices, exchange(): return lax.all_to_all(pieces, axis, 0, 0, tiled=True)  36.6 us
    all_to_all x2, blocking collectives, exchange(): return lax.all_to_all(pieces, axis, 0, 0, tiled=True)  34.2 us
    ppermute x1, waiting for transfers between devices, swapped(): lax.ppermute(block, 'col', [(c, (c + (2 if c % 2 else -2)) % cols) for c...  9.9 us
    dot_general x22, matrix products, product(): lax.dot_general(a, b, (((ca,), (cb,)), ((), ())), precision=PREC, preferr...  6.85 us
    ppermute x1, waiting for transfers between devices, swapped_back(): lax.ppermute(block, 'col', [(c, (c + (-2 if c % 2 else 2)) % cols) for c...  6.06 us
    ppermute x1, starting transfers between devices, swapped(): lax.ppermute(block, 'col', [(c, (c + (2 if c % 2 else -2)) % cols) for c...  5.8 us
    ppermute x1, starting transfers between devices, swapped_back(): lax.ppermute(block, 'col', [(c, (c + (-2 if c % 2 else 2)) % cols) for c...  3.99 us
  transfers between devices with their start and end apart: 6, of which 6 were waited for; matrix products, arithmetic and copies ran while one was open for 1% of the time, Pallas kernels for 0%

profile of v2, /device:TPU:1, one launch (start us, length us, event | category | flops | bytes accessed | tf_op | source)
XLA Modules:
  0.0 150.1 jit_solution(14973759337121096919)
XLA Ops:
  0.6 1.1 multiply_reduce_fusion.4
  1.8 0.4 fusion.53
  2.3 0.9 reshape.227
  3.3 12.9 %all-to-all-start = ((f32[64,1,1280]{2,1,0:T(1,128)}), f32[64,1,1280]{2,1,0:T(1,128)S(1)}, u32[]{:S(2)}, u32[]{:S(2)}) async-start(f32[64,1,1280]{2,1,0:T(1,128)} %reshape.227), calls=%async_computation | async-start | bytes 655360 | tf_op jit(solution)/shard_map/all_to_all | solution.py:30
  16.2 11.7 %all-to-all-done = f32[64,1,1280]{2,1,0:T(1,128)S(1)} async-done(((f32[64,1,1280]{2,1,0:T(1,128)}), f32[64,1,1280]{2,1,0:T(1,128)S(1)}, u32[]{:S(2)}, u32[]{:S(2)}) %all-to-all-start) | async-done | bytes 327712 | tf_op jit(solution)/shard_map/all_to_all | solution.py:30
  27.9 0.2 reduce_sum.96
  28.2 0.1 add_bitcast_fusion.1
  28.3 0.1 rsqrt_multiply_fusion.1
  28.4 17.4 %all_to_all.30 = f32[64,8,128]{2,1,0:T(8,128)S(1)} all-to-all(f32[64,8,128]{2,1,0:T(8,128)S(1)} %broadcast_in_dim.31), channel_id=1, replica_groups=mesh['col'=8,'row'=64] {'row'}, dimensions={0} | all-to-all | bytes 524288 | tf_op jit(solution)/shard_map/all_to_all | solution.py:30
  45.8 0.4 fusion.27
  46.2 0.3 fusion.26
  46.6 0.3 convolution_add_fusion.5
  46.9 0.3 fusion.56
  47.1 0.3 convolution_add_fusion.3
  47.4 0.3 fusion.54
  47.7 0.3 convolution_add_fusion.4
  48.0 0.3 fusion.55
  48.3 5.8 %collective-permute-start = (f32[256,256]{1,0:T(8,128)S(1)}, f32[256,256]{1,0:T(8,128)S(1)}, u32[]{:S(2)}, u32[]{:S(2)}) collective-permute-start(f32[256,256]{1,0:T(8,128)S(1)} %fusion.55), channel_id=1, source_target_pairs={{0,384},{64,192},{128,0},{192,320},{256,128},{320,448},{384,256},{... | collective-permute-start | bytes 786440 | tf_op jit(solution)/shard_map/ppermute | solution.py:11
  54.1 0.3 convolution_subtract_fusion.1
  54.5 0.3 multiply_reduce_fusion.3
  54.8 9.9 %collective-permute-done = f32[256,256]{1,0:T(8,128)S(1)} collective-permute-done((f32[256,256]{1,0:T(8,128)S(1)}, f32[256,256]{1,0:T(8,128)S(1)}, u32[]{:S(2)}, u32[]{:S(2)}) %collective-permute-start) | collective-permute-done | bytes 262176 | tf_op jit(solution)/shard_map/ppermute | solution.py:11
  64.7 0.4 fusion.57
  65.2 0.1 multiply_reduce_fusion.2
  65.3 0.2 reshape.232
  65.5 16.7 %all_to_all.31 = f32[64,1,1280]{2,1,0:T(1,128)S(1)} all-to-all(f32[64,1,1280]{2,1,0:T(1,128)S(1)} %reshape.232), channel_id=1, replica_groups=mesh['col'=8,'row'=64] {'row'}, dimensions={0} | all-to-all | bytes 655360 | tf_op jit(solution)/shard_map/all_to_all | solution.py:30
  82.2 0.2 reduce_sum.100
  82.5 0.1 add_bitcast_fusion
  82.6 0.1 rsqrt_multiply_fusion
  82.6 0.7 broadcast_in_dim.68
  83.4 5.3 %all-to-all-start.3 = ((f32[64,8,128]{2,1,0:T(8,128)}), f32[64,8,128]{2,1,0:T(8,128)S(1)}, u32[]{:S(2)}, u32[]{:S(2)}) async-start(f32[64,8,128]{2,1,0:T(8,128)} %broadcast_in_dim.68), calls=%async_computation.3 | async-start | bytes 524288 | tf_op jit(solution)/shard_map/all_to_all | solution.py:30
  88.7 10.7 %all-to-all-done.3 = f32[64,8,128]{2,1,0:T(8,128)S(1)} async-done(((f32[64,8,128]{2,1,0:T(8,128)}), f32[64,8,128]{2,1,0:T(8,128)S(1)}, u32[]{:S(2)}, u32[]{:S(2)}) %all-to-all-start.3) | async-done | bytes 262176 | tf_op jit(solution)/shard_map/all_to_all | solution.py:30
  99.4 0.4 fusion.25
  99.8 0.3 fusion.24
  100.1 0.3 fusion.59
  100.4 0.3 fusion.58
  100.7 0.3 convolution_add_fusion.1
  101.0 0.3 convolution_add_fusion.2
  101.3 0.3 multiply_reduce_fusion
  101.6 4.0 %collective-permute-start.1 = (f32[256,256]{1,0:T(8,128)S(1)}, f32[256,256]{1,0:T(8,128)S(1)}, u32[]{:S(2)}, u32[]{:S(2)}) collective-permute-start(f32[256,256]{1,0:T(8,128)S(1)} %get-tuple-element.42), channel_id=1, source_target_pairs={{0,128},{64,448},{128,256},{192,64},{256,384},{320,192},{384,0},{4... | collective-permute-start | bytes 786440 | tf_op jit(solution)/shard_map/ppermute | solution.py:18
  105.6 0.3 convolution_subtract_fusion
  105.9 0.3 convolution_add_fusion
  106.2 6.1 %collective-permute-done.1 = f32[256,256]{1,0:T(8,128)S(1)} collective-permute-done((f32[256,256]{1,0:T(8,128)S(1)}, f32[256,256]{1,0:T(8,128)S(1)}, u32[]{:S(2)}, u32[]{:S(2)}) %collective-permute-start.1) | collective-permute-done | bytes 262176 | tf_op jit(solution)/shard_map/ppermute | solution.py:18
  112.3 0.3 broadcast_select_fusion.1
  112.6 0.7 broadcast_in_dim.70
  113.3 4.6 %all-to-all-start.4 = ((f32[64,4,128]{2,1,0:T(4,128)}), f32[64,4,128]{2,1,0:T(4,128)S(1)}, u32[]{:S(2)}, u32[]{:S(2)}) async-start(f32[64,4,128]{2,1,0:T(4,128)} %broadcast_in_dim.70), calls=%async_computation.4 | async-start | bytes 262144 | tf_op jit(solution)/shard_map/all_to_all | solution.py:30
  117.9 0.0 copy-start
  117.9 0.6 copy-done
  118.5 0.1 broadcast_compare_fusion
  118.6 9.2 %all-to-all-done.4 = f32[64,4,128]{2,1,0:T(4,128)S(1)} async-done(((f32[64,4,128]{2,1,0:T(4,128)}), f32[64,4,128]{2,1,0:T(4,128)S(1)}, u32[]{:S(2)}, u32[]{:S(2)}) %all-to-all-start.4) | async-done | bytes 131104 | tf_op jit(solution)/shard_map/all_to_all | solution.py:30
  127.8 0.1 reduce_sum.104
  127.9 0.6 broadcast_in_dim.71
  128.5 13.8 %all-to-all-start.5 = ((f32[8,4,128]{2,1,0:T(4,128)}), f32[8,4,128]{2,1,0:T(4,128)S(1)}, u32[]{:S(2)}, u32[]{:S(2)}) async-start(f32[8,4,128]{2,1,0:T(4,128)} %broadcast_in_dim.71), calls=%async_computation.5 | async-start | bytes 32768 | tf_op jit(solution)/shard_map/all_to_all | solution.py:30
  142.3 0.9 pad_maximum_fusion
  143.2 6.2 %all-to-all-done.5 = f32[8,4,128]{2,1,0:T(4,128)S(1)} async-done(((f32[8,4,128]{2,1,0:T(4,128)}), f32[8,4,128]{2,1,0:T(4,128)S(1)}, u32[]{:S(2)}, u32[]{:S(2)}) %all-to-all-start.5) | async-done | bytes 16416 | tf_op jit(solution)/shard_map/all_to_all | solution.py:30
  149.4 0.1 stack.3
  149.4 0.1 select_reduce_fusion
  149.5 0.6 copy.6
  (27 shorter events, 0.4 us)
Async XLA Ops:
  3.3 24.7 %all-to-all-start = ((f32[64,1,1280]{2,1,0:T(1,128)}), f32[64,1,1280]{2,1,0:T(1,128)S(1)}, u32[]{:S(2)}, u32[]{:S(2)}) async-start(f32[64,1,1280]{2,1,0:T(1,128)} %reshape.227), calls=%async_computation | async-start | bytes 655360 | tf_op jit(solution)/shard_map/all_to_all | solution.py:30
  48.3 16.4 %collective-permute-start = (f32[256,256]{1,0:T(8,128)S(1)}, f32[256,256]{1,0:T(8,128)S(1)}, u32[]{:S(2)}, u32[]{:S(2)}) collective-permute-start(f32[256,256]{1,0:T(8,128)S(1)} %fusion.55), channel_id=1, source_target_pairs={{0,384},{64,192},{128,0},{192,320},{256,128},{320,448},{384,256},{... | collective-permute-start | bytes 786440 | tf_op jit(solution)/shard_map/ppermute | solution.py:11
  83.4 16.0 %all-to-all-start.3 = ((f32[64,8,128]{2,1,0:T(8,128)}), f32[64,8,128]{2,1,0:T(8,128)S(1)}, u32[]{:S(2)}, u32[]{:S(2)}) async-start(f32[64,8,128]{2,1,0:T(8,128)} %broadcast_in_dim.68), calls=%async_computation.3 | async-start | bytes 524288 | tf_op jit(solution)/shard_map/all_to_all | solution.py:30
  101.6 10.7 %collective-permute-start.1 = (f32[256,256]{1,0:T(8,128)S(1)}, f32[256,256]{1,0:T(8,128)S(1)}, u32[]{:S(2)}, u32[]{:S(2)}) collective-permute-start(f32[256,256]{1,0:T(8,128)S(1)} %get-tuple-element.42), channel_id=1, source_target_pairs={{0,128},{64,448},{128,256},{192,64},{256,384},{320,192},{384,0},{4... | collective-permute-start | bytes 786440 | tf_op jit(solution)/shard_map/ppermute | solution.py:18
  113.3 14.6 %all-to-all-start.4 = ((f32[64,4,128]{2,1,0:T(4,128)}), f32[64,4,128]{2,1,0:T(4,128)S(1)}, u32[]{:S(2)}, u32[]{:S(2)}) async-start(f32[64,4,128]{2,1,0:T(4,128)} %broadcast_in_dim.70), calls=%async_computation.4 | async-start | bytes 262144 | tf_op jit(solution)/shard_map/all_to_all | solution.py:30
  117.9 0.7 copy-start
  128.5 20.8 %all-to-all-start.5 = ((f32[8,4,128]{2,1,0:T(4,128)}), f32[8,4,128]{2,1,0:T(4,128)S(1)}, u32[]{:S(2)}, u32[]{:S(2)}) async-start(f32[8,4,128]{2,1,0:T(4,128)} %broadcast_in_dim.71), calls=%async_computation.5 | async-start | bytes 32768 | tf_op jit(solution)/shard_map/all_to_all | solution.py:30

commit v3 on v2

v3 whole, which is shorter than its diff:
```python
import functools

import jax
import jax.numpy as jnp
from jax import lax
from jax.experimental import pallas as pl
from jax.experimental.pallas import tpu as pltpu
from jax.sharding import PartitionSpec as P

W = 256
N_ROW = 64
N_COL = 8
PIECE = 10
LIMIT = 32 * 1024 * 1024


def split(a):
    high = a.astype(jnp.bfloat16)
    return high, (a - high.astype(jnp.float32)).astype(jnp.bfloat16)


def product(a, b, ca=1, cb=0):
    def one(p, q):
        return lax.dot_general(
            p, q, (((ca,), (cb,)), ((), ())), preferred_element_type=jnp.float32
        )

    return one(a[0], b[0]) + (one(a[0], b[1]) + one(a[1], b[0]))


def root(s, also):
    parts = split(s)
    s2 = product(parts, parts)
    other = also()
    rows = lax.broadcasted_iota(jnp.int32, s.shape, 0)
    cols = lax.broadcasted_iota(jnp.int32, s.shape, 1)
    eye = jnp.where(rows == cols, 1.0, 0.0).astype(jnp.float32)
    base = eye - 0.5 * s + 0.375 * s2
    return base + product(split(s2), split(0.0625 * s2 - 0.3125 * s)), other


def kept_part(keep, guest, x):
    z, mixed = root(product(x, x, 1, 1), lambda: keep - product(split(guest), x, 1, 1))
    return product(split(mixed), split(z))


def guest_part(keep, guest, x):
    z, mixed = root(product(x, x, 0, 0), lambda: guest + product(split(keep), x))
    return product(split(mixed), split(z))


def coupling_of(tiles):
    return split(jnp.concatenate([tiles[:W], tiles[W:]], axis=1))


def pack(keep, guest, out):
    cross = product(split(keep), split(guest), 0, 0)
    norm_keep = jnp.sum(keep * keep, axis=0, keepdims=True)
    norm_guest = jnp.sum(guest * guest, axis=0, keepdims=True)
    for r in range(N_ROW):
        i, half = r % 32, r // 32
        at = PIECE * r
        out[at : at + 8, :] = cross[8 * i : 8 * i + 8, 128 * half : 128 * half + 128]
        out[at + 8 : at + 9, :] = norm_keep[:, 128 * (i // 16) : 128 * (i // 16) + 128]
        out[at + 9 : at + 10, :] = norm_guest[:, 128 * half : 128 * half + 128]


def halves(matrix):
    odd = lax.rem(lax.axis_index("col"), 2)
    keep = matrix[:, pl.ds(pl.multiple_of(odd * W, W), W)]
    move = matrix[:, pl.ds(pl.multiple_of((1 - odd) * W, W), W)]
    return keep, move


def pack_first(matrix, out):
    pack(*halves(matrix), out)


def pack_second(keep, guest, out):
    pack(keep[...], guest[...], out)


def fold(total_rows, got, out):
    tile = got[0:8, :]
    norms = got[8:10, :]
    for r in range(1, N_ROW):
        tile += got[PIECE * r : PIECE * r + 8, :]
        norms += got[PIECE * r + 8 : PIECE * r + 10, :]
    sign = jnp.where(lax.rem(lax.axis_index("col"), 2) == 1, -0.5, 0.5)
    first = 8 * lax.rem(lax.axis_index("row"), 16)
    lanes = lax.broadcasted_iota(jnp.int32, (8, 128), 1)
    rows = lax.broadcasted_iota(jnp.int32, (8, 128), 0)
    means = norms / total_rows
    mean_keep = jnp.sum(
        jnp.where(lanes == first + rows, means[0:1], 0.0), axis=1, keepdims=True
    )
    x = sign * (tile / total_rows) / jnp.sqrt((mean_keep + 1e-06) * (means[1:2] + 1e-06))
    for r in range(N_ROW):
        out[8 * r : 8 * r + 8, :] = x


def first_move(matrix, tiles, out):
    out[...] = guest_part(*halves(matrix), coupling_of(tiles[...]))


def first_keep(matrix, tiles, out):
    out[...] = kept_part(*halves(matrix), coupling_of(tiles[...]))


def second(keep, guest, tiles, new_keep, new_guest, sums):
    x = coupling_of(tiles[...])
    old_keep, old_guest = keep[...], guest[...]
    moved = guest_part(old_keep, old_guest, x)
    new_guest[...] = moved
    kept = kept_part(old_keep, old_guest, x)
    new_keep[...] = kept
    of_keep = jnp.sum(kept * kept, axis=0, keepdims=True)
    of_guest = jnp.sum(moved * moved, axis=0, keepdims=True)
    four = [of_keep[:, :128], of_keep[:, 128:], of_guest[:, :128], of_guest[:, 128:]]
    tile = jnp.concatenate(four + four, axis=0)
    for r in range(4 * N_ROW // 8):
        sums[8 * r : 8 * r + 8, :] = tile


def fold_sums(total_rows, got, out):
    tile = got[0:8, :]
    for r in range(1, 4 * N_ROW // 8):
        tile += got[8 * r : 8 * r + 8, :]
    four = (tile[0:4] + tile[4:8]) / total_rows
    tile = jnp.concatenate([four, four], axis=0)
    for r in range(4 * N_COL // 8):
        out[8 * r : 8 * r + 8, :] = tile


def local(body, flops, *shapes):
    out = [jax.ShapeDtypeStruct(shape, jnp.float32) for shape in shapes]

    def call(*args):
        moved = sum(4 * a.size for a in args) + sum(4 * s.size for s in out)
        return pl.pallas_call(
            body,
            out_shape=out if len(out) > 1 else out[0],
            in_specs=[pl.BlockSpec(memory_space=pltpu.VMEM)] * len(args),
            out_specs=[pl.BlockSpec(memory_space=pltpu.VMEM)] * len(out)
            if len(out) > 1
            else pl.BlockSpec(memory_space=pltpu.VMEM),
            cost_estimate=pl.CostEstimate(flops=flops, bytes_accessed=moved, transcendentals=0),
            compiler_params=pltpu.CompilerParams(vmem_limit_bytes=LIMIT),
        )(*args)

    return call


def swapped(block):
    return lax.ppermute(
        block, "col", [(c, (c + (2 if c % 2 else -2)) % N_COL) for c in range(N_COL)]
    )


def swapped_back(block):
    return lax.ppermute(
        block, "col", [(c, (c + (-2 if c % 2 else 2)) % N_COL) for c in range(N_COL)]
    )


def exchange(pieces, axis):
    n = lax.axis_size(axis)
    rows = pieces.shape[0] // n
    shape = (n, rows, 128) if rows in (4, 8) else (n, 1, rows * 128)
    return lax.all_to_all(pieces.reshape(shape), axis, 0, 0, tiled=True).reshape(pieces.shape)


def on_device(matrix, seats):
    total_rows = matrix.shape[0] * N_ROW
    one = 6 * W**3
    fold_all = local(functools.partial(fold, total_rows), 1, (8 * N_ROW, 128))
    sent = local(pack_first, one, (PIECE * N_ROW, 128))(matrix)
    tiles = exchange(fold_all(exchange(sent, "row")), "row")
    move = local(first_move, 5 * one, (W, W))(matrix, tiles)
    guest = swapped(move)
    keep = local(first_keep, 5 * one, (W, W))(matrix, tiles)
    sent = local(pack_second, one, (PIECE * N_ROW, 128))(keep, guest)
    tiles = exchange(fold_all(exchange(sent, "row")), "row")
    keep, guest, sums = local(second, 10 * one, (W, W), (W, W), (4 * N_ROW, 128))(keep, guest, tiles)
    back = swapped_back(guest)
    sums = exchange(sums, "row")
    means = local(functools.partial(fold_sums, total_rows), 1, (4 * N_COL, 128))(sums)
    table = exchange(means, "col").reshape(N_COL, 4, 128)
    odd = lax.axis_index("col") % 2 == 1
    final = jnp.concatenate([jnp.where(odd, back, keep), jnp.where(odd, keep, back)], axis=1)
    kept = table[:, :2].reshape(N_COL, W)
    guests = table[:, 2:].reshape(N_COL, W)
    rows = []
    for c in range(N_COL):
        rows.append(guests[(c + 2) % N_COL] if c % 2 else kept[c])
        rows.append(kept[c] if c % 2 else guests[(c - 2) % N_COL])
    by_seat = jnp.stack(rows)
    wanted = 2 * lax.axis_index("col") + jnp.arange(2, dtype=jnp.int32)
    hit = seats[None, :] == wanted[:, None]
    picked = jnp.sum(jnp.where(hit[:, :, None], by_seat[None], 0.0), axis=1)
    return (final, picked.reshape(2 * W))


def solution(mesh):
    placed = (P("row", "col"), P())
    return jax.shard_map(
        on_device,
        mesh=mesh,
        in_specs=placed,
        out_specs=(P("row", "col"), P("col")),
        check_vma=False,
    )
```

time: 151 us -> 134 us (0.89)
  blocking collectives: 34.2 us -> 58.6 us
  waiting for transfers between devices: 53.8 us -> 31.5 us
  starting transfers between devices: 46.4 us -> 31.6 us
  Pallas kernels: 0 us -> 7.83 us
  matrix products: 6.85 us -> 0 us
  local copies, waits for them, and re-layouts: 4.68 us -> 2.33 us
  other arithmetic: 3.14 us -> 1.06 us
    all_to_all x2 -> x3, blocking collectives: 34.2 us -> 58.6 us  [exchange(): lax.all_to_all(pieces.reshape(shape), axis, 0, 0, tiled=True)]
    all_to_all x4 -> x3, waiting for transfers between devices: 37.9 us -> 22.2 us  [exchange(): lax.all_to_all(pieces.reshape(shape), axis, 0, 0, tiled=True)]
    all_to_all x4 -> x3, starting transfers between devices: 36.6 us -> 21.9 us  [exchange(): lax.all_to_all(pieces.reshape(shape), axis, 0, 0, tiled=True)]
    pallas_call x0 -> x8, Pallas kernels: none -> 7.83 us  [call(): pl.pallas_call(body, out_shape=out if len(out) > 1 else out[0], in_specs=...]
    dot_general x22 -> x0, matrix products: 6.85 us -> none  [product(): lax.dot_general(a, b, (((ca,), (cb,)), ((), ())), precision=PREC, preferr...]
    ppermute x2, waiting for transfers between devices: 16 us -> 9.25 us  [the longest x1 9.25 us: swapped(): lax.ppermute(block, 'col', [(c, (c + (2 if c % 2 else -2)) % N_COL) for c...]
    broadcast_in_dim x8 -> x0, local copies, waits for them, and re-layouts: 2.04 us -> none  [the longest x2 0.75 us: couplings(): jnp.broadcast_to(part[None], (n, 8, 128))]
    reduce_sum x5 -> x0, other arithmetic: 1.66 us -> none  [the longest x2 1.16 us: couplings(): sum_right = jnp.sum(right * right, axis=0).reshape(2, 128)]
  transfers between devices with their start and end apart: 6 -> 5, of which waited for: 6 -> 4; matrix products, arithmetic and copies ran while one was open for 1% -> 1% of each run, Pallas kernels for 0% -> 1%
where the time goes in v3:
time: 134 us
  blocking collectives  58.6 us (44%)
  starting transfers between devices  31.6 us (24%)
  waiting for transfers between devices  31.5 us (24%)
  Pallas kernels  7.83 us (6%)
  local copies, waits for them, and re-layouts  2.33 us (2%)
    all_to_all x3, blocking collectives, exchange(): lax.all_to_all(pieces.reshape(shape), axis, 0, 0, tiled=True)  58.6 us
    all_to_all x3, waiting for transfers between devices, exchange(): lax.all_to_all(pieces.reshape(shape), axis, 0, 0, tiled=True)  22.2 us
    all_to_all x3, starting transfers between devices, exchange(): lax.all_to_all(pieces.reshape(shape), axis, 0, 0, tiled=True)  21.9 us
    ppermute x1, waiting for transfers between devices, swapped(): lax.ppermute(block, 'col', [(c, (c + (2 if c % 2 else -2)) % N_COL) for c...  9.25 us
    pallas_call x8, Pallas kernels, call(): pl.pallas_call(body, out_shape=out if len(out) > 1 else out[0], in_specs=...  7.83 us
    ppermute x1, starting transfers between devices, swapped(): lax.ppermute(block, 'col', [(c, (c + (2 if c % 2 else -2)) % N_COL) for c...  5.82 us
    ppermute x1, starting transfers between devices, swapped_back(): lax.ppermute(block, 'col', [(c, (c + (-2 if c % 2 else 2)) % N_COL) for c...  3.94 us
  transfers between devices with their start and end apart: 5, of which 4 were waited for; matrix products, arithmetic and copies ran while one was open for 1% of the time, Pallas kernels for 1%

profile of v3, /device:TPU:1, one launch (start us, length us, event | category | flops | bytes accessed | tf_op | source)
XLA Modules:
  0.0 133.7 jit_solution(9196349440662392239)
XLA Ops:
  0.6 0.0 copy-start
  0.6 1.0 copy-done
  1.7 0.3 shard_map.41
  2.0 24.5 %all_to_all.30 = f32[64,1,1280]{2,1,0:T(1,128)S(1)} all-to-all(f32[64,1,1280]{2,1,0:T(1,128)S(1)} %bitcast.31), channel_id=1, replica_groups=mesh['col'=8,'row'=64] {'row'}, dimensions={0} | all-to-all | bytes 655360 | tf_op jit(solution)/shard_map/all_to_all | solution.py:170
  26.5 0.0 copy-start.1
  26.5 0.2 shard_map.42
  26.7 17.4 %all_to_all.31 = f32[64,8,128]{2,1,0:T(8,128)S(1)} all-to-all(f32[64,8,128]{2,1,0:T(8,128)S(1)} %bitcast.33), channel_id=1, replica_groups=mesh['col'=8,'row'=64] {'row'}, dimensions={0} | all-to-all | bytes 524288 | tf_op jit(solution)/shard_map/all_to_all | solution.py:170
  44.1 0.0 copy-done.1
  44.1 1.3 shard_map.44
  45.4 5.8 %collective-permute-start = (f32[256,256]{1,0:T(8,128)S(1)}, f32[256,256]{1,0:T(8,128)S(1)}, u32[]{:S(2)}, u32[]{:S(2)}) collective-permute-start(f32[256,256]{1,0:T(8,128)S(1)} %shard_map.44), channel_id=1, source_target_pairs={{0,384},{64,192},{128,0},{192,320},{256,128},{320,448},{384,256},{... | collective-permute-start | bytes 786440 | tf_op jit(solution)/shard_map/ppermute | solution.py:155
  51.2 1.3 shard_map.43.keep
  52.5 9.3 %collective-permute-done.guest = f32[256,256]{1,0:T(8,128)S(1)} collective-permute-done((f32[256,256]{1,0:T(8,128)S(1)}, f32[256,256]{1,0:T(8,128)S(1)}, u32[]{:S(2)}, u32[]{:S(2)}) %collective-permute-start) | collective-permute-done | bytes 262176 | tf_op jit(solution)/shard_map/ppermute | solution.py:155
  61.8 0.3 shard_map.45
  62.1 16.7 %all_to_all.32 = f32[64,1,1280]{2,1,0:T(1,128)S(1)} all-to-all(f32[64,1,1280]{2,1,0:T(1,128)S(1)} %bitcast.32), channel_id=1, replica_groups=mesh['col'=8,'row'=64] {'row'}, dimensions={0} | all-to-all | bytes 655360 | tf_op jit(solution)/shard_map/all_to_all | solution.py:170
  78.8 0.9 shard_map.46
  79.7 5.3 %all-to-all-start.3 = ((f32[64,8,128]{2,1,0:T(8,128)}), f32[64,8,128]{2,1,0:T(8,128)S(1)}, u32[]{:S(2)}, u32[]{:S(2)}) async-start(f32[64,8,128]{2,1,0:T(8,128)} %bitcast.6), calls=%async_computation.3 | async-start | bytes 524288 | tf_op jit(solution)/shard_map/all_to_all | solution.py:170
  85.0 10.7 %all-to-all-done.3 = f32[64,8,128]{2,1,0:T(8,128)S(1)} async-done(((f32[64,8,128]{2,1,0:T(8,128)}), f32[64,8,128]{2,1,0:T(8,128)S(1)}, u32[]{:S(2)}, u32[]{:S(2)}) %all-to-all-start.3) | async-done | bytes 262176 | tf_op jit(solution)/shard_map/all_to_all | solution.py:170
  95.7 2.9 %shard_map.47 = (f32[256,256]{1,0:T(8,128)S(1)}, f32[256,256]{1,0:T(8,128)S(1)}, f32[256,128]{1,0:T(8,128)}) custom-call(f32[256,256]{1,0:T(8,128)S(1)} %shard_map.43.keep, f32[256,256]{1,0:T(8,128)S(1)} %collective-permute-done.guest, f32[512,128]{1,0:T(8,128)S(1)} %bitcast.35), custom_call_target="tpu_custom_call" | custom-call | flops 1006632960 | bytes 1441792 | tf_op jit(solution)/shard_map/pallas_call | solution.py:140
  98.6 4.7 %all-to-all-start.4 = ((f32[64,4,128]{2,1,0:T(4,128)}), f32[64,4,128]{2,1,0:T(4,128)S(1)}, u32[]{:S(2)}, u32[]{:S(2)}) async-start(f32[64,4,128]{2,1,0:T(4,128)} %bitcast.8), calls=%async_computation.4 | async-start | bytes 262144 | tf_op jit(solution)/shard_map/all_to_all | solution.py:170
  103.3 3.9 %collective-permute-start.1 = (f32[256,256]{1,0:T(8,128)S(1)}, f32[256,256]{1,0:T(8,128)S(1)}, u32[]{:S(2)}, u32[]{:S(2)}) collective-permute-start(f32[256,256]{1,0:T(8,128)S(1)} %get-tuple-element.5), channel_id=1, source_target_pairs={{0,128},{64,448},{128,256},{192,64},{256,384},{320,192},{384,0},{4... | collective-permute-start | bytes 786440 | tf_op jit(solution)/shard_map/ppermute | solution.py:161
  107.3 0.0 copy-start.2
  107.3 0.6 copy-done.2
  107.9 0.1 broadcast_compare_fusion
  108.0 5.4 %all-to-all-done.4 = f32[64,4,128]{2,1,0:T(4,128)S(1)} async-done(((f32[64,4,128]{2,1,0:T(4,128)}), f32[64,4,128]{2,1,0:T(4,128)S(1)}, u32[]{:S(2)}, u32[]{:S(2)}) %all-to-all-start.4) | async-done | bytes 131104 | tf_op jit(solution)/shard_map/all_to_all | solution.py:170
  113.4 0.6 shard_map.48
  114.0 11.9 %all-to-all-start.5 = ((f32[8,4,128]{2,1,0:T(4,128)}), f32[8,4,128]{2,1,0:T(4,128)S(1)}, u32[]{:S(2)}, u32[]{:S(2)}) async-start(f32[8,4,128]{2,1,0:T(4,128)} %bitcast.10), calls=%async_computation.5 | async-start | bytes 32768 | tf_op jit(solution)/shard_map/all_to_all | solution.py:170
  125.9 0.0 collective-permute-done.1
  126.0 0.9 pad_maximum_fusion
  126.8 6.2 %all-to-all-done.5 = f32[8,4,128]{2,1,0:T(4,128)S(1)} async-done(((f32[8,4,128]{2,1,0:T(4,128)}), f32[8,4,128]{2,1,0:T(4,128)S(1)}, u32[]{:S(2)}, u32[]{:S(2)}) %all-to-all-start.5) | async-done | bytes 16416 | tf_op jit(solution)/shard_map/all_to_all | solution.py:170
  133.0 0.1 stack.3
  133.0 0.1 select_reduce_fusion
  133.1 0.6 copy.8
  (3 shorter events, 0.0 us)
Async XLA Ops:
  0.6 1.0 copy-start
  26.5 17.6 %copy-start.1 = (f32[256,512]{1,0:T(8,128)S(1)}, f32[256,512]{1,0:T(8,128)}, u32[]{:S(2)}) copy-start(f32[256,512]{1,0:T(8,128)} %matrix.5) | copy-start | bytes 1572868
  45.4 16.4 %collective-permute-start = (f32[256,256]{1,0:T(8,128)S(1)}, f32[256,256]{1,0:T(8,128)S(1)}, u32[]{:S(2)}, u32[]{:S(2)}) collective-permute-start(f32[256,256]{1,0:T(8,128)S(1)} %shard_map.44), channel_id=1, source_target_pairs={{0,384},{64,192},{128,0},{192,320},{256,128},{320,448},{384,256},{... | collective-permute-start | bytes 786440 | tf_op jit(solution)/shard_map/ppermute | solution.py:155
  79.7 16.0 %all-to-all-start.3 = ((f32[64,8,128]{2,1,0:T(8,128)}), f32[64,8,128]{2,1,0:T(8,128)S(1)}, u32[]{:S(2)}, u32[]{:S(2)}) async-start(f32[64,8,128]{2,1,0:T(8,128)} %bitcast.6), calls=%async_computation.3 | async-start | bytes 524288 | tf_op jit(solution)/shard_map/all_to_all | solution.py:170
  98.6 14.7 %all-to-all-start.4 = ((f32[64,4,128]{2,1,0:T(4,128)}), f32[64,4,128]{2,1,0:T(4,128)S(1)}, u32[]{:S(2)}, u32[]{:S(2)}) async-start(f32[64,4,128]{2,1,0:T(4,128)} %bitcast.8), calls=%async_computation.4 | async-start | bytes 262144 | tf_op jit(solution)/shard_map/all_to_all | solution.py:170
  103.3 22.6 %collective-permute-start.1 = (f32[256,256]{1,0:T(8,128)S(1)}, f32[256,256]{1,0:T(8,128)S(1)}, u32[]{:S(2)}, u32[]{:S(2)}) collective-permute-start(f32[256,256]{1,0:T(8,128)S(1)} %get-tuple-element.5), channel_id=1, source_target_pairs={{0,128},{64,448},{128,256},{192,64},{256,384},{320,192},{384,0},{4... | collective-permute-start | bytes 786440 | tf_op jit(solution)/shard_map/ppermute | solution.py:161
  107.3 0.7 copy-start.2
  114.0 19.0 %all-to-all-start.5 = ((f32[8,4,128]{2,1,0:T(4,128)}), f32[8,4,128]{2,1,0:T(4,128)S(1)}, u32[]{:S(2)}, u32[]{:S(2)}) async-start(f32[8,4,128]{2,1,0:T(4,128)} %bitcast.10), calls=%async_computation.5 | async-start | bytes 32768 | tf_op jit(solution)/shard_map/all_to_all | solution.py:170

commit v4 on v3

--- a/solution.py
+++ b/solution.py
@@ -11,6 +11,7 @@
 N_ROW = 64
 N_COL = 8
 PIECE = 10
+WIDE = 17
 LIMIT = 32 * 1024 * 1024
 
 
@@ -39,30 +40,21 @@
     return base + product(split(s2), split(0.0625 * s2 - 0.3125 * s)), other
 
 
-def kept_part(keep, guest, x):
-    z, mixed = root(product(x, x, 1, 1), lambda: keep - product(split(guest), x, 1, 1))
-    return product(split(mixed), split(z))
-
-
-def guest_part(keep, guest, x):
-    z, mixed = root(product(x, x, 0, 0), lambda: guest + product(split(keep), x))
-    return product(split(mixed), split(z))
-
-
-def coupling_of(tiles):
-    return split(jnp.concatenate([tiles[:W], tiles[W:]], axis=1))
-
-
-def pack(keep, guest, out):
-    cross = product(split(keep), split(guest), 0, 0)
-    norm_keep = jnp.sum(keep * keep, axis=0, keepdims=True)
-    norm_guest = jnp.sum(guest * guest, axis=0, keepdims=True)
-    for r in range(N_ROW):
-        i, half = r % 32, r // 32
-        at = PIECE * r
-        out[at : at + 8, :] = cross[8 * i : 8 * i + 8, 128 * half : 128 * half + 128]
-        out[at + 8 : at + 9, :] = norm_keep[:, 128 * (i // 16) : 128 * (i // 16) + 128]
-        out[at + 9 : at + 10, :] = norm_guest[:, 128 * half : 128 * half + 128]
+def tile_at(block, r):
+    i, half = r % 32, r // 32
+    return block[8 * i : 8 * i + 8, 128 * half : 128 * half + 128]
+
+
+def from_tiles(ref, first, step):
+    left = [ref[step * r + first : step * r + first + 8, :] for r in range(32)]
+    right = [ref[step * r + first : step * r + first + 8, :] for r in range(32, 64)]
+    return jnp.concatenate(
+        [jnp.concatenate(left, axis=0), jnp.concatenate(right, axis=0)], axis=1
+    )
+
+
+def column_squares(block):
+    return jnp.sum(block * block, axis=0, keepdims=True)
 
 
 def halves(matrix):
@@ -73,11 +65,33 @@
 
 
 def pack_first(matrix, out):
-    pack(*halves(matrix), out)
-
-
-def pack_second(keep, guest, out):
-    pack(keep[...], guest[...], out)
+    keep, move = halves(matrix)
+    cross = product(split(keep), split(move), 0, 0)
+    norm_keep, norm_move = column_squares(keep), column_squares(move)
+    for r in range(N_ROW):
+        i, half = r % 32, r // 32
+        at = PIECE * r
+        out[at : at + 8, :] = tile_at(cross, r)
+        out[at + 8 : at + 9, :] = norm_keep[:, 128 * (i // 16) : 128 * (i // 16) + 128]
+        out[at + 9 : at + 10, :] = norm_move[:, 128 * half : 128 * half + 128]
+
+
+def square_index():
+    rows = lax.broadcasted_iota(jnp.int32, (W, W), 0)
+    return rows, lax.broadcasted_iota(jnp.int32, (W, W), 1)
+
+
+def pack_second(keep, guest, gram_keep, out):
+    parts = split(guest[...])
+    cross = product(split(keep[...]), parts, 0, 0)
+    rows, cols = square_index()
+    grams = jnp.where(rows <= cols, gram_keep[...], product(parts, parts, 0, 0))
+    norm_guest = column_squares(guest[...])
+    for r in range(N_ROW):
+        half, at = r // 32, WIDE * r
+        out[at : at + 8, :] = tile_at(cross, r)
+        out[at + 8 : at + 16, :] = tile_at(grams, r)
+        out[at + 16 : at + 17, :] = norm_guest[:, 128 * half : 128 * half + 128]
 
 
 def fold(total_rows, got, out):
@@ -99,37 +113,88 @@
         out[8 * r : 8 * r + 8, :] = x
 
 
+def fold_wide(got, out):
+    piece = got[0:WIDE, :]
+    for r in range(1, N_ROW):
+        piece += got[WIDE * r : WIDE * r + WIDE, :]
+    for r in range(N_ROW):
+        out[WIDE * r : WIDE * r + WIDE, :] = piece
+
+
 def first_move(matrix, tiles, out):
-    out[...] = guest_part(*halves(matrix), coupling_of(tiles[...]))
-
-
-def first_keep(matrix, tiles, out):
-    out[...] = kept_part(*halves(matrix), coupling_of(tiles[...]))
-
-
-def second(keep, guest, tiles, new_keep, new_guest, sums):
-    x = coupling_of(tiles[...])
-    old_keep, old_guest = keep[...], guest[...]
-    moved = guest_part(old_keep, old_guest, x)
-    new_guest[...] = moved
-    kept = kept_part(old_keep, old_guest, x)
-    new_keep[...] = kept
-    of_keep = jnp.sum(kept * kept, axis=0, keepdims=True)
-    of_guest = jnp.sum(moved * moved, axis=0, keepdims=True)
-    four = [of_keep[:, :128], of_keep[:, 128:], of_guest[:, :128], of_guest[:, 128:]]
-    tile = jnp.concatenate(four + four, axis=0)
-    for r in range(4 * N_ROW // 8):
+    keep, move = halves(matrix)
+    x = split(from_tiles(tiles, 0, 8))
+    z, mixed = root(product(x, x, 0, 0), lambda: move + product(split(keep), x))
+    out[...] = product(split(mixed), split(z))
+
+
+def first_keep(matrix, tiles, out, gram):
+    keep, move = halves(matrix)
+    x = split(from_tiles(tiles, 0, 8))
+    z, mixed = root(product(x, x, 1, 1), lambda: keep - product(split(move), x, 1, 1))
+    kept = product(split(mixed), split(z))
+    out[...] = kept
+    parts = split(kept)
+    gram[...] = product(parts, parts, 0, 0)
+
+
+def guest_squares(got):
+    at = 32 * WIDE + 16
+    return jnp.concatenate([got[16:17, :], got[at : at + 1, :]], axis=1)
+
+
+def second_guest(total_rows, keep, guest, got, new_guest, x_out, z_out):
+    cross = from_tiles(got, 0, WIDE)
+    rows, cols = square_index()
+    on_diagonal = jnp.where(rows == cols, from_tiles(got, 8, WIDE), 0.0)
+    mean_keep = jnp.sum(on_diagonal, axis=1, keepdims=True) / total_rows
+    mean_guest = guest_squares(got) / total_rows
+    sign = jnp.where(lax.rem(lax.axis_index("col"), 2) == 1, -0.5, 0.5) / total_rows
+    x = cross * (sign * lax.rsqrt(mean_keep + 1e-06)) * lax.rsqrt(mean_guest + 1e-06)
+    x_out[...] = x
+    x = split(x)
+    z, mixed = root(product(x, x, 0, 0), lambda: guest[...] + product(split(keep[...]), x))
+    z_out[...] = z
+    new_guest[...] = product(split(mixed), split(z))
+
+
+def second_sums(total_rows, x_in, z_guest_in, got, z_out, sums):
+    x = split(x_in[...])
+    z, _ = root(product(x, x, 1, 1), lambda: None)
+    z_out[...] = z
+    cross = split(from_tiles(got, 0, WIDE))
+    grams = from_tiles(got, 8, WIDE)
+    flipped = grams.T
+    rows, cols = square_index()
+    of_keep = split(jnp.where(rows <= cols, grams, flipped))
+    of_guest = jnp.where(rows > cols, grams, flipped)
+    of_guest = split(jnp.where(rows == cols, guest_squares(got), of_guest))
+    z_guest = z_guest_in[...]
+    zs, zs_guest = split(z), split(z_guest)
+    v = product(x, zs, 0, 0)
+    w = product(x, zs_guest)
+    vs, ws = split(v), split(w)
+    sum_keep = jnp.sum(
+        z * (product(of_keep, zs) - 2.0 * product(cross, vs)) + v * product(of_guest, vs),
+        axis=0,
+        keepdims=True,
+    )
+    sum_guest = jnp.sum(
+        z_guest * product(of_guest, zs_guest)
+        + w * (product(of_keep, ws) + 2.0 * product(cross, zs_guest)),
+        axis=0,
+        keepdims=True,
+    )
+    four = [sum_keep[:, :128], sum_keep[:, 128:], sum_guest[:, :128], sum_guest[:, 128:]]
+    tile = jnp.maximum(jnp.concatenate(four + four, axis=0) / total_rows, 0.0)
+    for r in range(4 * N_COL // 8):
         sums[8 * r : 8 * r + 8, :] = tile
 
 
-def fold_sums(total_rows, got, out):
-    tile = got[0:8, :]
-    for r in range(1, 4 * N_ROW // 8):
-        tile += got[8 * r : 8 * r + 8, :]
-    four = (tile[0:4] + tile[4:8]) / total_rows
-    tile = jnp.concatenate([four, four], axis=0)
-    for r in range(4 * N_COL // 8):
-        out[8 * r : 8 * r + 8, :] = tile
+def second_keep(keep, guest, x_in, z_in, out):
+    x = split(x_in[...])
+    mixed = keep[...] - product(split(guest[...]), x, 1, 1)
+    out[...] = product(split(mixed), split(z_in[...]))
 
 
 def local(body, flops, *shapes):
@@ -178,14 +243,19 @@
     tiles = exchange(fold_all(exchange(sent, "row")), "row")
     move = local(first_move, 5 * one, (W, W))(matrix, tiles)
     guest = swapped(move)
-    keep = local(first_keep, 5 * one, (W, W))(matrix, tiles)
-    sent = local(pack_second, one, (PIECE * N_ROW, 128))(keep, guest)
-    tiles = exchange(fold_all(exchange(sent, "row")), "row")
-    keep, guest, sums = local(second, 10 * one, (W, W), (W, W), (4 * N_ROW, 128))(keep, guest, tiles)
-    back = swapped_back(guest)
-    sums = exchange(sums, "row")
-    means = local(functools.partial(fold_sums, total_rows), 1, (4 * N_COL, 128))(sums)
+    keep, gram = local(first_keep, 6 * one, (W, W), (W, W))(matrix, tiles)
+    sent = local(pack_second, 2 * one, (WIDE * N_ROW, 128))(keep, guest, gram)
+    folded = local(fold_wide, 1, (WIDE * N_ROW, 128))(exchange(sent, "row"))
+    got = exchange(folded, "row")
+    new_guest, x, z_guest = local(
+        functools.partial(second_guest, total_rows), 5 * one, (W, W), (W, W), (W, W)
+    )(keep, guest, got)
+    back = swapped_back(new_guest)
+    z, means = local(
+        functools.partial(second_sums, total_rows), 11 * one, (W, W), (4 * N_COL, 128)
+    )(x, z_guest, got)
     table = exchange(means, "col").reshape(N_COL, 4, 128)
+    keep = local(second_keep, 2 * one, (W, W))(keep, guest, x, z)
     odd = lax.axis_index("col") % 2 == 1
     final = jnp.concatenate([jnp.where(odd, back, keep), jnp.where(odd, keep, back)], axis=1)
     kept = table[:, :2].reshape(N_COL, W)

time: 134 us -> 132 us (0.985)
  waiting for transfers between devices: 31.5 us -> 27.4 us
  blocking collectives: 58.6 us -> 62.2 us
  starting transfers between devices: 31.6 us -> 29 us
  Pallas kernels: 7.83 us -> 9.56 us
    all_to_all x3 -> x2, waiting for transfers between devices: 22.2 us -> 15.4 us  [exchange(): lax.all_to_all(pieces.reshape(shape), axis, 0, 0, tiled=True)]
    all_to_all x3 -> x2, starting transfers between devices: 21.9 us -> 17.8 us  [exchange(): lax.all_to_all(pieces.reshape(shape), axis, 0, 0, tiled=True)]
    all_to_all x3, blocking collectives: 58.6 us -> 62.2 us  [exchange(): lax.all_to_all(pieces.reshape(shape), axis, 0, 0, tiled=True)]
    ppermute x1, waiting for transfers between devices: 0.01 us -> 3.16 us  [swapped_back(): lax.ppermute(block, 'col', [(c, (c + (-2 if c % 2 else 2)) % N_COL) for c...]
    pallas_call x8 -> x9, Pallas kernels: 7.83 us -> 9.56 us  [call(): pl.pallas_call(body, out_shape=out if len(out) > 1 else out[0], in_specs=...]
    ppermute x1, starting transfers between devices: 3.94 us -> 5.39 us  [swapped_back(): lax.ppermute(block, 'col', [(c, (c + (-2 if c % 2 else 2)) % N_COL) for c...]
  transfers between devices with their start and end apart: 5 -> 4, of which waited for: 4 -> 4; matrix products, arithmetic and copies ran while one was open for 1% -> 1% of each run, Pallas kernels for 1% -> 2%
where the time goes in v4:
time: 132 us
  blocking collectives  62.2 us (47%)
  starting transfers between devices  29 us (22%)
  waiting for transfers between devices  27.4 us (21%)
  Pallas kernels  9.56 us (7%)
  local copies, waits for them, and re-layouts  1.69 us (1%)
    all_to_all x3, blocking collectives, exchange(): lax.all_to_all(pieces.reshape(shape), axis, 0, 0, tiled=True)  62.2 us
    all_to_all x2, starting transfers between devices, exchange(): lax.all_to_all(pieces.reshape(shape), axis, 0, 0, tiled=True)  17.8 us
    all_to_all x2, waiting for transfers between devices, exchange(): lax.all_to_all(pieces.reshape(shape), axis, 0, 0, tiled=True)  15.4 us
    pallas_call x9, Pallas kernels, call(): pl.pallas_call(body, out_shape=out if len(out) > 1 else out[0], in_specs=...  9.56 us
    ppermute x1, waiting for transfers between devices, swapped(): lax.ppermute(block, 'col', [(c, (c + (2 if c % 2 else -2)) % N_COL) for c...  8.83 us
    ppermute x1, starting transfers between devices, swapped(): lax.ppermute(block, 'col', [(c, (c + (2 if c % 2 else -2)) % N_COL) for c...  5.81 us
    ppermute x1, starting transfers between devices, swapped_back(): lax.ppermute(block, 'col', [(c, (c + (-2 if c % 2 else 2)) % N_COL) for c...  5.39 us
    ppermute x1, waiting for transfers between devices, swapped_back(): lax.ppermute(block, 'col', [(c, (c + (-2 if c % 2 else 2)) % N_COL) for c...  3.16 us
  transfers between devices with their start and end apart: 4, of which 4 were waited for; matrix products, arithmetic and copies ran while one was open for 1% of the time, Pallas kernels for 2%

profile of v4, /device:TPU:1, one launch (start us, length us, event | category | flops | bytes accessed | tf_op | source)
XLA Modules:
  0.0 131.7 jit_solution(15188444641258980398)
XLA Ops:
  0.6 0.0 copy-start
  0.6 1.0 copy-done
  1.7 0.3 shard_map.41
  2.0 24.5 %all_to_all.25 = f32[64,1,1280]{2,1,0:T(1,128)S(1)} all-to-all(f32[64,1,1280]{2,1,0:T(1,128)S(1)} %bitcast.30), channel_id=1, replica_groups=mesh['col'=8,'row'=64] {'row'}, dimensions={0} | all-to-all | bytes 655360 | tf_op jit(solution)/shard_map/all_to_all | solution.py:235
  26.5 0.0 copy-start.1
  26.5 0.2 shard_map.42
  26.7 17.4 %all_to_all.26 = f32[64,8,128]{2,1,0:T(8,128)S(1)} all-to-all(f32[64,8,128]{2,1,0:T(8,128)S(1)} %bitcast.31), channel_id=1, replica_groups=mesh['col'=8,'row'=64] {'row'}, dimensions={0} | all-to-all | bytes 524288 | tf_op jit(solution)/shard_map/all_to_all | solution.py:235
  44.1 0.0 copy-done.1
  44.1 1.3 shard_map.44
  45.4 5.8 %collective-permute-start = (f32[256,256]{1,0:T(8,128)S(1)}, f32[256,256]{1,0:T(8,128)S(1)}, u32[]{:S(2)}, u32[]{:S(2)}) collective-permute-start(f32[256,256]{1,0:T(8,128)S(1)} %shard_map.44), channel_id=1, source_target_pairs={{0,384},{64,192},{128,0},{192,320},{256,128},{320,448},{384,256},{... | collective-permute-start | bytes 786440 | tf_op jit(solution)/shard_map/ppermute | solution.py:220
  51.2 1.7 %shard_map.43 = (f32[256,256]{1,0:T(8,128)S(1)}, f32[256,256]{1,0:T(8,128)S(1)}) custom-call(f32[256,512]{1,0:T(8,128)S(1)} %copy-done.1, f32[512,128]{1,0:T(8,128)S(1)} %bitcast.35), custom_call_target="tpu_custom_call" | custom-call | flops 603979776 | bytes 1310720 | tf_op jit(solution)/shard_map/pallas_call | solution.py:205
  53.0 8.8 %collective-permute-done.guest = f32[256,256]{1,0:T(8,128)S(1)} collective-permute-done((f32[256,256]{1,0:T(8,128)S(1)}, f32[256,256]{1,0:T(8,128)S(1)}, u32[]{:S(2)}, u32[]{:S(2)}) %collective-permute-start) | collective-permute-done | bytes 262176 | tf_op jit(solution)/shard_map/ppermute | solution.py:220
  61.8 0.4 shard_map.45
  62.2 20.3 %all_to_all.27 = f32[64,1,2176]{2,1,0:T(1,128)S(1)} all-to-all(f32[64,1,2176]{2,1,0:T(1,128)S(1)} %bitcast.27), channel_id=1, replica_groups=mesh['col'=8,'row'=64] {'row'}, dimensions={0} | all-to-all | bytes 1114112 | tf_op jit(solution)/shard_map/all_to_all | solution.py:235
  82.5 0.9 shard_map.46
  83.4 7.1 %all-to-all-start.3 = ((f32[64,1,2176]{2,1,0:T(1,128)}), f32[64,1,2176]{2,1,0:T(1,128)S(1)}, u32[]{:S(2)}, u32[]{:S(2)}) async-start(f32[64,1,2176]{2,1,0:T(1,128)} %bitcast.6), calls=%async_computation.3 | async-start | bytes 1114112 | tf_op jit(solution)/shard_map/all_to_all | solution.py:235
  90.6 14.4 %all-to-all-done.3 = f32[64,1,2176]{2,1,0:T(1,128)S(1)} async-done(((f32[64,1,2176]{2,1,0:T(1,128)}), f32[64,1,2176]{2,1,0:T(1,128)S(1)}, u32[]{:S(2)}, u32[]{:S(2)}) %all-to-all-start.3) | async-done | bytes 557088 | tf_op jit(solution)/shard_map/all_to_all | solution.py:235
  104.9 1.4 %shard_map.47 = (f32[256,256]{1,0:T(8,128)S(1)}, f32[256,256]{1,0:T(8,128)S(1)}, f32[256,256]{1,0:T(8,128)S(1)}) custom-call(f32[256,256]{1,0:T(8,128)S(1)} %get-tuple-element.9.keep, f32[256,256]{1,0:T(8,128)S(1)} %collective-permute-done.guest, f32[1088,128]{1,0:T(8,128)S(1)} %bitcast.32), custom_call_target="tpu_custom_call" | custom-call | flops 503316480 | bytes 1867776 | tf_op jit(solution)/shard_map/pallas_call | solution.py:205
  106.3 2.7 %shard_map.48 = (f32[256,256]{1,0:T(8,128)S(1)}, f32[32,128]{1,0:T(8,128)}) custom-call(f32[256,256]{1,0:T(8,128)S(1)} %get-tuple-element.12.x_in, f32[256,256]{1,0:T(8,128)S(1)} %get-tuple-element.13.z_guest_in, f32[1088,128]{1,0:T(8,128)S(1)} %bitcast.33), custom_call_target="tpu_custom_call" | custom-call | flops 1107296256 | bytes 1359872 | tf_op jit(solution)/shard_map/pallas_call | solution.py:205
  109.0 0.0 copy-start.2
  109.0 10.7 %all-to-all-start.4 = ((f32[8,4,128]{2,1,0:T(4,128)}), f32[8,4,128]{2,1,0:T(4,128)S(1)}, u32[]{:S(2)}, u32[]{:S(2)}) async-start(f32[8,4,128]{2,1,0:T(4,128)} %bitcast.8), calls=%async_computation.4 | async-start | bytes 32768 | tf_op jit(solution)/shard_map/all_to_all | solution.py:235
  119.7 0.0 copy-done.2
  119.7 0.1 broadcast_compare_fusion
  119.8 5.4 %collective-permute-start.1 = (f32[256,256]{1,0:T(8,128)S(1)}, f32[256,256]{1,0:T(8,128)S(1)}, u32[]{:S(2)}, u32[]{:S(2)}) collective-permute-start(f32[256,256]{1,0:T(8,128)S(1)} %get-tuple-element.11), channel_id=1, source_target_pairs={{0,128},{64,448},{128,256},{192,64},{256,384},{320,192},{384,0},{4... | collective-permute-start | bytes 786440 | tf_op jit(solution)/shard_map/ppermute | solution.py:226
  125.2 0.6 shard_map.49
  125.8 1.0 all-to-all-done.4
  126.9 0.1 stack.3
  126.9 0.1 select_reduce_fusion
  127.0 0.6 copy.10
  127.6 3.2 %collective-permute-done.1 = f32[256,256]{1,0:T(8,128)S(1)} collective-permute-done((f32[256,256]{1,0:T(8,128)S(1)}, f32[256,256]{1,0:T(8,128)S(1)}, u32[]{:S(2)}, u32[]{:S(2)}) %collective-permute-start.1) | collective-permute-done | bytes 262176 | tf_op jit(solution)/shard_map/ppermute | solution.py:226
  130.8 0.9 pad_maximum_fusion
  (3 shorter events, 0.0 us)
Async XLA Ops:
  0.6 1.0 copy-start
  26.5 17.6 %copy-start.1 = (f32[256,512]{1,0:T(8,128)S(1)}, f32[256,512]{1,0:T(8,128)}, u32[]{:S(2)}) copy-start(f32[256,512]{1,0:T(8,128)} %matrix.5) | copy-start | bytes 1572868
  45.4 16.4 %collective-permute-start = (f32[256,256]{1,0:T(8,128)S(1)}, f32[256,256]{1,0:T(8,128)S(1)}, u32[]{:S(2)}, u32[]{:S(2)}) collective-permute-start(f32[256,256]{1,0:T(8,128)S(1)} %shard_map.44), channel_id=1, source_target_pairs={{0,384},{64,192},{128,0},{192,320},{256,128},{320,448},{384,256},{... | collective-permute-start | bytes 786440 | tf_op jit(solution)/shard_map/ppermute | solution.py:220
  83.4 21.5 %all-to-all-start.3 = ((f32[64,1,2176]{2,1,0:T(1,128)}), f32[64,1,2176]{2,1,0:T(1,128)S(1)}, u32[]{:S(2)}, u32[]{:S(2)}) async-start(f32[64,1,2176]{2,1,0:T(1,128)} %bitcast.6), calls=%async_computation.3 | async-start | bytes 1114112 | tf_op jit(solution)/shard_map/all_to_all | solution.py:235
  109.0 10.7 %copy-start.2 = (s32[16]{0:T(128)S(1)}, s32[16]{0:T(128)}, u32[]{:S(2)}) copy-start(s32[16]{0:T(128)} %param.3) | copy-start | bytes 196
  109.0 17.9 %all-to-all-start.4 = ((f32[8,4,128]{2,1,0:T(4,128)}), f32[8,4,128]{2,1,0:T(4,128)S(1)}, u32[]{:S(2)}, u32[]{:S(2)}) async-start(f32[8,4,128]{2,1,0:T(4,128)} %bitcast.8), calls=%async_computation.4 | async-start | bytes 32768 | tf_op jit(solution)/shard_map/all_to_all | solution.py:235
  119.8 11.0 %collective-permute-start.1 = (f32[256,256]{1,0:T(8,128)S(1)}, f32[256,256]{1,0:T(8,128)S(1)}, u32[]{:S(2)}, u32[]{:S(2)}) collective-permute-start(f32[256,256]{1,0:T(8,128)S(1)} %get-tuple-element.11), channel_id=1, source_target_pairs={{0,128},{64,448},{128,256},{192,64},{256,384},{320,192},{384,0},{4... | collective-permute-start | bytes 786440 | tf_op jit(solution)/shard_map/ppermute | solution.py:226

commit v5 on v4

--- a/solution.py
+++ b/solution.py
@@ -12,7 +12,9 @@
 N_COL = 8
 PIECE = 10
 WIDE = 17
+LOADS = 8
 LIMIT = 32 * 1024 * 1024
+LOAD_LIMIT = 56000000
 
 
 def split(a):
@@ -64,7 +66,18 @@
     return keep, move
 
 
-def pack_first(matrix, out):
+def pack_first(whole, out, matrix, arrived):
+    rows = W // LOADS
+    copies = [
+        pltpu.make_async_copy(
+            whole.at[pl.ds(k * rows, rows)], matrix.at[pl.ds(k * rows, rows)], arrived.at[k]
+        )
+        for k in range(LOADS)
+    ]
+    for copy in copies:
+        copy.start()
+    for copy in copies:
+        copy.wait()
     keep, move = halves(matrix)
     cross = product(split(keep), split(move), 0, 0)
     norm_keep, norm_move = column_squares(keep), column_squares(move)
@@ -128,7 +141,13 @@
     out[...] = product(split(mixed), split(z))
 
 
-def first_keep(matrix, tiles, out, gram):
+def first_keep(matrix, tiles, seats, out, gram, hits):
+    first = 2 * lax.axis_index("col")
+    for k in range(2):
+        for seat in range(2 * N_COL):
+            at = 2 * N_COL * k + seat
+            hit = jnp.where(seats[seat] == first + k, 1.0, 0.0).astype(jnp.float32)
+            hits[at : at + 1, :] = jnp.full((1, 128), hit)
     keep, move = halves(matrix)
     x = split(from_tiles(tiles, 0, 8))
     z, mixed = root(product(x, x, 1, 1), lambda: keep - product(split(move), x, 1, 1))
@@ -158,10 +177,20 @@
     new_guest[...] = product(split(mixed), split(z))
 
 
-def second_sums(total_rows, x_in, z_guest_in, got, z_out, sums):
+def half_of(ref, odd):
+    return ref.at[:, pl.ds(pl.multiple_of(odd * W, W), W)]
+
+
+def second_sums(total_rows, x_in, z_guest_in, got, keep, guest, sums, final, kept, done):
     x = split(x_in[...])
-    z, _ = root(product(x, x, 1, 1), lambda: None)
-    z_out[...] = z
+    z, mixed = root(
+        product(x, x, 1, 1), lambda: keep[...] - product(split(guest[...]), x, 1, 1)
+    )
+    zs = split(z)
+    kept[...] = product(split(mixed), zs)
+    odd = lax.rem(lax.axis_index("col"), 2)
+    copy = pltpu.make_async_copy(kept, half_of(final, odd), done)
+    copy.start()
     cross = split(from_tiles(got, 0, WIDE))
     grams = from_tiles(got, 8, WIDE)
     flipped = grams.T
@@ -170,7 +199,7 @@
     of_guest = jnp.where(rows > cols, grams, flipped)
     of_guest = split(jnp.where(rows == cols, guest_squares(got), of_guest))
     z_guest = z_guest_in[...]
-    zs, zs_guest = split(z), split(z_guest)
+    zs_guest = split(z_guest)
     v = product(x, zs, 0, 0)
     w = product(x, zs_guest)
     vs, ws = split(v), split(w)
@@ -189,28 +218,48 @@
     tile = jnp.maximum(jnp.concatenate(four + four, axis=0) / total_rows, 0.0)
     for r in range(4 * N_COL // 8):
         sums[8 * r : 8 * r + 8, :] = tile
-
-
-def second_keep(keep, guest, x_in, z_in, out):
-    x = split(x_in[...])
-    mixed = keep[...] - product(split(guest[...]), x, 1, 1)
-    out[...] = product(split(mixed), split(z_in[...]))
-
-
-def local(body, flops, *shapes):
+    copy.wait()
+
+
+def finish(hits, back, table, begun, final, means, done):
+    del begun
+    col = lax.axis_index("col")
+    copy = pltpu.make_async_copy(back, half_of(final, 1 - lax.rem(col, 2)), done)
+    copy.start()
+    for k in range(2):
+        picked = jnp.zeros((2, 128), jnp.float32)
+        for c in range(N_COL):
+            kept = table[4 * c : 4 * c + 2, :]
+            at = 4 * ((c + (2 if c % 2 else -2)) % N_COL) + 2
+            hosted = table[at : at + 2, :]
+            for b, part in enumerate((hosted, kept) if c % 2 else (kept, hosted)):
+                seat = 2 * N_COL * k + 2 * c + b
+                picked += jnp.where(hits[seat : seat + 1, :] > 0.5, part, 0.0)
+        means[2 * k : 2 * k + 2, :] = picked
+    copy.wait()
+
+
+VMEM = pl.BlockSpec(memory_space=pltpu.VMEM)
+SMEM = pl.BlockSpec(memory_space=pltpu.SMEM)
+HBM = pl.BlockSpec(memory_space=pltpu.HBM)
+
+
+def local(body, flops, *shapes, ins=None, outs=None, scratch=(), aliases=None, limit=LIMIT):
     out = [jax.ShapeDtypeStruct(shape, jnp.float32) for shape in shapes]
+    outs = outs or [VMEM] * len(out)
+    one = len(out) == 1
 
     def call(*args):
         moved = sum(4 * a.size for a in args) + sum(4 * s.size for s in out)
         return pl.pallas_call(
             body,
-            out_shape=out if len(out) > 1 else out[0],
-            in_specs=[pl.BlockSpec(memory_space=pltpu.VMEM)] * len(args),
-            out_specs=[pl.BlockSpec(memory_space=pltpu.VMEM)] * len(out)
-            if len(out) > 1
-            else pl.BlockSpec(memory_space=pltpu.VMEM),
+            out_shape=out[0] if one else out,
+            in_specs=ins or [VMEM] * len(args),
+            out_specs=outs[0] if one else outs,
+            scratch_shapes=scratch,
+            input_output_aliases=aliases or {},
             cost_estimate=pl.CostEstimate(flops=flops, bytes_accessed=moved, transcendentals=0),
-            compiler_params=pltpu.CompilerParams(vmem_limit_bytes=LIMIT),
+            compiler_params=pltpu.CompilerParams(vmem_limit_bytes=limit),
         )(*args)
 
     return call
@@ -239,11 +288,20 @@
     total_rows = matrix.shape[0] * N_ROW
     one = 6 * W**3
     fold_all = local(functools.partial(fold, total_rows), 1, (8 * N_ROW, 128))
-    sent = local(pack_first, one, (PIECE * N_ROW, 128))(matrix)
+    sent = local(
+        pack_first,
+        one,
+        (PIECE * N_ROW, 128),
+        ins=[HBM],
+        limit=LOAD_LIMIT,
+        scratch=[pltpu.VMEM((W, 2 * W), jnp.float32), pltpu.SemaphoreType.DMA((LOADS,))],
+    )(matrix)
     tiles = exchange(fold_all(exchange(sent, "row")), "row")
     move = local(first_move, 5 * one, (W, W))(matrix, tiles)
     guest = swapped(move)
-    keep, gram = local(first_keep, 6 * one, (W, W), (W, W))(matrix, tiles)
+    keep, gram, hits = local(
+        first_keep, 6 * one, (W, W), (W, W), (4 * N_COL, 128), ins=[VMEM, VMEM, SMEM]
+    )(matrix, tiles, seats)
     sent = local(pack_second, 2 * one, (WIDE * N_ROW, 128))(keep, guest, gram)
     folded = local(fold_wide, 1, (WIDE * N_ROW, 128))(exchange(sent, "row"))
     got = exchange(folded, "row")
@@ -251,23 +309,25 @@
         functools.partial(second_guest, total_rows), 5 * one, (W, W), (W, W), (W, W)
     )(keep, guest, got)
     back = swapped_back(new_guest)
-    z, means = local(
-        functools.partial(second_sums, total_rows), 11 * one, (W, W), (4 * N_COL, 128)
-    )(x, z_guest, got)
-    table = exchange(means, "col").reshape(N_COL, 4, 128)
-    keep = local(second_keep, 2 * one, (W, W))(keep, guest, x, z)
-    odd = lax.axis_index("col") % 2 == 1
-    final = jnp.concatenate([jnp.where(odd, back, keep), jnp.where(odd, keep, back)], axis=1)
-    kept = table[:, :2].reshape(N_COL, W)
-    guests = table[:, 2:].reshape(N_COL, W)
-    rows = []
-    for c in range(N_COL):
-        rows.append(guests[(c + 2) % N_COL] if c % 2 else kept[c])
-        rows.append(kept[c] if c % 2 else guests[(c - 2) % N_COL])
-    by_seat = jnp.stack(rows)
-    wanted = 2 * lax.axis_index("col") + jnp.arange(2, dtype=jnp.int32)
-    hit = seats[None, :] == wanted[:, None]
-    picked = jnp.sum(jnp.where(hit[:, :, None], by_seat[None], 0.0), axis=1)
+    means, begun = local(
+        functools.partial(second_sums, total_rows),
+        13 * one,
+        (4 * N_COL, 128),
+        (W, 2 * W),
+        outs=[VMEM, HBM],
+        scratch=[pltpu.VMEM((W, W), jnp.float32), pltpu.SemaphoreType.DMA],
+    )(x, z_guest, got, keep, guest)
+    table = exchange(means, "col")
+    final, picked = local(
+        finish,
+        1,
+        (W, 2 * W),
+        (4, 128),
+        ins=[VMEM, VMEM, VMEM, HBM],
+        outs=[HBM, VMEM],
+        scratch=[pltpu.SemaphoreType.DMA],
+        aliases={3: 0},
+    )(hits, back, table, begun)
     return (final, picked.reshape(2 * W))
 
 

time: 132 us -> 129 us (0.977)
  blocking collectives: 62.2 us -> 101 us
  starting transfers between devices: 29 us -> 7.73 us
  waiting for transfers between devices: 27.4 us -> 8.27 us
  local copies, waits for them, and re-layouts: 1.69 us -> 0.01 us
    all_to_all x3 -> x5, blocking collectives: 62.2 us -> 101 us  [exchange(): lax.all_to_all(pieces.reshape(shape), axis, 0, 0, tiled=True)]
    all_to_all x2 -> x0, starting transfers between devices: 17.8 us -> none  [exchange(): lax.all_to_all(pieces.reshape(shape), axis, 0, 0, tiled=True)]
    all_to_all x2 -> x0, waiting for transfers between devices: 15.4 us -> none  [exchange(): lax.all_to_all(pieces.reshape(shape), axis, 0, 0, tiled=True)]
    ppermute x1, starting transfers between devices: 5.39 us -> 1.92 us  [swapped_back(): lax.ppermute(block, 'col', [(c, (c + (-2 if c % 2 else 2)) % N_COL) for c...]
    ppermute x1, waiting for transfers between devices: 3.16 us -> 0.01 us  [swapped_back(): lax.ppermute(block, 'col', [(c, (c + (-2 if c % 2 else 2)) % N_COL) for c...]
    unnamed x7 -> x4, local copies, waits for them, and re-layouts: 1.63 us -> 0.01 us
  transfers between devices with their start and end apart: 4 -> 2, of which waited for: 4 -> 1; matrix products, arithmetic and copies ran while one was open for 1% -> 0% of each run, Pallas kernels for 2% -> 3%
where the time goes in v5:
time: 129 us
  blocking collectives  101 us (78%)
  Pallas kernels  10.6 us (8%)
  waiting for transfers between devices  8.27 us (6%)
  starting transfers between devices  7.73 us (6%)
    all_to_all x5, blocking collectives, exchange(): lax.all_to_all(pieces.reshape(shape), axis, 0, 0, tiled=True)  101 us
    pallas_call x9, Pallas kernels, call(): pl.pallas_call(body, out_shape=out[0] if one else out, in_specs=ins or [V...  10.6 us
    ppermute x1, waiting for transfers between devices, swapped(): lax.ppermute(block, 'col', [(c, (c + (2 if c % 2 else -2)) % N_COL) for c...  8.27 us
    ppermute x1, starting transfers between devices, swapped(): lax.ppermute(block, 'col', [(c, (c + (2 if c % 2 else -2)) % N_COL) for c...  5.81 us
  transfers between devices with their start and end apart: 2, of which 1 were waited for; matrix products, arithmetic and copies ran while one was open for 0% of the time, Pallas kernels for 3%

profile of v5, /device:TPU:1, one launch (start us, length us, event | category | flops | bytes accessed | tf_op | source)
XLA Modules:
  0.0 128.8 jit_solution(6567961527308832123)
XLA Ops:
  0.6 1.5 %shard_map.41 = f32[640,128]{1,0:T(8,128)S(1)} custom-call(f32[256,512]{1,0:T(8,128)} %matrix.3), custom_call_target="tpu_custom_call" | custom-call | flops 100663296 | bytes 851968 | tf_op jit(solution)/shard_map/pallas_call | solution.py:254
  2.1 24.5 %all_to_all.25 = f32[64,1,1280]{2,1,0:T(1,128)S(1)} all-to-all(f32[64,1,1280]{2,1,0:T(1,128)S(1)} %bitcast.15), channel_id=1, replica_groups=mesh['col'=8,'row'=64] {'row'}, dimensions={0} | all-to-all | bytes 655360 | tf_op jit(solution)/shard_map/all_to_all | solution.py:284
  26.6 0.0 copy-start
  26.6 0.2 shard_map.42
  26.8 17.4 %all_to_all.26 = f32[64,8,128]{2,1,0:T(8,128)S(1)} all-to-all(f32[64,8,128]{2,1,0:T(8,128)S(1)} %bitcast.16), channel_id=1, replica_groups=mesh['col'=8,'row'=64] {'row'}, dimensions={0} | all-to-all | bytes 524288 | tf_op jit(solution)/shard_map/all_to_all | solution.py:284
  44.2 0.0 copy-done
  44.2 0.0 copy-start.1
  44.2 1.3 %shard_map.44 = f32[256,256]{1,0:T(8,128)S(1)} custom-call(f32[256,512]{1,0:T(8,128)S(1)} %copy-done, f32[512,128]{1,0:T(8,128)S(1)} %bitcast.19), custom_call_target="tpu_custom_call" | custom-call | flops 503316480 | bytes 1048576 | tf_op jit(solution)/shard_map/pallas_call | solution.py:254
  45.5 5.8 %collective-permute-start = (f32[256,256]{1,0:T(8,128)S(1)}, f32[256,256]{1,0:T(8,128)S(1)}, u32[]{:S(2)}, u32[]{:S(2)}) collective-permute-start(f32[256,256]{1,0:T(8,128)S(1)} %shard_map.44), channel_id=1, source_target_pairs={{0,384},{64,192},{128,0},{192,320},{256,128},{320,448},{384,256},{... | collective-permute-start | bytes 786440 | tf_op jit(solution)/shard_map/ppermute | solution.py:269
  51.3 0.0 copy-done.1
  51.3 2.3 %shard_map.43 = (f32[256,256]{1,0:T(8,128)S(1)}, f32[256,256]{1,0:T(8,128)S(1)}, f32[32,128]{1,0:T(8,128)S(1)}) custom-call(f32[256,512]{1,0:T(8,128)S(1)} %copy-done, f32[512,128]{1,0:T(8,128)S(1)} %bitcast.20, s32[16]{0:T(128)S(1)} %copy-done.1), custom_call_target="tpu_custom_call" | custom-call | flops 603979776 | bytes 1327168 | tf_op jit(solution)/shard_map/pallas_call | solution.py:254
  53.6 8.3 %collective-permute-done.guest = f32[256,256]{1,0:T(8,128)S(1)} collective-permute-done((f32[256,256]{1,0:T(8,128)S(1)}, f32[256,256]{1,0:T(8,128)S(1)}, u32[]{:S(2)}, u32[]{:S(2)}) %collective-permute-start) | collective-permute-done | bytes 262176 | tf_op jit(solution)/shard_map/ppermute | solution.py:269
  61.9 0.4 shard_map.45
  62.3 20.3 %all_to_all.27 = f32[64,1,2176]{2,1,0:T(1,128)S(1)} all-to-all(f32[64,1,2176]{2,1,0:T(1,128)S(1)} %bitcast.11), channel_id=1, replica_groups=mesh['col'=8,'row'=64] {'row'}, dimensions={0} | all-to-all | bytes 1114112 | tf_op jit(solution)/shard_map/all_to_all | solution.py:284
  82.6 0.1 shard_map.46
  82.7 21.3 %all_to_all.28 = f32[64,1,2176]{2,1,0:T(1,128)S(1)} all-to-all(f32[64,1,2176]{2,1,0:T(1,128)S(1)} %bitcast.13), channel_id=1, replica_groups=mesh['col'=8,'row'=64] {'row'}, dimensions={0} | all-to-all | bytes 1114112 | tf_op jit(solution)/shard_map/all_to_all | solution.py:284
  104.0 1.4 %shard_map.47 = (f32[256,256]{1,0:T(8,128)S(1)}, f32[256,256]{1,0:T(8,128)S(1)}, f32[256,256]{1,0:T(8,128)S(1)}) custom-call(f32[256,256]{1,0:T(8,128)S(1)} %get-tuple-element.13.keep, f32[256,256]{1,0:T(8,128)S(1)} %collective-permute-done.guest, f32[1088,128]{1,0:T(8,128)S(1)} %bitcast.17), custom_call_target="tpu_custom_call" | custom-call | flops 503316480 | bytes 1867776 | tf_op jit(solution)/shard_map/pallas_call | solution.py:254
  105.4 1.9 %collective-permute-start.1 = (f32[256,256]{1,0:T(8,128)S(1)}, f32[256,256]{1,0:T(8,128)S(1)}, u32[]{:S(2)}, u32[]{:S(2)}) collective-permute-start(f32[256,256]{1,0:T(8,128)S(1)} %get-tuple-element.15), channel_id=1, source_target_pairs={{0,128},{64,448},{128,256},{192,64},{256,384},{320,192},{384,0},{4... | collective-permute-start | bytes 786440 | tf_op jit(solution)/shard_map/ppermute | solution.py:275
  107.4 2.2 %shard_map.48 = (f32[32,128]{1,0:T(8,128)S(1)}, f32[256,512]{1,0:T(8,128)}) custom-call(f32[256,256]{1,0:T(8,128)S(1)} %get-tuple-element.16.x_in, f32[256,256]{1,0:T(8,128)S(1)} %get-tuple-element.17.z_guest_in, f32[1088,128]{1,0:T(8,128)S(1)} %bitcast.18, f32[256,256]{1,0:T(8,128)S(1)} %get-tuple-element.13.keep, f32[256,256]{1,0:T(8,128)S(1)} %collective-permute-done.guest), custom_call_target="tpu_custom_call" | custom-call | flops 1308622848 | bytes 2146304 | tf_op jit(solution)/shard_map/pallas_call | solution.py:254
  109.5 18.0 %all_to_all.29 = f32[8,4,128]{2,1,0:T(4,128)S(1)} all-to-all(f32[8,4,128]{2,1,0:T(4,128)S(1)} %bitcast.22), channel_id=1, replica_groups=mesh['col'=8,'row'=64] {'col'}, dimensions={0} | all-to-all | bytes 32768 | tf_op jit(solution)/shard_map/all_to_all | solution.py:284
  127.5 0.0 collective-permute-done.1.back
  127.5 1.3 %shard_map.49 = (f32[256,512]{1,0:T(8,128)}, f32[4,128]{1,0:T(4,128)}) custom-call(f32[32,128]{1,0:T(8,128)S(1)} %get-tuple-element.12.hits, f32[256,256]{1,0:T(8,128)S(1)} %collective-permute-done.1.back, f32[32,128]{1,0:T(8,128)S(1)} %bitcast.21, f32[256,512]{1,0:T(8,128)} %get-tuple-element.19.begun), custom_call_target="tpu_custom_call", output_to_operand_aliasing={{0}: (3, {})} | custom-call | flops 1 | bytes 1345536 | tf_op jit(solution)/shard_map/pallas_call | solution.py:254
Async XLA Ops:
  26.6 17.6 %copy-start = (f32[256,512]{1,0:T(8,128)S(1)}, f32[256,512]{1,0:T(8,128)}, u32[]{:S(2)}) copy-start(f32[256,512]{1,0:T(8,128)} %matrix.3) | copy-start | bytes 1572868
  44.2 7.1 %copy-start.1 = (s32[16]{0:T(128)S(1)}, s32[16]{0:T(128)}, u32[]{:S(2)}) copy-start(s32[16]{0:T(128)} %seats.1) | copy-start | bytes 196
  45.5 16.4 %collective-permute-start = (f32[256,256]{1,0:T(8,128)S(1)}, f32[256,256]{1,0:T(8,128)S(1)}, u32[]{:S(2)}, u32[]{:S(2)}) collective-permute-start(f32[256,256]{1,0:T(8,128)S(1)} %shard_map.44), channel_id=1, source_target_pairs={{0,384},{64,192},{128,0},{192,320},{256,128},{320,448},{384,256},{... | collective-permute-start | bytes 786440 | tf_op jit(solution)/shard_map/ppermute | solution.py:269
  105.4 22.1 %collective-permute-start.1 = (f32[256,256]{1,0:T(8,128)S(1)}, f32[256,256]{1,0:T(8,128)S(1)}, u32[]{:S(2)}, u32[]{:S(2)}) collective-permute-start(f32[256,256]{1,0:T(8,128)S(1)} %get-tuple-element.15), channel_id=1, source_target_pairs={{0,128},{64,448},{128,256},{192,64},{256,384},{320,192},{384,0},{4... | collective-permute-start | bytes 786440 | tf_op jit(solution)/shard_map/ppermute | solution.py:275

commit v6 on v5

--- a/solution.py
+++ b/solution.py
@@ -53,6 +53,17 @@
     return jnp.concatenate(
         [jnp.concatenate(left, axis=0), jnp.concatenate(right, axis=0)], axis=1
     )
+
+
+def roots(*squares):
+    parts = [split(s) for s in squares]
+    seconds = [product(p, p) for p in parts]
+    rows, cols = square_index()
+    eye = jnp.where(rows == cols, 1.0, 0.0).astype(jnp.float32)
+    return [
+        eye - 0.5 * s + 0.375 * s2 + product(split(s2), split(0.0625 * s2 - 0.3125 * s))
+        for s, s2 in zip(squares, seconds)
+    ]
 
 
 def column_squares(block):
@@ -162,7 +173,7 @@
     return jnp.concatenate([got[16:17, :], got[at : at + 1, :]], axis=1)
 
 
-def second_guest(total_rows, keep, guest, got, new_guest, x_out, z_out):
+def second_guest(total_rows, keep, guest, got, new_guest, x_out, z_keep_out, z_guest_out):
     cross = from_tiles(got, 0, WIDE)
     rows, cols = square_index()
     on_diagonal = jnp.where(rows == cols, from_tiles(got, 8, WIDE), 0.0)
@@ -171,22 +182,30 @@
     sign = jnp.where(lax.rem(lax.axis_index("col"), 2) == 1, -0.5, 0.5) / total_rows
     x = cross * (sign * lax.rsqrt(mean_keep + 1e-06)) * lax.rsqrt(mean_guest + 1e-06)
     x_out[...] = x
+    flipped = split(x.T)
     x = split(x)
-    z, mixed = root(product(x, x, 0, 0), lambda: guest[...] + product(split(keep[...]), x))
-    z_out[...] = z
-    new_guest[...] = product(split(mixed), split(z))
+    s_guest = product(flipped, flipped, 1, 1)
+    s_keep = product(x, x, 1, 1)
+    mixed = guest[...] + product(split(keep[...]), x)
+    z_guest, z_keep = roots(s_guest, s_keep)
+    z_guest_out[...] = z_guest
+    z_keep_out[...] = z_keep
+    new_guest[...] = product(split(mixed), split(z_guest))
 
 
 def half_of(ref, odd):
     return ref.at[:, pl.ds(pl.multiple_of(odd * W, W), W)]
 
 
-def second_sums(total_rows, x_in, z_guest_in, got, keep, guest, sums, final, kept, done):
-    x = split(x_in[...])
-    z, mixed = root(
-        product(x, x, 1, 1), lambda: keep[...] - product(split(guest[...]), x, 1, 1)
-    )
+def second_sums(
+    total_rows, x_in, z_keep_in, z_guest_in, got, keep, guest, sums, final, kept, done
+):
+    x = x_in[...]
+    flipped_x = split(x.T)
+    x = split(x)
+    z = z_keep_in[...]
     zs = split(z)
+    mixed = keep[...] - product(split(guest[...]), x, 1, 1)
     kept[...] = product(split(mixed), zs)
     odd = lax.rem(lax.axis_index("col"), 2)
     copy = pltpu.make_async_copy(kept, half_of(final, odd), done)
@@ -200,7 +219,7 @@
     of_guest = split(jnp.where(rows == cols, guest_squares(got), of_guest))
     z_guest = z_guest_in[...]
     zs_guest = split(z_guest)
-    v = product(x, zs, 0, 0)
+    v = product(flipped_x, zs)
     w = product(x, zs_guest)
     vs, ws = split(v), split(w)
     sum_keep = jnp.sum(
@@ -221,22 +240,25 @@
     copy.wait()
 
 
-def finish(hits, back, table, begun, final, means, done):
+def finish(hits, back, table, begun, final, means, picked, done):
     del begun
     col = lax.axis_index("col")
-    copy = pltpu.make_async_copy(back, half_of(final, 1 - lax.rem(col, 2)), done)
+    copy = pltpu.make_async_copy(back, half_of(final, 1 - lax.rem(col, 2)), done.at[0])
     copy.start()
     for k in range(2):
-        picked = jnp.zeros((2, 128), jnp.float32)
+        one = jnp.zeros((2, 128), jnp.float32)
         for c in range(N_COL):
             kept = table[4 * c : 4 * c + 2, :]
             at = 4 * ((c + (2 if c % 2 else -2)) % N_COL) + 2
             hosted = table[at : at + 2, :]
             for b, part in enumerate((hosted, kept) if c % 2 else (kept, hosted)):
                 seat = 2 * N_COL * k + 2 * c + b
-                picked += jnp.where(hits[seat : seat + 1, :] > 0.5, part, 0.0)
-        means[2 * k : 2 * k + 2, :] = picked
+                one += jnp.where(hits[seat : seat + 1, :] > 0.5, part, 0.0)
+        picked[2 * k : 2 * k + 2, :] = one
+    means_copy = pltpu.make_async_copy(picked, means, done.at[1])
+    means_copy.start()
     copy.wait()
+    means_copy.wait()
 
 
 VMEM = pl.BlockSpec(memory_space=pltpu.VMEM)
@@ -305,18 +327,18 @@
     sent = local(pack_second, 2 * one, (WIDE * N_ROW, 128))(keep, guest, gram)
     folded = local(fold_wide, 1, (WIDE * N_ROW, 128))(exchange(sent, "row"))
     got = exchange(folded, "row")
-    new_guest, x, z_guest = local(
-        functools.partial(second_guest, total_rows), 5 * one, (W, W), (W, W), (W, W)
+    new_guest, x, z_keep, z_guest = local(
+        functools.partial(second_guest, total_rows), 8 * one, (W, W), (W, W), (W, W), (W, W)
     )(keep, guest, got)
     back = swapped_back(new_guest)
     means, begun = local(
         functools.partial(second_sums, total_rows),
-        13 * one,
+        10 * one,
         (4 * N_COL, 128),
         (W, 2 * W),
         outs=[VMEM, HBM],
         scratch=[pltpu.VMEM((W, W), jnp.float32), pltpu.SemaphoreType.DMA],
-    )(x, z_guest, got, keep, guest)
+    )(x, z_keep, z_guest, got, keep, guest)
     table = exchange(means, "col")
     final, picked = local(
         finish,
@@ -324,8 +346,8 @@
         (W, 2 * W),
         (4, 128),
         ins=[VMEM, VMEM, VMEM, HBM],
-        outs=[HBM, VMEM],
-        scratch=[pltpu.SemaphoreType.DMA],
+        outs=[HBM, HBM],
+        scratch=[pltpu.VMEM((4, 128), jnp.float32), pltpu.SemaphoreType.DMA((2,))],
         aliases={3: 0},
     )(hits, back, table, begun)
     return (final, picked.reshape(2 * W))

time: 129 us -> 129 us (level)
  no operation moved by 1% of the time
where the time goes in v6:
time: 129 us; the launch traced here: 128 us
  blocking collectives  101 us (78%)
  Pallas kernels  10 us (8%)
  waiting for transfers between devices  8.27 us (6%)
  starting transfers between devices  7.73 us (6%)
    all_to_all x5, blocking collectives, exchange(): lax.all_to_all(pieces.reshape(shape), axis, 0, 0, tiled=True)  101 us
    pallas_call x9, Pallas kernels, call(): pl.pallas_call(body, out_shape=out[0] if one else out, in_specs=ins or [V...  10 us
    ppermute x1, waiting for transfers between devices, swapped(): lax.ppermute(block, 'col', [(c, (c + (2 if c % 2 else -2)) % N_COL) for c...  8.27 us
    ppermute x1, starting transfers between devices, swapped(): lax.ppermute(block, 'col', [(c, (c + (2 if c % 2 else -2)) % N_COL) for c...  5.81 us
  transfers between devices with their start and end apart: 2, of which 1 were waited for; matrix products, arithmetic and copies ran while one was open for 0% of the time, Pallas kernels for 3%

profile of v6, /device:TPU:1, one launch (start us, length us, event | category | flops | bytes accessed | tf_op | source)
XLA Modules:
  0.0 128.2 jit_solution(1745134270508427094)
XLA Ops:
  0.6 1.5 %shard_map.41 = f32[640,128]{1,0:T(8,128)S(1)} custom-call(f32[256,512]{1,0:T(8,128)} %matrix.3), custom_call_target="tpu_custom_call" | custom-call | flops 100663296 | bytes 851968 | tf_op jit(solution)/shard_map/pallas_call | solution.py:276
  2.1 24.5 %all_to_all.25 = f32[64,1,1280]{2,1,0:T(1,128)S(1)} all-to-all(f32[64,1,1280]{2,1,0:T(1,128)S(1)} %bitcast.15), channel_id=1, replica_groups=mesh['col'=8,'row'=64] {'row'}, dimensions={0} | all-to-all | bytes 655360 | tf_op jit(solution)/shard_map/all_to_all | solution.py:306
  26.6 0.0 copy-start
  26.6 0.2 shard_map.42
  26.8 17.4 %all_to_all.26 = f32[64,8,128]{2,1,0:T(8,128)S(1)} all-to-all(f32[64,8,128]{2,1,0:T(8,128)S(1)} %bitcast.16), channel_id=1, replica_groups=mesh['col'=8,'row'=64] {'row'}, dimensions={0} | all-to-all | bytes 524288 | tf_op jit(solution)/shard_map/all_to_all | solution.py:306
  44.2 0.0 copy-done
  44.2 0.0 copy-start.1
  44.2 1.3 %shard_map.44 = f32[256,256]{1,0:T(8,128)S(1)} custom-call(f32[256,512]{1,0:T(8,128)S(1)} %copy-done, f32[512,128]{1,0:T(8,128)S(1)} %bitcast.19), custom_call_target="tpu_custom_call" | custom-call | flops 503316480 | bytes 1048576 | tf_op jit(solution)/shard_map/pallas_call | solution.py:276
  45.5 5.8 %collective-permute-start = (f32[256,256]{1,0:T(8,128)S(1)}, f32[256,256]{1,0:T(8,128)S(1)}, u32[]{:S(2)}, u32[]{:S(2)}) collective-permute-start(f32[256,256]{1,0:T(8,128)S(1)} %shard_map.44), channel_id=1, source_target_pairs={{0,384},{64,192},{128,0},{192,320},{256,128},{320,448},{384,256},{... | collective-permute-start | bytes 786440 | tf_op jit(solution)/shard_map/ppermute | solution.py:291
  51.3 0.0 copy-done.1
  51.3 2.3 %shard_map.43 = (f32[256,256]{1,0:T(8,128)S(1)}, f32[256,256]{1,0:T(8,128)S(1)}, f32[32,128]{1,0:T(8,128)S(1)}) custom-call(f32[256,512]{1,0:T(8,128)S(1)} %copy-done, f32[512,128]{1,0:T(8,128)S(1)} %bitcast.20, s32[16]{0:T(128)S(1)} %copy-done.1), custom_call_target="tpu_custom_call" | custom-call | flops 603979776 | bytes 1327168 | tf_op jit(solution)/shard_map/pallas_call | solution.py:276
  53.6 8.3 %collective-permute-done.guest = f32[256,256]{1,0:T(8,128)S(1)} collective-permute-done((f32[256,256]{1,0:T(8,128)S(1)}, f32[256,256]{1,0:T(8,128)S(1)}, u32[]{:S(2)}, u32[]{:S(2)}) %collective-permute-start) | collective-permute-done | bytes 262176 | tf_op jit(solution)/shard_map/ppermute | solution.py:291
  61.9 0.4 shard_map.45
  62.3 20.3 %all_to_all.27 = f32[64,1,2176]{2,1,0:T(1,128)S(1)} all-to-all(f32[64,1,2176]{2,1,0:T(1,128)S(1)} %bitcast.11), channel_id=1, replica_groups=mesh['col'=8,'row'=64] {'row'}, dimensions={0} | all-to-all | bytes 1114112 | tf_op jit(solution)/shard_map/all_to_all | solution.py:306
  82.6 0.1 shard_map.46
  82.7 21.3 %all_to_all.28 = f32[64,1,2176]{2,1,0:T(1,128)S(1)} all-to-all(f32[64,1,2176]{2,1,0:T(1,128)S(1)} %bitcast.13), channel_id=1, replica_groups=mesh['col'=8,'row'=64] {'row'}, dimensions={0} | all-to-all | bytes 1114112 | tf_op jit(solution)/shard_map/all_to_all | solution.py:306
  104.0 1.6 %shard_map.47 = (f32[256,256]{1,0:T(8,128)S(1)}, f32[256,256]{1,0:T(8,128)S(1)}, f32[256,256]{1,0:T(8,128)S(1)}, f32[256,256]{1,0:T(8,128)S(1)}) custom-call(f32[256,256]{1,0:T(8,128)S(1)} %get-tuple-element.14.keep, f32[256,256]{1,0:T(8,128)S(1)} %collective-permute-done.guest, f32[1088,128]{1,0:T(8,128)S(1)} %bitcast.17), custom_call_target="tpu_custom_call" | custom-call | flops 805306368 | bytes 2129920 | tf_op jit(solution)/shard_map/pallas_call | solution.py:276
  105.6 1.9 %collective-permute-start.1 = (f32[256,256]{1,0:T(8,128)S(1)}, f32[256,256]{1,0:T(8,128)S(1)}, u32[]{:S(2)}, u32[]{:S(2)}) collective-permute-start(f32[256,256]{1,0:T(8,128)S(1)} %get-tuple-element.16), channel_id=1, source_target_pairs={{0,128},{64,448},{128,256},{192,64},{256,384},{320,192},{384,0},{4... | collective-permute-start | bytes 786440 | tf_op jit(solution)/shard_map/ppermute | solution.py:297
  107.5 2.0 %shard_map.48 = (f32[32,128]{1,0:T(8,128)S(1)}, f32[256,512]{1,0:T(8,128)}) custom-call(f32[256,256]{1,0:T(8,128)S(1)} %get-tuple-element.17.x_in, f32[256,256]{1,0:T(8,128)S(1)} %get-tuple-element.18.z_keep_in, f32[256,256]{1,0:T(8,128)S(1)} %get-tuple-element.19.z_guest_in, f32[1088,128]{1,0:T(8,128)S(1)} %bitcast.18, ...), custom_call_target="tpu_custom_call" | custom-call | flops 1006632960 | bytes 2408448 | tf_op jit(solution)/shard_map/pallas_call | solution.py:276
  109.5 18.0 %all_to_all.29 = f32[8,4,128]{2,1,0:T(4,128)S(1)} all-to-all(f32[8,4,128]{2,1,0:T(4,128)S(1)} %bitcast.22), channel_id=1, replica_groups=mesh['col'=8,'row'=64] {'col'}, dimensions={0} | all-to-all | bytes 32768 | tf_op jit(solution)/shard_map/all_to_all | solution.py:306
  127.5 0.0 collective-permute-done.1.back
  127.5 0.7 shard_map.49
Async XLA Ops:
  26.6 17.6 %copy-start = (f32[256,512]{1,0:T(8,128)S(1)}, f32[256,512]{1,0:T(8,128)}, u32[]{:S(2)}) copy-start(f32[256,512]{1,0:T(8,128)} %matrix.3) | copy-start | bytes 1572868
  44.2 7.1 %copy-start.1 = (s32[16]{0:T(128)S(1)}, s32[16]{0:T(128)}, u32[]{:S(2)}) copy-start(s32[16]{0:T(128)} %seats.1) | copy-start | bytes 196
  45.5 16.4 %collective-permute-start = (f32[256,256]{1,0:T(8,128)S(1)}, f32[256,256]{1,0:T(8,128)S(1)}, u32[]{:S(2)}, u32[]{:S(2)}) collective-permute-start(f32[256,256]{1,0:T(8,128)S(1)} %shard_map.44), channel_id=1, source_target_pairs={{0,384},{64,192},{128,0},{192,320},{256,128},{320,448},{384,256},{... | collective-permute-start | bytes 786440 | tf_op jit(solution)/shard_map/ppermute | solution.py:291
  105.6 21.9 %collective-permute-start.1 = (f32[256,256]{1,0:T(8,128)S(1)}, f32[256,256]{1,0:T(8,128)S(1)}, u32[]{:S(2)}, u32[]{:S(2)}) collective-permute-start(f32[256,256]{1,0:T(8,128)S(1)} %get-tuple-element.16), channel_id=1, source_target_pairs={{0,128},{64,448},{128,256},{192,64},{256,384},{320,192},{384,0},{4... | collective-permute-start | bytes 786440 | tf_op jit(solution)/shard_map/ppermute | solution.py:297

commit v7 on v6

--- a/solution.py
+++ b/solution.py
@@ -173,52 +173,38 @@
     return jnp.concatenate([got[16:17, :], got[at : at + 1, :]], axis=1)
 
 
-def second_guest(total_rows, keep, guest, got, new_guest, x_out, z_keep_out, z_guest_out):
-    cross = from_tiles(got, 0, WIDE)
+def half_of(ref, odd):
+    return ref.at[:, pl.ds(pl.multiple_of(odd * W, W), W)]
+
+
+def second(total_rows, keep, guest, got, new_guest, sums, final, kept, done):
+    crosses = from_tiles(got, 0, WIDE)
+    grams = from_tiles(got, 8, WIDE)
     rows, cols = square_index()
-    on_diagonal = jnp.where(rows == cols, from_tiles(got, 8, WIDE), 0.0)
+    on_diagonal = jnp.where(rows == cols, grams, 0.0)
     mean_keep = jnp.sum(on_diagonal, axis=1, keepdims=True) / total_rows
     mean_guest = guest_squares(got) / total_rows
     sign = jnp.where(lax.rem(lax.axis_index("col"), 2) == 1, -0.5, 0.5) / total_rows
-    x = cross * (sign * lax.rsqrt(mean_keep + 1e-06)) * lax.rsqrt(mean_guest + 1e-06)
-    x_out[...] = x
-    flipped = split(x.T)
-    x = split(x)
-    s_guest = product(flipped, flipped, 1, 1)
-    s_keep = product(x, x, 1, 1)
-    mixed = guest[...] + product(split(keep[...]), x)
-    z_guest, z_keep = roots(s_guest, s_keep)
-    z_guest_out[...] = z_guest
-    z_keep_out[...] = z_keep
-    new_guest[...] = product(split(mixed), split(z_guest))
-
-
-def half_of(ref, odd):
-    return ref.at[:, pl.ds(pl.multiple_of(odd * W, W), W)]
-
-
-def second_sums(
-    total_rows, x_in, z_keep_in, z_guest_in, got, keep, guest, sums, final, kept, done
-):
-    x = x_in[...]
+    x = crosses * (sign * lax.rsqrt(mean_keep + 1e-06)) * lax.rsqrt(mean_guest + 1e-06)
     flipped_x = split(x.T)
     x = split(x)
-    z = z_keep_in[...]
-    zs = split(z)
-    mixed = keep[...] - product(split(guest[...]), x, 1, 1)
-    kept[...] = product(split(mixed), zs)
+    s_guest = product(flipped_x, flipped_x, 1, 1)
+    s_keep = product(x, x, 1, 1)
+    old_keep, old_guest = keep[...], guest[...]
+    mixed_keep = old_keep - product(split(old_guest), x, 1, 1)
+    mixed_guest = old_guest + product(split(old_keep), x)
+    z_guest, z = roots(s_guest, s_keep)
+    zs, zs_guest = split(z), split(z_guest)
+    kept[...] = product(split(mixed_keep), zs)
     odd = lax.rem(lax.axis_index("col"), 2)
     copy = pltpu.make_async_copy(kept, half_of(final, odd), done)
     copy.start()
-    cross = split(from_tiles(got, 0, WIDE))
-    grams = from_tiles(got, 8, WIDE)
+    new_guest[...] = product(split(mixed_guest), zs_guest)
+    cross = split(crosses)
     flipped = grams.T
-    rows, cols = square_index()
     of_keep = split(jnp.where(rows <= cols, grams, flipped))
     of_guest = jnp.where(rows > cols, grams, flipped)
     of_guest = split(jnp.where(rows == cols, guest_squares(got), of_guest))
-    z_guest = z_guest_in[...]
-    zs_guest = split(z_guest)
     v = product(flipped_x, zs)
     w = product(x, zs_guest)
     vs, ws = split(v), split(w)
@@ -327,18 +313,16 @@
     sent = local(pack_second, 2 * one, (WIDE * N_ROW, 128))(keep, guest, gram)
     folded = local(fold_wide, 1, (WIDE * N_ROW, 128))(exchange(sent, "row"))
     got = exchange(folded, "row")
-    new_guest, x, z_keep, z_guest = local(
-        functools.partial(second_guest, total_rows), 8 * one, (W, W), (W, W), (W, W), (W, W)
+    new_guest, means, begun = local(
+        functools.partial(second, total_rows),
+        18 * one,
+        (W, W),
+        (4 * N_COL, 128),
+        (W, 2 * W),
+        outs=[VMEM, VMEM, HBM],
+        scratch=[pltpu.VMEM((W, W), jnp.float32), pltpu.SemaphoreType.DMA],
     )(keep, guest, got)
     back = swapped_back(new_guest)
-    means, begun = local(
-        functools.partial(second_sums, total_rows),
-        10 * one,
-        (4 * N_COL, 128),
-        (W, 2 * W),
-        outs=[VMEM, HBM],
-        scratch=[pltpu.VMEM((W, W), jnp.float32), pltpu.SemaphoreType.DMA],
-    )(x, z_keep, z_guest, got, keep, guest)
     table = exchange(means, "col")
     final, picked = local(
         finish,

time: 129 us -> 128 us (level)
    pallas_call x9 -> x8, Pallas kernels: 10 us -> 9.13 us  [call(): pl.pallas_call(body, out_shape=out[0] if one else out, in_specs=ins or [V...]
  transfers between devices with their start and end apart: 2 -> 2, of which waited for: 1 -> 1; matrix products, arithmetic and copies ran while one was open for 0% -> 0% of each run, Pallas kernels for 3% -> 2%
where the time goes in v7:
time: 128 us; the launch traced here: 127 us
  blocking collectives  101 us (79%)
  Pallas kernels  9.13 us (7%)
  waiting for transfers between devices  8.27 us (6%)
  starting transfers between devices  7.73 us (6%)
    all_to_all x5, blocking collectives, exchange(): lax.all_to_all(pieces.reshape(shape), axis, 0, 0, tiled=True)  101 us
    pallas_call x8, Pallas kernels, call(): pl.pallas_call(body, out_shape=out[0] if one else out, in_specs=ins or [V...  9.13 us
    ppermute x1, waiting for transfers between devices, swapped(): lax.ppermute(block, 'col', [(c, (c + (2 if c % 2 else -2)) % N_COL) for c...  8.27 us
    ppermute x1, starting transfers between devices, swapped(): lax.ppermute(block, 'col', [(c, (c + (2 if c % 2 else -2)) % N_COL) for c...  5.81 us
  transfers between devices with their start and end apart: 2, of which 1 were waited for; matrix products, arithmetic and copies ran while one was open for 0% of the time, Pallas kernels for 2%

profile of v7, /device:TPU:1, one launch (start us, length us, event | category | flops | bytes accessed | tf_op | source)
XLA Modules:
  0.0 127.3 jit_solution(2558022263153065010)
XLA Ops:
  0.6 1.5 %shard_map.41 = f32[640,128]{1,0:T(8,128)S(1)} custom-call(f32[256,512]{1,0:T(8,128)} %matrix.3), custom_call_target="tpu_custom_call" | custom-call | flops 100663296 | bytes 851968 | tf_op jit(solution)/shard_map/pallas_call | solution.py:262
  2.1 24.5 %all_to_all.25 = f32[64,1,1280]{2,1,0:T(1,128)S(1)} all-to-all(f32[64,1,1280]{2,1,0:T(1,128)S(1)} %bitcast.15), channel_id=1, replica_groups=mesh['col'=8,'row'=64] {'row'}, dimensions={0} | all-to-all | bytes 655360 | tf_op jit(solution)/shard_map/all_to_all | solution.py:292
  26.6 0.0 copy-start
  26.6 0.2 shard_map.42
  26.8 17.4 %all_to_all.26 = f32[64,8,128]{2,1,0:T(8,128)S(1)} all-to-all(f32[64,8,128]{2,1,0:T(8,128)S(1)} %bitcast.16), channel_id=1, replica_groups=mesh['col'=8,'row'=64] {'row'}, dimensions={0} | all-to-all | bytes 524288 | tf_op jit(solution)/shard_map/all_to_all | solution.py:292
  44.2 0.0 copy-done
  44.2 0.0 copy-start.1
  44.2 1.3 %shard_map.44 = f32[256,256]{1,0:T(8,128)S(1)} custom-call(f32[256,512]{1,0:T(8,128)S(1)} %copy-done, f32[512,128]{1,0:T(8,128)S(1)} %bitcast.18), custom_call_target="tpu_custom_call" | custom-call | flops 503316480 | bytes 1048576 | tf_op jit(solution)/shard_map/pallas_call | solution.py:262
  45.5 5.8 %collective-permute-start = (f32[256,256]{1,0:T(8,128)S(1)}, f32[256,256]{1,0:T(8,128)S(1)}, u32[]{:S(2)}, u32[]{:S(2)}) collective-permute-start(f32[256,256]{1,0:T(8,128)S(1)} %shard_map.44), channel_id=1, source_target_pairs={{0,384},{64,192},{128,0},{192,320},{256,128},{320,448},{384,256},{... | collective-permute-start | bytes 786440 | tf_op jit(solution)/shard_map/ppermute | solution.py:277
  51.3 0.0 copy-done.1
  51.3 2.3 %shard_map.43 = (f32[256,256]{1,0:T(8,128)S(1)}, f32[256,256]{1,0:T(8,128)S(1)}, f32[32,128]{1,0:T(8,128)S(1)}) custom-call(f32[256,512]{1,0:T(8,128)S(1)} %copy-done, f32[512,128]{1,0:T(8,128)S(1)} %bitcast.19, s32[16]{0:T(128)S(1)} %copy-done.1), custom_call_target="tpu_custom_call" | custom-call | flops 603979776 | bytes 1327168 | tf_op jit(solution)/shard_map/pallas_call | solution.py:262
  53.6 8.3 %collective-permute-done.guest = f32[256,256]{1,0:T(8,128)S(1)} collective-permute-done((f32[256,256]{1,0:T(8,128)S(1)}, f32[256,256]{1,0:T(8,128)S(1)}, u32[]{:S(2)}, u32[]{:S(2)}) %collective-permute-start) | collective-permute-done | bytes 262176 | tf_op jit(solution)/shard_map/ppermute | solution.py:277
  61.9 0.4 shard_map.45
  62.3 20.3 %all_to_all.27 = f32[64,1,2176]{2,1,0:T(1,128)S(1)} all-to-all(f32[64,1,2176]{2,1,0:T(1,128)S(1)} %bitcast.11), channel_id=1, replica_groups=mesh['col'=8,'row'=64] {'row'}, dimensions={0} | all-to-all | bytes 1114112 | tf_op jit(solution)/shard_map/all_to_all | solution.py:292
  82.6 0.1 shard_map.46
  82.7 21.3 %all_to_all.28 = f32[64,1,2176]{2,1,0:T(1,128)S(1)} all-to-all(f32[64,1,2176]{2,1,0:T(1,128)S(1)} %bitcast.13), channel_id=1, replica_groups=mesh['col'=8,'row'=64] {'row'}, dimensions={0} | all-to-all | bytes 1114112 | tf_op jit(solution)/shard_map/all_to_all | solution.py:292
  104.0 2.6 %shard_map.47 = (f32[256,256]{1,0:T(8,128)S(1)}, f32[32,128]{1,0:T(8,128)S(1)}, f32[256,512]{1,0:T(8,128)}) custom-call(f32[256,256]{1,0:T(8,128)S(1)} %get-tuple-element.11.keep, f32[256,256]{1,0:T(8,128)S(1)} %collective-permute-done.guest, f32[1088,128]{1,0:T(8,128)S(1)} %bitcast.17), custom_call_target="tpu_custom_call" | custom-call | flops 1811939328 | bytes 1884160 | tf_op jit(solution)/shard_map/pallas_call | solution.py:262
  106.7 1.9 %collective-permute-start.1 = (f32[256,256]{1,0:T(8,128)S(1)}, f32[256,256]{1,0:T(8,128)S(1)}, u32[]{:S(2)}, u32[]{:S(2)}) collective-permute-start(f32[256,256]{1,0:T(8,128)S(1)} %get-tuple-element.13), channel_id=1, source_target_pairs={{0,128},{64,448},{128,256},{192,64},{256,384},{320,192},{384,0},{4... | collective-permute-start | bytes 786440 | tf_op jit(solution)/shard_map/ppermute | solution.py:283
  108.6 18.0 %all_to_all.29 = f32[8,4,128]{2,1,0:T(4,128)S(1)} all-to-all(f32[8,4,128]{2,1,0:T(4,128)S(1)} %bitcast.21), channel_id=1, replica_groups=mesh['col'=8,'row'=64] {'col'}, dimensions={0} | all-to-all | bytes 32768 | tf_op jit(solution)/shard_map/all_to_all | solution.py:292
  126.6 0.0 collective-permute-done.1.back
  126.6 0.7 shard_map.48
Async XLA Ops:
  26.6 17.6 %copy-start = (f32[256,512]{1,0:T(8,128)S(1)}, f32[256,512]{1,0:T(8,128)}, u32[]{:S(2)}) copy-start(f32[256,512]{1,0:T(8,128)} %matrix.3) | copy-start | bytes 1572868
  44.2 7.1 %copy-start.1 = (s32[16]{0:T(128)S(1)}, s32[16]{0:T(128)}, u32[]{:S(2)}) copy-start(s32[16]{0:T(128)} %seats.1) | copy-start | bytes 196
  45.5 16.4 %collective-permute-start = (f32[256,256]{1,0:T(8,128)S(1)}, f32[256,256]{1,0:T(8,128)S(1)}, u32[]{:S(2)}, u32[]{:S(2)}) collective-permute-start(f32[256,256]{1,0:T(8,128)S(1)} %shard_map.44), channel_id=1, source_target_pairs={{0,384},{64,192},{128,0},{192,320},{256,128},{320,448},{384,256},{... | collective-permute-start | bytes 786440 | tf_op jit(solution)/shard_map/ppermute | solution.py:277
  106.7 19.9 %collective-permute-start.1 = (f32[256,256]{1,0:T(8,128)S(1)}, f32[256,256]{1,0:T(8,128)S(1)}, u32[]{:S(2)}, u32[]{:S(2)}) collective-permute-start(f32[256,256]{1,0:T(8,128)S(1)} %get-tuple-element.13), channel_id=1, source_target_pairs={{0,128},{64,448},{128,256},{192,64},{256,384},{320,192},{384,0},{4... | collective-permute-start | bytes 786440 | tf_op jit(solution)/shard_map/ppermute | solution.py:283

commit v8 on v7

--- a/solution.py
+++ b/solution.py
@@ -5,13 +5,16 @@
 from jax import lax
 from jax.experimental import pallas as pl
 from jax.experimental.pallas import tpu as pltpu
+from jax.sharding import Mesh
 from jax.sharding import PartitionSpec as P
 
 W = 256
 N_ROW = 64
 N_COL = 8
+ZL, Y, X = 2, 8, 4
 PIECE = 10
-WIDE = 17
+WIDE_N = 8
+WIDE = 136
 LOADS = 8
 LIMIT = 32 * 1024 * 1024
 LOAD_LIMIT = 56000000
@@ -105,17 +108,22 @@
     return rows, lax.broadcasted_iota(jnp.int32, (W, W), 1)
 
 
+def stacked(block):
+    return jnp.concatenate([block[:, :128], block[:, 128:]], axis=0)
+
+
 def pack_second(keep, guest, gram_keep, out):
     parts = split(guest[...])
-    cross = product(split(keep[...]), parts, 0, 0)
+    cross = stacked(product(split(keep[...]), parts, 0, 0))
     rows, cols = square_index()
-    grams = jnp.where(rows <= cols, gram_keep[...], product(parts, parts, 0, 0))
-    norm_guest = column_squares(guest[...])
-    for r in range(N_ROW):
-        half, at = r // 32, WIDE * r
-        out[at : at + 8, :] = tile_at(cross, r)
-        out[at + 8 : at + 16, :] = tile_at(grams, r)
-        out[at + 16 : at + 17, :] = norm_guest[:, 128 * half : 128 * half + 128]
+    grams = stacked(jnp.where(rows <= cols, gram_keep[...], product(parts, parts, 0, 0)))
+    norms = column_squares(guest[...])
+    norms = jnp.concatenate([norms[:, :128], norms[:, 128:]] * 4, axis=0)
+    for r in range(WIDE_N):
+        at = WIDE * r
+        out[at : at + 64, :] = cross[64 * r : 64 * r + 64]
+        out[at + 64 : at + 128, :] = grams[64 * r : 64 * r + 64]
+        out[at + 128 : at + 136, :] = norms
 
 
 def fold(total_rows, got, out):
@@ -125,7 +133,7 @@
         tile += got[PIECE * r : PIECE * r + 8, :]
         norms += got[PIECE * r + 8 : PIECE * r + 10, :]
     sign = jnp.where(lax.rem(lax.axis_index("col"), 2) == 1, -0.5, 0.5)
-    first = 8 * lax.rem(lax.axis_index("row"), 16)
+    first = 8 * lax.rem(lax.axis_index("y") * X + lax.axis_index("x"), 16)
     lanes = lax.broadcasted_iota(jnp.int32, (8, 128), 1)
     rows = lax.broadcasted_iota(jnp.int32, (8, 128), 0)
     means = norms / total_rows
@@ -139,10 +147,19 @@
 
 def fold_wide(got, out):
     piece = got[0:WIDE, :]
-    for r in range(1, N_ROW):
+    for r in range(1, WIDE_N):
         piece += got[WIDE * r : WIDE * r + WIDE, :]
-    for r in range(N_ROW):
+    for r in range(WIDE_N):
         out[WIDE * r : WIDE * r + WIDE, :] = piece
+
+
+def from_wide(ref, first):
+    at = [WIDE * r + first for r in range(WIDE_N)]
+    left = [ref[k : k + 64, :] for k in at[:4]]
+    right = [ref[k : k + 64, :] for k in at[4:]]
+    return jnp.concatenate(
+        [jnp.concatenate(left, axis=0), jnp.concatenate(right, axis=0)], axis=1
+    )
 
 
 def first_move(matrix, tiles, out):
@@ -169,8 +186,7 @@
 
 
 def guest_squares(got):
-    at = 32 * WIDE + 16
-    return jnp.concatenate([got[16:17, :], got[at : at + 1, :]], axis=1)
+    return jnp.concatenate([got[128:129, :], got[129:130, :]], axis=1)
 
 
 def half_of(ref, odd):
@@ -178,8 +194,8 @@
 
 
 def second(total_rows, keep, guest, got, new_guest, sums, final, kept, done):
-    crosses = from_tiles(got, 0, WIDE)
-    grams = from_tiles(got, 8, WIDE)
+    crosses = from_wide(got, 0)
+    grams = from_wide(got, 64)
     rows, cols = square_index()
     on_diagonal = jnp.where(rows == cols, grams, 0.0)
     mean_keep = jnp.sum(on_diagonal, axis=1, keepdims=True) / total_rows
@@ -285,10 +301,13 @@
     )
 
 
+ROW = ("zl", "y", "x")
+
+
 def exchange(pieces, axis):
     n = lax.axis_size(axis)
     rows = pieces.shape[0] // n
-    shape = (n, rows, 128) if rows in (4, 8) else (n, 1, rows * 128)
+    shape = (n, rows, 128) if rows in (4, 8, WIDE) else (n, 1, rows * 128)
     return lax.all_to_all(pieces.reshape(shape), axis, 0, 0, tiled=True).reshape(pieces.shape)
 
 
@@ -304,15 +323,17 @@
         limit=LOAD_LIMIT,
         scratch=[pltpu.VMEM((W, 2 * W), jnp.float32), pltpu.SemaphoreType.DMA((LOADS,))],
     )(matrix)
-    tiles = exchange(fold_all(exchange(sent, "row")), "row")
+    tiles = exchange(fold_all(exchange(sent, ROW)), ROW)
     move = local(first_move, 5 * one, (W, W))(matrix, tiles)
     guest = swapped(move)
     keep, gram, hits = local(
         first_keep, 6 * one, (W, W), (W, W), (4 * N_COL, 128), ins=[VMEM, VMEM, SMEM]
     )(matrix, tiles, seats)
-    sent = local(pack_second, 2 * one, (WIDE * N_ROW, 128))(keep, guest, gram)
-    folded = local(fold_wide, 1, (WIDE * N_ROW, 128))(exchange(sent, "row"))
-    got = exchange(folded, "row")
+    sent = local(pack_second, 2 * one, (WIDE * WIDE_N, 128))(keep, guest, gram)
+    fold_eight = local(fold_wide, 1, (WIDE * WIDE_N, 128))
+    folded = fold_eight(exchange(sent, ("zl", "x")))
+    folded = fold_eight(exchange(folded, "y"))
+    got = exchange(folded, ("zl", "x"))
     new_guest, means, begun = local(
         functools.partial(second, total_rows),
         18 * one,
@@ -338,11 +359,12 @@
 
 
 def solution(mesh):
-    placed = (P("row", "col"), P())
+    parts = Mesh(mesh.devices.reshape(N_COL, ZL, Y, X), ("col",) + ROW)
+    placed = (P(ROW, "col"), P())
     return jax.shard_map(
         on_device,
-        mesh=mesh,
+        mesh=parts,
         in_specs=placed,
-        out_specs=(P("row", "col"), P("col")),
+        out_specs=(P(ROW, "col"), P("col")),
         check_vma=False,
     )

time: 128 us -> 127 us (level)
  blocking collectives: 101 us -> 98.8 us
  starting transfers between devices: 7.73 us -> 9.5 us
    all_to_all x5 -> x6, blocking collectives: 101 us -> 98.8 us  [exchange(): lax.all_to_all(pieces.reshape(shape), axis, 0, 0, tiled=True)]
    ppermute x1, starting transfers between devices: 1.92 us -> 3.69 us  [swapped_back(): lax.ppermute(block, 'col', [(c, (c + (-2 if c % 2 else 2)) % N_COL) for c...]
    pallas_call x8 -> x9, Pallas kernels: 9.13 us -> 9.09 us  [call(): pl.pallas_call(body, out_shape=out[0] if one else out, in_specs=ins or [V...]
where the time goes in v8:
time: 127 us; the launch traced here: 126 us
  blocking collectives  98.8 us (78%)
  starting transfers between devices  9.5 us (7%)
  Pallas kernels  9.09 us (7%)
  waiting for transfers between devices  8.27 us (7%)
    all_to_all x6, blocking collectives, exchange(): lax.all_to_all(pieces.reshape(shape), axis, 0, 0, tiled=True)  98.8 us
    pallas_call x9, Pallas kernels, call(): pl.pallas_call(body, out_shape=out[0] if one else out, in_specs=ins or [V...  9.09 us
    ppermute x1, waiting for transfers between devices, swapped(): lax.ppermute(block, 'col', [(c, (c + (2 if c % 2 else -2)) % N_COL) for c...  8.27 us
    ppermute x1, starting transfers between devices, swapped(): lax.ppermute(block, 'col', [(c, (c + (2 if c % 2 else -2)) % N_COL) for c...  5.81 us
    ppermute x1, starting transfers between devices, swapped_back(): lax.ppermute(block, 'col', [(c, (c + (-2 if c % 2 else 2)) % N_COL) for c...  3.69 us
  transfers between devices with their start and end apart: 2, of which 1 were waited for; matrix products, arithmetic and copies ran while one was open for 0% of the time, Pallas kernels for 2%

profile of v8, /device:TPU:1, one launch (start us, length us, event | category | flops | bytes accessed | tf_op | source)
XLA Modules:
  0.0 126.4 jit_solution(6964452552581127574)
XLA Ops:
  0.6 1.5 %shard_map.41 = f32[640,128]{1,0:T(8,128)S(1)} custom-call(f32[256,512]{1,0:T(8,128)} %matrix.3), custom_call_target="tpu_custom_call" | custom-call | flops 100663296 | bytes 851968 | tf_op jit(solution)/shard_map/pallas_call | solution.py:278
  2.1 24.5 %all_to_all.30 = f32[64,1,1280]{2,1,0:T(1,128)S(1)} all-to-all(f32[64,1,1280]{2,1,0:T(1,128)S(1)} %bitcast.19), channel_id=1, replica_groups=mesh['col'=8,'zl'=2,'y'=8,'x'=4] {'zl','y','x'}, dimensions={0} | all-to-all | bytes 655360 | tf_op jit(solution)/shard_map/all_to_all | solution.py:311
  26.6 0.0 copy-start
  26.6 0.2 shard_map.42
  26.8 17.4 %all_to_all.31 = f32[64,8,128]{2,1,0:T(8,128)S(1)} all-to-all(f32[64,8,128]{2,1,0:T(8,128)S(1)} %bitcast.20), channel_id=1, replica_groups=mesh['col'=8,'zl'=2,'y'=8,'x'=4] {'zl','y','x'}, dimensions={0} | all-to-all | bytes 524288 | tf_op jit(solution)/shard_map/all_to_all | solution.py:311
  44.2 0.0 copy-done
  44.2 0.0 copy-start.1
  44.2 1.3 %shard_map.44 = f32[256,256]{1,0:T(8,128)S(1)} custom-call(f32[256,512]{1,0:T(8,128)S(1)} %copy-done, f32[512,128]{1,0:T(8,128)S(1)} %bitcast.22), custom_call_target="tpu_custom_call" | custom-call | flops 503316480 | bytes 1048576 | tf_op jit(solution)/shard_map/pallas_call | solution.py:278
  45.5 5.8 %collective-permute-start = (f32[256,256]{1,0:T(8,128)S(1)}, f32[256,256]{1,0:T(8,128)S(1)}, u32[]{:S(2)}, u32[]{:S(2)}) collective-permute-start(f32[256,256]{1,0:T(8,128)S(1)} %shard_map.44), channel_id=1, source_target_pairs={{0,384},{64,192},{128,0},{192,320},{256,128},{320,448},{384,256},{... | collective-permute-start | bytes 786440 | tf_op jit(solution)/shard_map/ppermute | solution.py:293
  51.3 0.0 copy-done.1
  51.3 2.3 %shard_map.43 = (f32[256,256]{1,0:T(8,128)S(1)}, f32[256,256]{1,0:T(8,128)S(1)}, f32[32,128]{1,0:T(8,128)S(1)}) custom-call(f32[256,512]{1,0:T(8,128)S(1)} %copy-done, f32[512,128]{1,0:T(8,128)S(1)} %bitcast.23, s32[16]{0:T(128)S(1)} %copy-done.1), custom_call_target="tpu_custom_call" | custom-call | flops 603979776 | bytes 1327168 | tf_op jit(solution)/shard_map/pallas_call | solution.py:278
  53.6 8.3 %collective-permute-done.guest = f32[256,256]{1,0:T(8,128)S(1)} collective-permute-done((f32[256,256]{1,0:T(8,128)S(1)}, f32[256,256]{1,0:T(8,128)S(1)}, u32[]{:S(2)}, u32[]{:S(2)}) %collective-permute-start) | collective-permute-done | bytes 262176 | tf_op jit(solution)/shard_map/ppermute | solution.py:293
  61.9 0.4 shard_map.45
  62.3 10.9 %all_to_all.32 = f32[8,136,128]{2,1,0:T(8,128)S(1)} all-to-all(f32[8,136,128]{2,1,0:T(8,128)S(1)} %bitcast.13), channel_id=1, replica_groups=mesh['col'=8,'zl'=2,'y'=8,'x'=4] {'zl','x'}, dimensions={0} | all-to-all | bytes 1114112 | tf_op jit(solution)/shard_map/all_to_all | solution.py:311
  73.2 16.1 %all_to_all.33 = f32[8,136,128]{2,1,0:T(8,128)S(1)} all-to-all(f32[8,136,128]{2,1,0:T(8,128)S(1)} %bitcast.15), channel_id=1, replica_groups=mesh['col'=8,'zl'=2,'y'=8,'x'=4] {'y'}, dimensions={0} | all-to-all | bytes 1114112 | tf_op jit(solution)/shard_map/all_to_all | solution.py:311
  89.4 10.5 %all_to_all.34 = f32[8,136,128]{2,1,0:T(8,128)S(1)} all-to-all(f32[8,136,128]{2,1,0:T(8,128)S(1)} %bitcast.17), channel_id=1, replica_groups=mesh['col'=8,'zl'=2,'y'=8,'x'=4] {'zl','x'}, dimensions={0} | all-to-all | bytes 1114112 | tf_op jit(solution)/shard_map/all_to_all | solution.py:311
  99.9 2.6 %shard_map.48 = (f32[256,256]{1,0:T(8,128)S(1)}, f32[32,128]{1,0:T(8,128)S(1)}, f32[256,512]{1,0:T(8,128)}) custom-call(f32[256,256]{1,0:T(8,128)S(1)} %get-tuple-element.11.keep, f32[256,256]{1,0:T(8,128)S(1)} %collective-permute-done.guest, f32[1088,128]{1,0:T(8,128)S(1)} %bitcast.21), custom_call_target="tpu_custom_call" | custom-call | flops 1811939328 | bytes 1884160 | tf_op jit(solution)/shard_map/pallas_call | solution.py:278
  102.5 3.7 %collective-permute-start.1 = (f32[256,256]{1,0:T(8,128)S(1)}, f32[256,256]{1,0:T(8,128)S(1)}, u32[]{:S(2)}, u32[]{:S(2)}) collective-permute-start(f32[256,256]{1,0:T(8,128)S(1)} %get-tuple-element.13), channel_id=1, source_target_pairs={{0,128},{64,448},{128,256},{192,64},{256,384},{320,192},{384,0},{4... | collective-permute-start | bytes 786440 | tf_op jit(solution)/shard_map/ppermute | solution.py:299
  106.2 19.4 %all_to_all.35 = f32[8,4,128]{2,1,0:T(4,128)S(1)} all-to-all(f32[8,4,128]{2,1,0:T(4,128)S(1)} %bitcast.25), channel_id=1, replica_groups=mesh['col'=8,'zl'=2,'y'=8,'x'=4] {'col'}, dimensions={0} | all-to-all | bytes 32768 | tf_op jit(solution)/shard_map/all_to_all | solution.py:311
  125.6 0.0 collective-permute-done.1.back
  125.7 0.7 shard_map.49
  (2 shorter events, 0.1 us)
Async XLA Ops:
  26.6 17.6 %copy-start = (f32[256,512]{1,0:T(8,128)S(1)}, f32[256,512]{1,0:T(8,128)}, u32[]{:S(2)}) copy-start(f32[256,512]{1,0:T(8,128)} %matrix.3) | copy-start | bytes 1572868
  44.2 7.1 %copy-start.1 = (s32[16]{0:T(128)S(1)}, s32[16]{0:T(128)}, u32[]{:S(2)}) copy-start(s32[16]{0:T(128)} %seats.1) | copy-start | bytes 196
  45.5 16.4 %collective-permute-start = (f32[256,256]{1,0:T(8,128)S(1)}, f32[256,256]{1,0:T(8,128)S(1)}, u32[]{:S(2)}, u32[]{:S(2)}) collective-permute-start(f32[256,256]{1,0:T(8,128)S(1)} %shard_map.44), channel_id=1, source_target_pairs={{0,384},{64,192},{128,0},{192,320},{256,128},{320,448},{384,256},{... | collective-permute-start | bytes 786440 | tf_op jit(solution)/shard_map/ppermute | solution.py:293
  102.5 23.1 %collective-permute-start.1 = (f32[256,256]{1,0:T(8,128)S(1)}, f32[256,256]{1,0:T(8,128)S(1)}, u32[]{:S(2)}, u32[]{:S(2)}) collective-permute-start(f32[256,256]{1,0:T(8,128)S(1)} %get-tuple-element.13), channel_id=1, source_target_pairs={{0,128},{64,448},{128,256},{192,64},{256,384},{320,192},{384,0},{4... | collective-permute-start | bytes 786440 | tf_op jit(solution)/shard_map/ppermute | solution.py:299

commit v9 on v8

--- a/solution.py
+++ b/solution.py
@@ -12,8 +12,8 @@
 N_ROW = 64
 N_COL = 8
 ZL, Y, X = 2, 8, 4
-PIECE = 10
-WIDE_N = 8
+EIGHT = 8
+NARROW = 72
 WIDE = 136
 LOADS = 8
 LIMIT = 32 * 1024 * 1024
@@ -45,17 +45,8 @@
     return base + product(split(s2), split(0.0625 * s2 - 0.3125 * s)), other
 
 
-def tile_at(block, r):
-    i, half = r % 32, r // 32
-    return block[8 * i : 8 * i + 8, 128 * half : 128 * half + 128]
-
-
-def from_tiles(ref, first, step):
-    left = [ref[step * r + first : step * r + first + 8, :] for r in range(32)]
-    right = [ref[step * r + first : step * r + first + 8, :] for r in range(32, 64)]
-    return jnp.concatenate(
-        [jnp.concatenate(left, axis=0), jnp.concatenate(right, axis=0)], axis=1
-    )
+def unstacked(ref):
+    return jnp.concatenate([ref[:W, :], ref[W:, :]], axis=1)
 
 
 def roots(*squares):
@@ -93,14 +84,15 @@
     for copy in copies:
         copy.wait()
     keep, move = halves(matrix)
-    cross = product(split(keep), split(move), 0, 0)
+    cross = stacked(product(split(keep), split(move), 0, 0))
     norm_keep, norm_move = column_squares(keep), column_squares(move)
-    for r in range(N_ROW):
-        i, half = r % 32, r // 32
-        at = PIECE * r
-        out[at : at + 8, :] = tile_at(cross, r)
-        out[at + 8 : at + 9, :] = norm_keep[:, 128 * (i // 16) : 128 * (i // 16) + 128]
-        out[at + 9 : at + 10, :] = norm_move[:, 128 * half : 128 * half + 128]
+    for r in range(EIGHT):
+        at = NARROW * r
+        out[at : at + 64, :] = cross[64 * r : 64 * r + 64]
+        half = (r % 4) // 2
+        pair = [norm_keep[:, 128 * half : 128 * half + 128]]
+        pair.append(norm_move[:, 128 * (r // 4) : 128 * (r // 4) + 128])
+        out[at + 64 : at + 72, :] = jnp.concatenate(pair * 4, axis=0)
 
 
 def square_index():
@@ -119,42 +111,42 @@
     grams = stacked(jnp.where(rows <= cols, gram_keep[...], product(parts, parts, 0, 0)))
     norms = column_squares(guest[...])
     norms = jnp.concatenate([norms[:, :128], norms[:, 128:]] * 4, axis=0)
-    for r in range(WIDE_N):
+    for r in range(EIGHT):
         at = WIDE * r
         out[at : at + 64, :] = cross[64 * r : 64 * r + 64]
         out[at + 64 : at + 128, :] = grams[64 * r : 64 * r + 64]
         out[at + 128 : at + 136, :] = norms
 
 
-def fold(total_rows, got, out):
-    tile = got[0:8, :]
-    norms = got[8:10, :]
-    for r in range(1, N_ROW):
-        tile += got[PIECE * r : PIECE * r + 8, :]
-        norms += got[PIECE * r + 8 : PIECE * r + 10, :]
+def added(got, size):
+    piece = got[0:size, :]
+    for r in range(1, EIGHT):
+        piece += got[size * r : size * r + size, :]
+    return piece
+
+
+def fold(size, got, out):
+    piece = added(got, size)
+    for r in range(EIGHT):
+        out[size * r : size * r + size, :] = piece
+
+
+def fold_first(total_rows, got, out):
+    piece = added(got, NARROW) / total_rows
     sign = jnp.where(lax.rem(lax.axis_index("col"), 2) == 1, -0.5, 0.5)
-    first = 8 * lax.rem(lax.axis_index("y") * X + lax.axis_index("x"), 16)
-    lanes = lax.broadcasted_iota(jnp.int32, (8, 128), 1)
-    rows = lax.broadcasted_iota(jnp.int32, (8, 128), 0)
-    means = norms / total_rows
+    first = 64 * lax.rem(lax.axis_index("x"), 2)
+    lanes = lax.broadcasted_iota(jnp.int32, (64, 128), 1)
+    rows = lax.broadcasted_iota(jnp.int32, (64, 128), 0)
     mean_keep = jnp.sum(
-        jnp.where(lanes == first + rows, means[0:1], 0.0), axis=1, keepdims=True
-    )
-    x = sign * (tile / total_rows) / jnp.sqrt((mean_keep + 1e-06) * (means[1:2] + 1e-06))
-    for r in range(N_ROW):
-        out[8 * r : 8 * r + 8, :] = x
-
-
-def fold_wide(got, out):
-    piece = got[0:WIDE, :]
-    for r in range(1, WIDE_N):
-        piece += got[WIDE * r : WIDE * r + WIDE, :]
-    for r in range(WIDE_N):
-        out[WIDE * r : WIDE * r + WIDE, :] = piece
+        jnp.where(lanes == first + rows, piece[64:65], 0.0), axis=1, keepdims=True
+    )
+    x = sign * piece[:64] / jnp.sqrt((mean_keep + 1e-06) * (piece[65:66] + 1e-06))
+    for r in range(EIGHT):
+        out[64 * r : 64 * r + 64, :] = x
 
 
 def from_wide(ref, first):
-    at = [WIDE * r + first for r in range(WIDE_N)]
+    at = [WIDE * r + first for r in range(EIGHT)]
     left = [ref[k : k + 64, :] for k in at[:4]]
     right = [ref[k : k + 64, :] for k in at[4:]]
     return jnp.concatenate(
@@ -164,7 +156,7 @@
 
 def first_move(matrix, tiles, out):
     keep, move = halves(matrix)
-    x = split(from_tiles(tiles, 0, 8))
+    x = split(unstacked(tiles))
     z, mixed = root(product(x, x, 0, 0), lambda: move + product(split(keep), x))
     out[...] = product(split(mixed), split(z))
 
@@ -177,7 +169,7 @@
             hit = jnp.where(seats[seat] == first + k, 1.0, 0.0).astype(jnp.float32)
             hits[at : at + 1, :] = jnp.full((1, 128), hit)
     keep, move = halves(matrix)
-    x = split(from_tiles(tiles, 0, 8))
+    x = split(unstacked(tiles))
     z, mixed = root(product(x, x, 1, 1), lambda: keep - product(split(move), x, 1, 1))
     kept = product(split(mixed), split(z))
     out[...] = kept
@@ -305,32 +297,35 @@
 
 
 def exchange(pieces, axis):
-    n = lax.axis_size(axis)
-    rows = pieces.shape[0] // n
-    shape = (n, rows, 128) if rows in (4, 8, WIDE) else (n, 1, rows * 128)
-    return lax.all_to_all(pieces.reshape(shape), axis, 0, 0, tiled=True).reshape(pieces.shape)
+    split_up = pieces.reshape(lax.axis_size(axis), -1, 128)
+    return lax.all_to_all(split_up, axis, 0, 0, tiled=True).reshape(pieces.shape)
 
 
 def on_device(matrix, seats):
     total_rows = matrix.shape[0] * N_ROW
     one = 6 * W**3
-    fold_all = local(functools.partial(fold, total_rows), 1, (8 * N_ROW, 128))
     sent = local(
         pack_first,
         one,
-        (PIECE * N_ROW, 128),
+        (NARROW * EIGHT, 128),
         ins=[HBM],
         limit=LOAD_LIMIT,
         scratch=[pltpu.VMEM((W, 2 * W), jnp.float32), pltpu.SemaphoreType.DMA((LOADS,))],
     )(matrix)
-    tiles = exchange(fold_all(exchange(sent, ROW)), ROW)
+    folded = local(functools.partial(fold, NARROW), 1, (NARROW * EIGHT, 128))(
+        exchange(sent, ("zl", "x"))
+    )
+    tiles = local(functools.partial(fold_first, total_rows), 1, (64 * EIGHT, 128))(
+        exchange(folded, "y")
+    )
+    tiles = exchange(tiles, ("zl", "x"))
     move = local(first_move, 5 * one, (W, W))(matrix, tiles)
     guest = swapped(move)
     keep, gram, hits = local(
         first_keep, 6 * one, (W, W), (W, W), (4 * N_COL, 128), ins=[VMEM, VMEM, SMEM]
     )(matrix, tiles, seats)
-    sent = local(pack_second, 2 * one, (WIDE * WIDE_N, 128))(keep, guest, gram)
-    fold_eight = local(fold_wide, 1, (WIDE * WIDE_N, 128))
+    sent = local(pack_second, 2 * one, (WIDE * EIGHT, 128))(keep, guest, gram)
+    fold_eight = local(functools.partial(fold, WIDE), 1, (WIDE * EIGHT, 128))
     folded = fold_eight(exchange(sent, ("zl", "x")))
     folded = fold_eight(exchange(folded, "y"))
     got = exchange(folded, ("zl", "x"))

time: 127 us -> 126 us (level)
  blocking collectives: 98.8 us -> 97 us
    all_to_all x6 -> x7, blocking collectives: 98.8 us -> 97 us  [exchange(): lax.all_to_all(split_up, axis, 0, 0, tiled=True).reshape(pieces.shape)]
    pallas_call x9 -> x10, Pallas kernels: 9.09 us -> 9.05 us  [call(): pl.pallas_call(body, out_shape=out[0] if one else out, in_specs=ins or [V...]
where the time goes in v9:
time: 126 us; the launch traced here: 125 us
  blocking collectives  97 us (77%)
  starting transfers between devices  10.3 us (8%)
  Pallas kernels  9.05 us (7%)
  waiting for transfers between devices  8.28 us (7%)
    all_to_all x7, blocking collectives, exchange(): lax.all_to_all(split_up, axis, 0, 0, tiled=True).reshape(pieces.shape)  97 us
    pallas_call x10, Pallas kernels, call(): pl.pallas_call(body, out_shape=out[0] if one else out, in_specs=ins or [V...  9.05 us
    ppermute x1, waiting for transfers between devices, swapped(): lax.ppermute(block, 'col', [(c, (c + (2 if c % 2 else -2)) % N_COL) for c...  8.28 us
    ppermute x1, starting transfers between devices, swapped(): lax.ppermute(block, 'col', [(c, (c + (2 if c % 2 else -2)) % N_COL) for c...  5.81 us
    ppermute x1, starting transfers between devices, swapped_back(): lax.ppermute(block, 'col', [(c, (c + (-2 if c % 2 else 2)) % N_COL) for c...  4.48 us
  transfers between devices with their start and end apart: 2, of which 1 were waited for; matrix products, arithmetic and copies ran while one was open for 0% of the time, Pallas kernels for 2%

profile of v9, /device:TPU:1, one launch (start us, length us, event | category | flops | bytes accessed | tf_op | source)
XLA Modules:
  0.0 125.3 jit_solution(17181018677537431672)
XLA Ops:
  0.6 1.5 %shard_map.41 = f32[576,128]{1,0:T(8,128)S(1)} custom-call(f32[256,512]{1,0:T(8,128)} %matrix.3), custom_call_target="tpu_custom_call" | custom-call | flops 100663296 | bytes 819200 | tf_op jit(solution)/shard_map/pallas_call | solution.py:270
  2.1 13.0 %all_to_all.35 = f32[8,72,128]{2,1,0:T(8,128)S(1)} all-to-all(f32[8,72,128]{2,1,0:T(8,128)S(1)} %bitcast.20), channel_id=1, replica_groups=mesh['col'=8,'zl'=2,'y'=8,'x'=4] {'zl','x'}, dimensions={0} | all-to-all | bytes 589824 | tf_op jit(solution)/shard_map/all_to_all | solution.py:301
  15.1 16.5 %all_to_all.36 = f32[8,72,128]{2,1,0:T(8,128)S(1)} all-to-all(f32[8,72,128]{2,1,0:T(8,128)S(1)} %bitcast.22), channel_id=1, replica_groups=mesh['col'=8,'zl'=2,'y'=8,'x'=4] {'y'}, dimensions={0} | all-to-all | bytes 589824 | tf_op jit(solution)/shard_map/all_to_all | solution.py:301
  31.6 0.0 copy-start
  31.6 0.1 shard_map.43
  31.7 9.8 %all_to_all.37 = f32[8,64,128]{2,1,0:T(8,128)S(1)} all-to-all(f32[8,64,128]{2,1,0:T(8,128)S(1)} %bitcast.24), channel_id=1, replica_groups=mesh['col'=8,'zl'=2,'y'=8,'x'=4] {'zl','x'}, dimensions={0} | all-to-all | bytes 524288 | tf_op jit(solution)/shard_map/all_to_all | solution.py:301
  41.5 0.0 copy-done
  41.5 0.0 copy-start.1
  41.5 1.3 %shard_map.45 = f32[256,256]{1,0:T(8,128)S(1)} custom-call(f32[256,512]{1,0:T(8,128)S(1)} %copy-done, f32[512,128]{1,0:T(8,128)S(1)} %bitcast.26), custom_call_target="tpu_custom_call" | custom-call | flops 503316480 | bytes 1048576 | tf_op jit(solution)/shard_map/pallas_call | solution.py:270
  42.8 5.8 %collective-permute-start = (f32[256,256]{1,0:T(8,128)S(1)}, f32[256,256]{1,0:T(8,128)S(1)}, u32[]{:S(2)}, u32[]{:S(2)}) collective-permute-start(f32[256,256]{1,0:T(8,128)S(1)} %shard_map.45), channel_id=1, source_target_pairs={{0,384},{64,192},{128,0},{192,320},{256,128},{320,448},{384,256},{... | collective-permute-start | bytes 786440 | tf_op jit(solution)/shard_map/ppermute | solution.py:285
  48.6 0.0 copy-done.1
  48.7 2.3 %shard_map.44 = (f32[256,256]{1,0:T(8,128)S(1)}, f32[256,256]{1,0:T(8,128)S(1)}, f32[32,128]{1,0:T(8,128)S(1)}) custom-call(f32[256,512]{1,0:T(8,128)S(1)} %copy-done, f32[512,128]{1,0:T(8,128)S(1)} %bitcast.27, s32[16]{0:T(128)S(1)} %copy-done.1), custom_call_target="tpu_custom_call" | custom-call | flops 603979776 | bytes 1327168 | tf_op jit(solution)/shard_map/pallas_call | solution.py:270
  50.9 8.3 %collective-permute-done.guest = f32[256,256]{1,0:T(8,128)S(1)} collective-permute-done((f32[256,256]{1,0:T(8,128)S(1)}, f32[256,256]{1,0:T(8,128)S(1)}, u32[]{:S(2)}, u32[]{:S(2)}) %collective-permute-start) | collective-permute-done | bytes 262176 | tf_op jit(solution)/shard_map/ppermute | solution.py:285
  59.2 0.4 shard_map.46
  59.6 10.3 %all_to_all.38 = f32[8,136,128]{2,1,0:T(8,128)S(1)} all-to-all(f32[8,136,128]{2,1,0:T(8,128)S(1)} %bitcast.15), channel_id=1, replica_groups=mesh['col'=8,'zl'=2,'y'=8,'x'=4] {'zl','x'}, dimensions={0} | all-to-all | bytes 1114112 | tf_op jit(solution)/shard_map/all_to_all | solution.py:301
  70.0 15.4 %all_to_all.39 = f32[8,136,128]{2,1,0:T(8,128)S(1)} all-to-all(f32[8,136,128]{2,1,0:T(8,128)S(1)} %bitcast.17), channel_id=1, replica_groups=mesh['col'=8,'zl'=2,'y'=8,'x'=4] {'y'}, dimensions={0} | all-to-all | bytes 1114112 | tf_op jit(solution)/shard_map/all_to_all | solution.py:301
  85.5 10.3 %all_to_all.40 = f32[8,136,128]{2,1,0:T(8,128)S(1)} all-to-all(f32[8,136,128]{2,1,0:T(8,128)S(1)} %bitcast.19), channel_id=1, replica_groups=mesh['col'=8,'zl'=2,'y'=8,'x'=4] {'zl','x'}, dimensions={0} | all-to-all | bytes 1114112 | tf_op jit(solution)/shard_map/all_to_all | solution.py:301
  95.8 2.6 %shard_map.49 = (f32[256,256]{1,0:T(8,128)S(1)}, f32[32,128]{1,0:T(8,128)S(1)}, f32[256,512]{1,0:T(8,128)}) custom-call(f32[256,256]{1,0:T(8,128)S(1)} %get-tuple-element.11.keep, f32[256,256]{1,0:T(8,128)S(1)} %collective-permute-done.guest, f32[1088,128]{1,0:T(8,128)S(1)} %bitcast.25), custom_call_target="tpu_custom_call" | custom-call | flops 1811939328 | bytes 1884160 | tf_op jit(solution)/shard_map/pallas_call | solution.py:270
  98.4 4.5 %collective-permute-start.1 = (f32[256,256]{1,0:T(8,128)S(1)}, f32[256,256]{1,0:T(8,128)S(1)}, u32[]{:S(2)}, u32[]{:S(2)}) collective-permute-start(f32[256,256]{1,0:T(8,128)S(1)} %get-tuple-element.13), channel_id=1, source_target_pairs={{0,128},{64,448},{128,256},{192,64},{256,384},{320,192},{384,0},{4... | collective-permute-start | bytes 786440 | tf_op jit(solution)/shard_map/ppermute | solution.py:291
  102.9 21.7 %all_to_all.41 = f32[8,4,128]{2,1,0:T(4,128)S(1)} all-to-all(f32[8,4,128]{2,1,0:T(4,128)S(1)} %bitcast.29), channel_id=1, replica_groups=mesh['col'=8,'zl'=2,'y'=8,'x'=4] {'col'}, dimensions={0} | all-to-all | bytes 32768 | tf_op jit(solution)/shard_map/all_to_all | solution.py:301
  124.6 0.0 collective-permute-done.1.back
  124.6 0.7 shard_map.50
  (3 shorter events, 0.1 us)
Async XLA Ops:
  31.6 10.0 %copy-start = (f32[256,512]{1,0:T(8,128)S(1)}, f32[256,512]{1,0:T(8,128)}, u32[]{:S(2)}) copy-start(f32[256,512]{1,0:T(8,128)} %matrix.3) | copy-start | bytes 1572868
  41.5 7.1 %copy-start.1 = (s32[16]{0:T(128)S(1)}, s32[16]{0:T(128)}, u32[]{:S(2)}) copy-start(s32[16]{0:T(128)} %seats.1) | copy-start | bytes 196
  42.8 16.4 %collective-permute-start = (f32[256,256]{1,0:T(8,128)S(1)}, f32[256,256]{1,0:T(8,128)S(1)}, u32[]{:S(2)}, u32[]{:S(2)}) collective-permute-start(f32[256,256]{1,0:T(8,128)S(1)} %shard_map.45), channel_id=1, source_target_pairs={{0,384},{64,192},{128,0},{192,320},{256,128},{320,448},{384,256},{... | collective-permute-start | bytes 786440 | tf_op jit(solution)/shard_map/ppermute | solution.py:285
  98.4 26.2 %collective-permute-start.1 = (f32[256,256]{1,0:T(8,128)S(1)}, f32[256,256]{1,0:T(8,128)S(1)}, u32[]{:S(2)}, u32[]{:S(2)}) collective-permute-start(f32[256,256]{1,0:T(8,128)S(1)} %get-tuple-element.13), channel_id=1, source_target_pairs={{0,128},{64,448},{128,256},{192,64},{256,384},{320,192},{384,0},{4... | collective-permute-start | bytes 786440 | tf_op jit(solution)/shard_map/ppermute | solution.py:291

commit v10 on v9

--- a/solution.py
+++ b/solution.py
@@ -13,8 +13,8 @@
 N_COL = 8
 ZL, Y, X = 2, 8, 4
 EIGHT = 8
-NARROW = 72
-WIDE = 136
+NARROW = 66
+WIDE = 129
 LOADS = 8
 LIMIT = 32 * 1024 * 1024
 LOAD_LIMIT = 56000000
@@ -90,9 +90,8 @@
         at = NARROW * r
         out[at : at + 64, :] = cross[64 * r : 64 * r + 64]
         half = (r % 4) // 2
-        pair = [norm_keep[:, 128 * half : 128 * half + 128]]
-        pair.append(norm_move[:, 128 * (r // 4) : 128 * (r // 4) + 128])
-        out[at + 64 : at + 72, :] = jnp.concatenate(pair * 4, axis=0)
+        out[at + 64 : at + 65, :] = norm_keep[:, 128 * half : 128 * half + 128]
+        out[at + 65 : at + 66, :] = norm_move[:, 128 * (r // 4) : 128 * (r // 4) + 128]
 
 
 def square_index():
@@ -110,12 +109,11 @@
     rows, cols = square_index()
     grams = stacked(jnp.where(rows <= cols, gram_keep[...], product(parts, parts, 0, 0)))
     norms = column_squares(guest[...])
-    norms = jnp.concatenate([norms[:, :128], norms[:, 128:]] * 4, axis=0)
     for r in range(EIGHT):
         at = WIDE * r
         out[at : at + 64, :] = cross[64 * r : 64 * r + 64]
         out[at + 64 : at + 128, :] = grams[64 * r : 64 * r + 64]
-        out[at + 128 : at + 136, :] = norms
+        out[at + 128 : at + 129, :] = norms[:, 128 * (r // 4) : 128 * (r // 4) + 128]
 
 
 def added(got, size):
@@ -178,7 +176,8 @@
 
 
 def guest_squares(got):
-    return jnp.concatenate([got[128:129, :], got[129:130, :]], axis=1)
+    at = 4 * WIDE + 128
+    return jnp.concatenate([got[128:129, :], got[at : at + 1, :]], axis=1)
 
 
 def half_of(ref, odd):
@@ -297,7 +296,10 @@
 
 
 def exchange(pieces, axis):
-    split_up = pieces.reshape(lax.axis_size(axis), -1, 128)
+    n = lax.axis_size(axis)
+    rows = pieces.shape[0] // n
+    shape = (n, rows, 128) if rows % 4 == 0 else (n, 1, rows * 128)
+    split_up = pieces.reshape(shape)
     return lax.all_to_all(split_up, axis, 0, 0, tiled=True).reshape(pieces.shape)
 
 

time: 126 us -> 127 us (level)
  no operation moved by 1% of the time
where the time goes in v10:
time: 127 us; the launch traced here: 126 us
  blocking collectives  97.9 us (77%)
  starting transfers between devices  10.2 us (8%)
  Pallas kernels  9.1 us (7%)
  waiting for transfers between devices  8.28 us (7%)
    all_to_all x7, blocking collectives, exchange(): lax.all_to_all(split_up, axis, 0, 0, tiled=True).reshape(pieces.shape)  97.9 us
    pallas_call x10, Pallas kernels, call(): pl.pallas_call(body, out_shape=out[0] if one else out, in_specs=ins or [V...  9.1 us
    ppermute x1, waiting for transfers between devices, swapped(): lax.ppermute(block, 'col', [(c, (c + (2 if c % 2 else -2)) % N_COL) for c...  8.28 us
    ppermute x1, starting transfers between devices, swapped(): lax.ppermute(block, 'col', [(c, (c + (2 if c % 2 else -2)) % N_COL) for c...  5.81 us
    ppermute x1, starting transfers between devices, swapped_back(): lax.ppermute(block, 'col', [(c, (c + (-2 if c % 2 else 2)) % N_COL) for c...  4.42 us
  transfers between devices with their start and end apart: 2, of which 1 were waited for; matrix products, arithmetic and copies ran while one was open for 0% of the time, Pallas kernels for 2%

profile of v10, /device:TPU:1, one launch (start us, length us, event | category | flops | bytes accessed | tf_op | source)
XLA Modules:
  0.0 126.2 jit_solution(1016692314200651763)
XLA Ops:
  0.6 1.5 %shard_map.41 = f32[528,128]{1,0:T(8,128)S(1)} custom-call(f32[256,512]{1,0:T(8,128)} %matrix.3), custom_call_target="tpu_custom_call" | custom-call | flops 100663296 | bytes 794624 | tf_op jit(solution)/shard_map/pallas_call | solution.py:269
  2.1 12.9 %all_to_all.35 = f32[8,1,8448]{2,1,0:T(1,128)S(1)} all-to-all(f32[8,1,8448]{2,1,0:T(1,128)S(1)} %bitcast.20), channel_id=1, replica_groups=mesh['col'=8,'zl'=2,'y'=8,'x'=4] {'zl','x'}, dimensions={0} | all-to-all | bytes 540672 | tf_op jit(solution)/shard_map/all_to_all | solution.py:303
  15.0 16.1 %all_to_all.36 = f32[8,1,8448]{2,1,0:T(1,128)S(1)} all-to-all(f32[8,1,8448]{2,1,0:T(1,128)S(1)} %bitcast.22), channel_id=1, replica_groups=mesh['col'=8,'zl'=2,'y'=8,'x'=4] {'y'}, dimensions={0} | all-to-all | bytes 540672 | tf_op jit(solution)/shard_map/all_to_all | solution.py:303
  31.1 0.0 copy-start
  31.1 0.1 shard_map.43
  31.3 8.6 %all_to_all.37 = f32[8,64,128]{2,1,0:T(8,128)S(1)} all-to-all(f32[8,64,128]{2,1,0:T(8,128)S(1)} %bitcast.24), channel_id=1, replica_groups=mesh['col'=8,'zl'=2,'y'=8,'x'=4] {'zl','x'}, dimensions={0} | all-to-all | bytes 524288 | tf_op jit(solution)/shard_map/all_to_all | solution.py:303
  39.9 0.0 copy-done
  39.9 0.0 copy-start.1
  39.9 1.3 %shard_map.45 = f32[256,256]{1,0:T(8,128)S(1)} custom-call(f32[256,512]{1,0:T(8,128)S(1)} %copy-done, f32[512,128]{1,0:T(8,128)S(1)} %bitcast.26), custom_call_target="tpu_custom_call" | custom-call | flops 503316480 | bytes 1048576 | tf_op jit(solution)/shard_map/pallas_call | solution.py:269
  41.2 5.8 %collective-permute-start = (f32[256,256]{1,0:T(8,128)S(1)}, f32[256,256]{1,0:T(8,128)S(1)}, u32[]{:S(2)}, u32[]{:S(2)}) collective-permute-start(f32[256,256]{1,0:T(8,128)S(1)} %shard_map.45), channel_id=1, source_target_pairs={{0,384},{64,192},{128,0},{192,320},{256,128},{320,448},{384,256},{... | collective-permute-start | bytes 786440 | tf_op jit(solution)/shard_map/ppermute | solution.py:284
  47.0 0.0 copy-done.1
  47.0 2.3 %shard_map.44 = (f32[256,256]{1,0:T(8,128)S(1)}, f32[256,256]{1,0:T(8,128)S(1)}, f32[32,128]{1,0:T(8,128)S(1)}) custom-call(f32[256,512]{1,0:T(8,128)S(1)} %copy-done, f32[512,128]{1,0:T(8,128)S(1)} %bitcast.27, s32[16]{0:T(128)S(1)} %copy-done.1), custom_call_target="tpu_custom_call" | custom-call | flops 603979776 | bytes 1327168 | tf_op jit(solution)/shard_map/pallas_call | solution.py:269
  49.3 8.3 %collective-permute-done.guest = f32[256,256]{1,0:T(8,128)S(1)} collective-permute-done((f32[256,256]{1,0:T(8,128)S(1)}, f32[256,256]{1,0:T(8,128)S(1)}, u32[]{:S(2)}, u32[]{:S(2)}) %collective-permute-start) | collective-permute-done | bytes 262176 | tf_op jit(solution)/shard_map/ppermute | solution.py:284
  57.6 0.4 shard_map.46
  58.0 10.2 %all_to_all.38 = f32[8,1,16512]{2,1,0:T(1,128)S(1)} all-to-all(f32[8,1,16512]{2,1,0:T(1,128)S(1)} %bitcast.15), channel_id=1, replica_groups=mesh['col'=8,'zl'=2,'y'=8,'x'=4] {'zl','x'}, dimensions={0} | all-to-all | bytes 1056768 | tf_op jit(solution)/shard_map/all_to_all | solution.py:303
  68.2 0.1 shard_map.47
  68.3 14.7 %all_to_all.39 = f32[8,1,16512]{2,1,0:T(1,128)S(1)} all-to-all(f32[8,1,16512]{2,1,0:T(1,128)S(1)} %bitcast.17), channel_id=1, replica_groups=mesh['col'=8,'zl'=2,'y'=8,'x'=4] {'y'}, dimensions={0} | all-to-all | bytes 1056768 | tf_op jit(solution)/shard_map/all_to_all | solution.py:303
  83.0 0.1 shard_map.48
  83.1 10.2 %all_to_all.40 = f32[8,1,16512]{2,1,0:T(1,128)S(1)} all-to-all(f32[8,1,16512]{2,1,0:T(1,128)S(1)} %bitcast.19), channel_id=1, replica_groups=mesh['col'=8,'zl'=2,'y'=8,'x'=4] {'zl','x'}, dimensions={0} | all-to-all | bytes 1056768 | tf_op jit(solution)/shard_map/all_to_all | solution.py:303
  93.3 2.7 %shard_map.49 = (f32[256,256]{1,0:T(8,128)S(1)}, f32[32,128]{1,0:T(8,128)S(1)}, f32[256,512]{1,0:T(8,128)}) custom-call(f32[256,256]{1,0:T(8,128)S(1)} %get-tuple-element.11.keep, f32[256,256]{1,0:T(8,128)S(1)} %collective-permute-done.guest, f32[1032,128]{1,0:T(8,128)S(1)} %bitcast.25), custom_call_target="tpu_custom_call" | custom-call | flops 1811939328 | bytes 1855488 | tf_op jit(solution)/shard_map/pallas_call | solution.py:269
  96.0 4.4 %collective-permute-start.1 = (f32[256,256]{1,0:T(8,128)S(1)}, f32[256,256]{1,0:T(8,128)S(1)}, u32[]{:S(2)}, u32[]{:S(2)}) collective-permute-start(f32[256,256]{1,0:T(8,128)S(1)} %get-tuple-element.13), channel_id=1, source_target_pairs={{0,128},{64,448},{128,256},{192,64},{256,384},{320,192},{384,0},{4... | collective-permute-start | bytes 786440 | tf_op jit(solution)/shard_map/ppermute | solution.py:290
  100.4 25.1 %all_to_all.41 = f32[8,4,128]{2,1,0:T(4,128)S(1)} all-to-all(f32[8,4,128]{2,1,0:T(4,128)S(1)} %bitcast.29), channel_id=1, replica_groups=mesh['col'=8,'zl'=2,'y'=8,'x'=4] {'col'}, dimensions={0} | all-to-all | bytes 32768 | tf_op jit(solution)/shard_map/all_to_all | solution.py:303
  125.5 0.0 collective-permute-done.1.back
  125.5 0.7 shard_map.50
  (1 shorter events, 0.0 us)
Async XLA Ops:
  31.1 8.7 %copy-start = (f32[256,512]{1,0:T(8,128)S(1)}, f32[256,512]{1,0:T(8,128)}, u32[]{:S(2)}) copy-start(f32[256,512]{1,0:T(8,128)} %matrix.3) | copy-start | bytes 1572868
  39.9 7.1 %copy-start.1 = (s32[16]{0:T(128)S(1)}, s32[16]{0:T(128)}, u32[]{:S(2)}) copy-start(s32[16]{0:T(128)} %seats.1) | copy-start | bytes 196
  41.2 16.4 %collective-permute-start = (f32[256,256]{1,0:T(8,128)S(1)}, f32[256,256]{1,0:T(8,128)S(1)}, u32[]{:S(2)}, u32[]{:S(2)}) collective-permute-start(f32[256,256]{1,0:T(8,128)S(1)} %shard_map.45), channel_id=1, source_target_pairs={{0,384},{64,192},{128,0},{192,320},{256,128},{320,448},{384,256},{... | collective-permute-start | bytes 786440 | tf_op jit(solution)/shard_map/ppermute | solution.py:284
  96.0 29.5 %collective-permute-start.1 = (f32[256,256]{1,0:T(8,128)S(1)}, f32[256,256]{1,0:T(8,128)S(1)}, u32[]{:S(2)}, u32[]{:S(2)}) collective-permute-start(f32[256,256]{1,0:T(8,128)S(1)} %get-tuple-element.13), channel_id=1, source_target_pairs={{0,128},{64,448},{128,256},{192,64},{256,384},{320,192},{384,0},{4... | collective-permute-start | bytes 786440 | tf_op jit(solution)/shard_map/ppermute | solution.py:290

commit v11 on v10

--- a/solution.py
+++ b/solution.py
@@ -11,7 +11,7 @@
 W = 256
 N_ROW = 64
 N_COL = 8
-ZL, Y, X = 2, 8, 4
+ROW_PARTS = (2, 4, 2, 4)
 EIGHT = 8
 NARROW = 66
 WIDE = 129
@@ -292,7 +292,7 @@
     )
 
 
-ROW = ("zl", "y", "x")
+ROW = ("z", "far", "near", "x")
 
 
 def exchange(pieces, axis):
@@ -315,12 +315,12 @@
         scratch=[pltpu.VMEM((W, 2 * W), jnp.float32), pltpu.SemaphoreType.DMA((LOADS,))],
     )(matrix)
     folded = local(functools.partial(fold, NARROW), 1, (NARROW * EIGHT, 128))(
-        exchange(sent, ("zl", "x"))
+        exchange(sent, ("z", "x"))
     )
     tiles = local(functools.partial(fold_first, total_rows), 1, (64 * EIGHT, 128))(
-        exchange(folded, "y")
-    )
-    tiles = exchange(tiles, ("zl", "x"))
+        exchange(folded, ("far", "near"))
+    )
+    tiles = exchange(tiles, ("z", "x"))
     move = local(first_move, 5 * one, (W, W))(matrix, tiles)
     guest = swapped(move)
     keep, gram, hits = local(
@@ -328,9 +328,9 @@
     )(matrix, tiles, seats)
     sent = local(pack_second, 2 * one, (WIDE * EIGHT, 128))(keep, guest, gram)
     fold_eight = local(functools.partial(fold, WIDE), 1, (WIDE * EIGHT, 128))
-    folded = fold_eight(exchange(sent, ("zl", "x")))
-    folded = fold_eight(exchange(folded, "y"))
-    got = exchange(folded, ("zl", "x"))
+    folded = fold_eight(exchange(sent, ("near", "x")))
+    folded = fold_eight(exchange(folded, ("z", "far")))
+    got = exchange(folded, ("near", "x"))
     new_guest, means, begun = local(
         functools.partial(second, total_rows),
         18 * one,
@@ -356,7 +356,7 @@
 
 
 def solution(mesh):
-    parts = Mesh(mesh.devices.reshape(N_COL, ZL, Y, X), ("col",) + ROW)
+    parts = Mesh(mesh.devices.reshape(N_COL, *ROW_PARTS), ("col",) + ROW)
     placed = (P(ROW, "col"), P())
     return jax.shard_map(
         on_device,

time: 127 us -> 130 us (1.024)
  blocking collectives: 97.9 us -> 101 us
    all_to_all x7, blocking collectives: 97.9 us -> 101 us  [exchange(): lax.all_to_all(split_up, axis, 0, 0, tiled=True).reshape(pieces.shape)]
where the time goes in v11:
time: 130 us; the launch traced here: 129 us
  blocking collectives  101 us (78%)
  starting transfers between devices  10.6 us (8%)
  Pallas kernels  9.1 us (7%)
  waiting for transfers between devices  8.28 us (6%)
    all_to_all x7, blocking collectives, exchange(): lax.all_to_all(split_up, axis, 0, 0, tiled=True).reshape(pieces.shape)  101 us
    pallas_call x10, Pallas kernels, call(): pl.pallas_call(body, out_shape=out[0] if one else out, in_specs=ins or [V...  9.1 us
    ppermute x1, waiting for transfers between devices, swapped(): lax.ppermute(block, 'col', [(c, (c + (2 if c % 2 else -2)) % N_COL) for c...  8.28 us
    ppermute x1, starting transfers between devices, swapped(): lax.ppermute(block, 'col', [(c, (c + (2 if c % 2 else -2)) % N_COL) for c...  5.81 us
    ppermute x1, starting transfers between devices, swapped_back(): lax.ppermute(block, 'col', [(c, (c + (-2 if c % 2 else 2)) % N_COL) for c...  4.81 us
  transfers between devices with their start and end apart: 2, of which 1 were waited for; matrix products, arithmetic and copies ran while one was open for 0% of the time, Pallas kernels for 2%

profile of v11, /device:TPU:1, one launch (start us, length us, event | category | flops | bytes accessed | tf_op | source)
XLA Modules:
  0.0 129.4 jit_solution(8969631290991471744)
XLA Ops:
  0.6 1.5 %shard_map.41 = f32[528,128]{1,0:T(8,128)S(1)} custom-call(f32[256,512]{1,0:T(8,128)} %matrix.3), custom_call_target="tpu_custom_call" | custom-call | flops 100663296 | bytes 794624 | tf_op jit(solution)/shard_map/pallas_call | solution.py:269
  2.1 12.9 %all_to_all.35 = f32[8,1,8448]{2,1,0:T(1,128)S(1)} all-to-all(f32[8,1,8448]{2,1,0:T(1,128)S(1)} %bitcast.20), channel_id=1, replica_groups=mesh['col'=8,'z'=2,'far'=4,'near'=2,'x'=4] {'z','x'}, dimensions={0} | all-to-all | bytes 540672 | tf_op jit(solution)/shard_map/all_to_all | solution.py:303
  15.0 16.1 %all_to_all.36 = f32[8,1,8448]{2,1,0:T(1,128)S(1)} all-to-all(f32[8,1,8448]{2,1,0:T(1,128)S(1)} %bitcast.22), channel_id=1, replica_groups=mesh['col'=8,'z'=2,'far'=4,'near'=2,'x'=4] {'far','near'}, dimensions={0} | all-to-all | bytes 540672 | tf_op jit(solution)/shard_map/all_to_all | solution.py:303
  31.1 0.0 copy-start
  31.1 0.1 shard_map.43
  31.3 8.6 %all_to_all.37 = f32[8,64,128]{2,1,0:T(8,128)S(1)} all-to-all(f32[8,64,128]{2,1,0:T(8,128)S(1)} %bitcast.24), channel_id=1, replica_groups=mesh['col'=8,'z'=2,'far'=4,'near'=2,'x'=4] {'z','x'}, dimensions={0} | all-to-all | bytes 524288 | tf_op jit(solution)/shard_map/all_to_all | solution.py:303
  39.9 0.0 copy-done
  39.9 0.0 copy-start.1
  39.9 1.3 shard_map.45
  41.2 5.8 %collective-permute-start = (f32[256,256]{1,0:T(8,128)S(1)}, f32[256,256]{1,0:T(8,128)S(1)}, u32[]{:S(2)}, u32[]{:S(2)}) collective-permute-start(f32[256,256]{1,0:T(8,128)S(1)} %shard_map.45), channel_id=1, source_target_pairs={{0,384},{64,192},{128,0},{192,320},{256,128},{320,448},{384,256},{... | collective-permute-start | bytes 786440 | tf_op jit(solution)/shard_map/ppermute | solution.py:284
  47.0 0.0 copy-done.1
  47.0 2.3 %shard_map.44 = (f32[256,256]{1,0:T(8,128)S(1)}, f32[256,256]{1,0:T(8,128)S(1)}, f32[32,128]{1,0:T(8,128)S(1)}) custom-call(f32[256,512]{1,0:T(8,128)S(1)} %copy-done, f32[512,128]{1,0:T(8,128)S(1)} %bitcast.27, s32[16]{0:T(128)S(1)} %copy-done.1), custom_call_target="tpu_custom_call" | custom-call | flops 603979776 | bytes 1327168 | tf_op jit(solution)/shard_map/pallas_call | solution.py:269
  49.3 8.3 %collective-permute-done.guest = f32[256,256]{1,0:T(8,128)S(1)} collective-permute-done((f32[256,256]{1,0:T(8,128)S(1)}, f32[256,256]{1,0:T(8,128)S(1)}, u32[]{:S(2)}, u32[]{:S(2)}) %collective-permute-start) | collective-permute-done | bytes 262176 | tf_op jit(solution)/shard_map/ppermute | solution.py:284
  57.6 0.4 shard_map.46
  58.0 10.2 %all_to_all.38 = f32[8,1,16512]{2,1,0:T(1,128)S(1)} all-to-all(f32[8,1,16512]{2,1,0:T(1,128)S(1)} %bitcast.15), channel_id=1, replica_groups=mesh['col'=8,'z'=2,'far'=4,'near'=2,'x'=4] {'near','x'}, dimensions={0} | all-to-all | bytes 1056768 | tf_op jit(solution)/shard_map/all_to_all | solution.py:303
  68.2 0.1 shard_map.47
  68.3 15.7 %all_to_all.39 = f32[8,1,16512]{2,1,0:T(1,128)S(1)} all-to-all(f32[8,1,16512]{2,1,0:T(1,128)S(1)} %bitcast.17), channel_id=1, replica_groups=mesh['col'=8,'z'=2,'far'=4,'near'=2,'x'=4] {'z','far'}, dimensions={0} | all-to-all | bytes 1056768 | tf_op jit(solution)/shard_map/all_to_all | solution.py:303
  84.0 0.1 shard_map.48
  84.0 10.2 %all_to_all.40 = f32[8,1,16512]{2,1,0:T(1,128)S(1)} all-to-all(f32[8,1,16512]{2,1,0:T(1,128)S(1)} %bitcast.19), channel_id=1, replica_groups=mesh['col'=8,'z'=2,'far'=4,'near'=2,'x'=4] {'near','x'}, dimensions={0} | all-to-all | bytes 1056768 | tf_op jit(solution)/shard_map/all_to_all | solution.py:303
  94.3 2.7 %shard_map.49 = (f32[256,256]{1,0:T(8,128)S(1)}, f32[32,128]{1,0:T(8,128)S(1)}, f32[256,512]{1,0:T(8,128)}) custom-call(f32[256,256]{1,0:T(8,128)S(1)} %get-tuple-element.11.keep, f32[256,256]{1,0:T(8,128)S(1)} %collective-permute-done.guest, f32[1032,128]{1,0:T(8,128)S(1)} %bitcast.25), custom_call_target="tpu_custom_call" | custom-call | flops 1811939328 | bytes 1855488 | tf_op jit(solution)/shard_map/pallas_call | solution.py:269
  96.9 4.8 %collective-permute-start.1 = (f32[256,256]{1,0:T(8,128)S(1)}, f32[256,256]{1,0:T(8,128)S(1)}, u32[]{:S(2)}, u32[]{:S(2)}) collective-permute-start(f32[256,256]{1,0:T(8,128)S(1)} %get-tuple-element.13), channel_id=1, source_target_pairs={{0,128},{64,448},{128,256},{192,64},{256,384},{320,192},{384,0},{4... | collective-permute-start | bytes 786440 | tf_op jit(solution)/shard_map/ppermute | solution.py:290
  101.7 26.9 %all_to_all.41 = f32[8,4,128]{2,1,0:T(4,128)S(1)} all-to-all(f32[8,4,128]{2,1,0:T(4,128)S(1)} %bitcast.29), channel_id=1, replica_groups=mesh['col'=8,'z'=2,'far'=4,'near'=2,'x'=4] {'col'}, dimensions={0} | all-to-all | bytes 32768 | tf_op jit(solution)/shard_map/all_to_all | solution.py:303
  128.6 0.0 collective-permute-done.1.back
  128.6 0.7 shard_map.50
  (1 shorter events, 0.0 us)
Async XLA Ops:
  31.1 8.7 %copy-start = (f32[256,512]{1,0:T(8,128)S(1)}, f32[256,512]{1,0:T(8,128)}, u32[]{:S(2)}) copy-start(f32[256,512]{1,0:T(8,128)} %matrix.3) | copy-start | bytes 1572868
  39.9 7.1 %copy-start.1 = (s32[16]{0:T(128)S(1)}, s32[16]{0:T(128)}, u32[]{:S(2)}) copy-start(s32[16]{0:T(128)} %seats.1) | copy-start | bytes 196
  41.2 16.4 %collective-permute-start = (f32[256,256]{1,0:T(8,128)S(1)}, f32[256,256]{1,0:T(8,128)S(1)}, u32[]{:S(2)}, u32[]{:S(2)}) collective-permute-start(f32[256,256]{1,0:T(8,128)S(1)} %shard_map.45), channel_id=1, source_target_pairs={{0,384},{64,192},{128,0},{192,320},{256,128},{320,448},{384,256},{... | collective-permute-start | bytes 786440 | tf_op jit(solution)/shard_map/ppermute | solution.py:284
  96.9 31.7 %collective-permute-start.1 = (f32[256,256]{1,0:T(8,128)S(1)}, f32[256,256]{1,0:T(8,128)S(1)}, u32[]{:S(2)}, u32[]{:S(2)}) collective-permute-start(f32[256,256]{1,0:T(8,128)S(1)} %get-tuple-element.13), channel_id=1, source_target_pairs={{0,128},{64,448},{128,256},{192,64},{256,384},{320,192},{384,0},{4... | collective-permute-start | bytes 786440 | tf_op jit(solution)/shard_map/ppermute | solution.py:290

commit v12 on v10

--- a/solution.py
+++ b/solution.py
@@ -14,7 +14,7 @@
 ZL, Y, X = 2, 8, 4
 EIGHT = 8
 NARROW = 66
-WIDE = 129
+WIDE = 136
 LOADS = 8
 LIMIT = 32 * 1024 * 1024
 LOAD_LIMIT = 56000000
@@ -109,11 +109,12 @@
     rows, cols = square_index()
     grams = stacked(jnp.where(rows <= cols, gram_keep[...], product(parts, parts, 0, 0)))
     norms = column_squares(guest[...])
+    norms = jnp.concatenate([norms[:, :128], norms[:, 128:]] * 4, axis=0)
     for r in range(EIGHT):
         at = WIDE * r
         out[at : at + 64, :] = cross[64 * r : 64 * r + 64]
         out[at + 64 : at + 128, :] = grams[64 * r : 64 * r + 64]
-        out[at + 128 : at + 129, :] = norms[:, 128 * (r // 4) : 128 * (r // 4) + 128]
+        out[at + 128 : at + 136, :] = norms
 
 
 def added(got, size):
@@ -176,8 +177,7 @@
 
 
 def guest_squares(got):
-    at = 4 * WIDE + 128
-    return jnp.concatenate([got[128:129, :], got[at : at + 1, :]], axis=1)
+    return jnp.concatenate([got[128:129, :], got[129:130, :]], axis=1)
 
 
 def half_of(ref, odd):

time: 127 us -> 127 us (level)
  no operation moved by 1% of the time
where the time goes in v12:
time: 127 us
  blocking collectives  98.6 us (78%)
  starting transfers between devices  10.3 us (8%)
  Pallas kernels  9.05 us (7%)
  waiting for transfers between devices  8.28 us (7%)
    all_to_all x7, blocking collectives, exchange(): lax.all_to_all(split_up, axis, 0, 0, tiled=True).reshape(pieces.shape)  98.6 us
    pallas_call x10, Pallas kernels, call(): pl.pallas_call(body, out_shape=out[0] if one else out, in_specs=ins or [V...  9.05 us
    ppermute x1, waiting for transfers between devices, swapped(): lax.ppermute(block, 'col', [(c, (c + (2 if c % 2 else -2)) % N_COL) for c...  8.28 us
    ppermute x1, starting transfers between devices, swapped(): lax.ppermute(block, 'col', [(c, (c + (2 if c % 2 else -2)) % N_COL) for c...  5.81 us
    ppermute x1, starting transfers between devices, swapped_back(): lax.ppermute(block, 'col', [(c, (c + (-2 if c % 2 else 2)) % N_COL) for c...  4.46 us
  transfers between devices with their start and end apart: 2, of which 1 were waited for; matrix products, arithmetic and copies ran while one was open for 0% of the time, Pallas kernels for 2%

profile of v12, /device:TPU:1, one launch (start us, length us, event | category | flops | bytes accessed | tf_op | source)
XLA Modules:
  0.0 126.9 jit_solution(9014387011870014709)
XLA Ops:
  0.6 1.5 %shard_map.41 = f32[528,128]{1,0:T(8,128)S(1)} custom-call(f32[256,512]{1,0:T(8,128)} %matrix.3), custom_call_target="tpu_custom_call" | custom-call | flops 100663296 | bytes 794624 | tf_op jit(solution)/shard_map/pallas_call | solution.py:269
  2.1 12.9 %all_to_all.35 = f32[8,1,8448]{2,1,0:T(1,128)S(1)} all-to-all(f32[8,1,8448]{2,1,0:T(1,128)S(1)} %bitcast.20), channel_id=1, replica_groups=mesh['col'=8,'zl'=2,'y'=8,'x'=4] {'zl','x'}, dimensions={0} | all-to-all | bytes 540672 | tf_op jit(solution)/shard_map/all_to_all | solution.py:303
  15.0 16.1 %all_to_all.36 = f32[8,1,8448]{2,1,0:T(1,128)S(1)} all-to-all(f32[8,1,8448]{2,1,0:T(1,128)S(1)} %bitcast.22), channel_id=1, replica_groups=mesh['col'=8,'zl'=2,'y'=8,'x'=4] {'y'}, dimensions={0} | all-to-all | bytes 540672 | tf_op jit(solution)/shard_map/all_to_all | solution.py:303
  31.1 0.0 copy-start
  31.1 0.1 shard_map.43
  31.3 8.6 %all_to_all.37 = f32[8,64,128]{2,1,0:T(8,128)S(1)} all-to-all(f32[8,64,128]{2,1,0:T(8,128)S(1)} %bitcast.24), channel_id=1, replica_groups=mesh['col'=8,'zl'=2,'y'=8,'x'=4] {'zl','x'}, dimensions={0} | all-to-all | bytes 524288 | tf_op jit(solution)/shard_map/all_to_all | solution.py:303
  39.9 0.0 copy-done
  39.9 0.0 copy-start.1
  39.9 1.3 %shard_map.45 = f32[256,256]{1,0:T(8,128)S(1)} custom-call(f32[256,512]{1,0:T(8,128)S(1)} %copy-done, f32[512,128]{1,0:T(8,128)S(1)} %bitcast.26), custom_call_target="tpu_custom_call" | custom-call | flops 503316480 | bytes 1048576 | tf_op jit(solution)/shard_map/pallas_call | solution.py:269
  41.2 5.8 %collective-permute-start = (f32[256,256]{1,0:T(8,128)S(1)}, f32[256,256]{1,0:T(8,128)S(1)}, u32[]{:S(2)}, u32[]{:S(2)}) collective-permute-start(f32[256,256]{1,0:T(8,128)S(1)} %shard_map.45), channel_id=1, source_target_pairs={{0,384},{64,192},{128,0},{192,320},{256,128},{320,448},{384,256},{... | collective-permute-start | bytes 786440 | tf_op jit(solution)/shard_map/ppermute | solution.py:284
  47.0 0.0 copy-done.1
  47.0 2.3 %shard_map.44 = (f32[256,256]{1,0:T(8,128)S(1)}, f32[256,256]{1,0:T(8,128)S(1)}, f32[32,128]{1,0:T(8,128)S(1)}) custom-call(f32[256,512]{1,0:T(8,128)S(1)} %copy-done, f32[512,128]{1,0:T(8,128)S(1)} %bitcast.27, s32[16]{0:T(128)S(1)} %copy-done.1), custom_call_target="tpu_custom_call" | custom-call | flops 603979776 | bytes 1327168 | tf_op jit(solution)/shard_map/pallas_call | solution.py:269
  49.3 8.3 %collective-permute-done.guest = f32[256,256]{1,0:T(8,128)S(1)} collective-permute-done((f32[256,256]{1,0:T(8,128)S(1)}, f32[256,256]{1,0:T(8,128)S(1)}, u32[]{:S(2)}, u32[]{:S(2)}) %collective-permute-start) | collective-permute-done | bytes 262176 | tf_op jit(solution)/shard_map/ppermute | solution.py:284
  57.6 0.4 shard_map.46
  58.0 10.3 %all_to_all.38 = f32[8,136,128]{2,1,0:T(8,128)S(1)} all-to-all(f32[8,136,128]{2,1,0:T(8,128)S(1)} %bitcast.15), channel_id=1, replica_groups=mesh['col'=8,'zl'=2,'y'=8,'x'=4] {'zl','x'}, dimensions={0} | all-to-all | bytes 1114112 | tf_op jit(solution)/shard_map/all_to_all | solution.py:303
  68.3 14.9 %all_to_all.39 = f32[8,136,128]{2,1,0:T(8,128)S(1)} all-to-all(f32[8,136,128]{2,1,0:T(8,128)S(1)} %bitcast.17), channel_id=1, replica_groups=mesh['col'=8,'zl'=2,'y'=8,'x'=4] {'y'}, dimensions={0} | all-to-all | bytes 1114112 | tf_op jit(solution)/shard_map/all_to_all | solution.py:303
  83.3 10.3 %all_to_all.40 = f32[8,136,128]{2,1,0:T(8,128)S(1)} all-to-all(f32[8,136,128]{2,1,0:T(8,128)S(1)} %bitcast.19), channel_id=1, replica_groups=mesh['col'=8,'zl'=2,'y'=8,'x'=4] {'zl','x'}, dimensions={0} | all-to-all | bytes 1114112 | tf_op jit(solution)/shard_map/all_to_all | solution.py:303
  93.6 2.6 %shard_map.49 = (f32[256,256]{1,0:T(8,128)S(1)}, f32[32,128]{1,0:T(8,128)S(1)}, f32[256,512]{1,0:T(8,128)}) custom-call(f32[256,256]{1,0:T(8,128)S(1)} %get-tuple-element.11.keep, f32[256,256]{1,0:T(8,128)S(1)} %collective-permute-done.guest, f32[1088,128]{1,0:T(8,128)S(1)} %bitcast.25), custom_call_target="tpu_custom_call" | custom-call | flops 1811939328 | bytes 1884160 | tf_op jit(solution)/shard_map/pallas_call | solution.py:269
  96.2 4.5 %collective-permute-start.1 = (f32[256,256]{1,0:T(8,128)S(1)}, f32[256,256]{1,0:T(8,128)S(1)}, u32[]{:S(2)}, u32[]{:S(2)}) collective-permute-start(f32[256,256]{1,0:T(8,128)S(1)} %get-tuple-element.13), channel_id=1, source_target_pairs={{0,128},{64,448},{128,256},{192,64},{256,384},{320,192},{384,0},{4... | collective-permute-start | bytes 786440 | tf_op jit(solution)/shard_map/ppermute | solution.py:290
  100.7 25.4 %all_to_all.41 = f32[8,4,128]{2,1,0:T(4,128)S(1)} all-to-all(f32[8,4,128]{2,1,0:T(4,128)S(1)} %bitcast.29), channel_id=1, replica_groups=mesh['col'=8,'zl'=2,'y'=8,'x'=4] {'col'}, dimensions={0} | all-to-all | bytes 32768 | tf_op jit(solution)/shard_map/all_to_all | solution.py:303
  126.2 0.0 collective-permute-done.1.back
  126.2 0.7 shard_map.50
  (3 shorter events, 0.1 us)
Async XLA Ops:
  31.1 8.7 %copy-start = (f32[256,512]{1,0:T(8,128)S(1)}, f32[256,512]{1,0:T(8,128)}, u32[]{:S(2)}) copy-start(f32[256,512]{1,0:T(8,128)} %matrix.3) | copy-start | bytes 1572868
  39.9 7.1 %copy-start.1 = (s32[16]{0:T(128)S(1)}, s32[16]{0:T(128)}, u32[]{:S(2)}) copy-start(s32[16]{0:T(128)} %seats.1) | copy-start | bytes 196
  41.2 16.4 %collective-permute-start = (f32[256,256]{1,0:T(8,128)S(1)}, f32[256,256]{1,0:T(8,128)S(1)}, u32[]{:S(2)}, u32[]{:S(2)}) collective-permute-start(f32[256,256]{1,0:T(8,128)S(1)} %shard_map.45), channel_id=1, source_target_pairs={{0,384},{64,192},{128,0},{192,320},{256,128},{320,448},{384,256},{... | collective-permute-start | bytes 786440 | tf_op jit(solution)/shard_map/ppermute | solution.py:284
  96.2 29.9 %collective-permute-start.1 = (f32[256,256]{1,0:T(8,128)S(1)}, f32[256,256]{1,0:T(8,128)S(1)}, u32[]{:S(2)}, u32[]{:S(2)}) collective-permute-start(f32[256,256]{1,0:T(8,128)S(1)} %get-tuple-element.13), channel_id=1, source_target_pairs={{0,128},{64,448},{128,256},{192,64},{256,384},{320,192},{384,0},{4... | collective-permute-start | bytes 786440 | tf_op jit(solution)/shard_map/ppermute | solution.py:290

commit v13 on v9

--- a/solution.py
+++ b/solution.py
@@ -185,7 +185,7 @@
     return ref.at[:, pl.ds(pl.multiple_of(odd * W, W), W)]
 
 
-def second(total_rows, keep, guest, got, new_guest, sums, final, kept, done):
+def second(total_rows, keep, guest, got, new_guest, sums, x_out, z_out):
     crosses = from_wide(got, 0)
     grams = from_wide(got, 64)
     rows, cols = square_index()
@@ -194,19 +194,15 @@
     mean_guest = guest_squares(got) / total_rows
     sign = jnp.where(lax.rem(lax.axis_index("col"), 2) == 1, -0.5, 0.5) / total_rows
     x = crosses * (sign * lax.rsqrt(mean_keep + 1e-06)) * lax.rsqrt(mean_guest + 1e-06)
+    x_out[...] = x
     flipped_x = split(x.T)
     x = split(x)
     s_guest = product(flipped_x, flipped_x, 1, 1)
     s_keep = product(x, x, 1, 1)
-    old_keep, old_guest = keep[...], guest[...]
-    mixed_keep = old_keep - product(split(old_guest), x, 1, 1)
-    mixed_guest = old_guest + product(split(old_keep), x)
+    mixed_guest = guest[...] + product(split(keep[...]), x)
     z_guest, z = roots(s_guest, s_keep)
     zs, zs_guest = split(z), split(z_guest)
-    kept[...] = product(split(mixed_keep), zs)
-    odd = lax.rem(lax.axis_index("col"), 2)
-    copy = pltpu.make_async_copy(kept, half_of(final, odd), done)
-    copy.start()
+    z_out[...] = z
     new_guest[...] = product(split(mixed_guest), zs_guest)
     cross = split(crosses)
     flipped = grams.T
@@ -231,6 +227,14 @@
     tile = jnp.maximum(jnp.concatenate(four + four, axis=0) / total_rows, 0.0)
     for r in range(4 * N_COL // 8):
         sums[8 * r : 8 * r + 8, :] = tile
+
+
+def second_keep(keep, guest, x_in, z_in, final, kept, done):
+    mixed = keep[...] - product(split(guest[...]), split(x_in[...]), 1, 1)
+    kept[...] = product(split(mixed), split(z_in[...]))
+    odd = lax.rem(lax.axis_index("col"), 2)
+    copy = pltpu.make_async_copy(kept, half_of(final, odd), done)
+    copy.start()
     copy.wait()
 
 
@@ -329,15 +333,21 @@
     folded = fold_eight(exchange(sent, ("zl", "x")))
     folded = fold_eight(exchange(folded, "y"))
     got = exchange(folded, ("zl", "x"))
-    new_guest, means, begun = local(
+    new_guest, means, x, z = local(
         functools.partial(second, total_rows),
-        18 * one,
+        16 * one,
         (W, W),
         (4 * N_COL, 128),
+        (W, W),
+        (W, W),
+    )(keep, guest, got)
+    begun = local(
+        second_keep,
+        2 * one,
         (W, 2 * W),
-        outs=[VMEM, VMEM, HBM],
+        outs=[HBM],
         scratch=[pltpu.VMEM((W, W), jnp.float32), pltpu.SemaphoreType.DMA],
-    )(keep, guest, got)
+    )(keep, guest, x, z)
     back = swapped_back(new_guest)
     table = exchange(means, "col")
     final, picked = local(

time: 126 us -> 126 us (level)
  blocking collectives: 97 us -> 75.3 us
  starting transfers between devices: 10.3 us -> 24.6 us
  waiting for transfers between devices: 8.28 us -> 14 us
  Pallas kernels: 9.05 us -> 10.8 us
    all_to_all x7 -> x6, blocking collectives: 97 us -> 75.3 us  [exchange(): lax.all_to_all(split_up, axis, 0, 0, tiled=True).reshape(pieces.shape)]
    all_to_all x0 -> x1, starting transfers between devices: none -> 14.3 us  [exchange(): lax.all_to_all(split_up, axis, 0, 0, tiled=True).reshape(pieces.shape)]
    all_to_all x0 -> x1, waiting for transfers between devices: none -> 5.7 us  [exchange(): lax.all_to_all(split_up, axis, 0, 0, tiled=True).reshape(pieces.shape)]
    pallas_call x10 -> x11, Pallas kernels: 9.05 us -> 10.8 us  [call(): pl.pallas_call(body, out_shape=out[0] if one else out, in_specs=ins or [V...]
  transfers between devices with their start and end apart: 2 -> 3, of which waited for: 1 -> 2; matrix products, arithmetic and copies ran while one was open for 0% -> 0% of each run, Pallas kernels for 2% -> 3%
where the time goes in v13:
time: 126 us; the launch traced here: 125 us
  blocking collectives  75.3 us (60%)
  starting transfers between devices  24.6 us (20%)
  waiting for transfers between devices  14 us (11%)
  Pallas kernels  10.8 us (9%)
    all_to_all x6, blocking collectives, exchange(): lax.all_to_all(split_up, axis, 0, 0, tiled=True).reshape(pieces.shape)  75.3 us
    all_to_all x1, starting transfers between devices, exchange(): lax.all_to_all(split_up, axis, 0, 0, tiled=True).reshape(pieces.shape)  14.3 us
    pallas_call x11, Pallas kernels, call(): pl.pallas_call(body, out_shape=out[0] if one else out, in_specs=ins or [V...  10.8 us
    ppermute x1, waiting for transfers between devices, swapped(): lax.ppermute(block, 'col', [(c, (c + (2 if c % 2 else -2)) % N_COL) for c...  8.27 us
    ppermute x1, starting transfers between devices, swapped(): lax.ppermute(block, 'col', [(c, (c + (2 if c % 2 else -2)) % N_COL) for c...  5.81 us
    all_to_all x1, waiting for transfers between devices, exchange(): lax.all_to_all(split_up, axis, 0, 0, tiled=True).reshape(pieces.shape)  5.7 us
    ppermute x1, starting transfers between devices, swapped_back(): lax.ppermute(block, 'col', [(c, (c + (-2 if c % 2 else 2)) % N_COL) for c...  4.47 us
  transfers between devices with their start and end apart: 3, of which 2 were waited for; matrix products, arithmetic and copies ran while one was open for 0% of the time, Pallas kernels for 3%

profile of v13, /device:TPU:1, one launch (start us, length us, event | category | flops | bytes accessed | tf_op | source)
XLA Modules:
  0.0 125.4 jit_solution(4374932075555457724)
XLA Ops:
  0.6 1.5 %shard_map.41 = f32[576,128]{1,0:T(8,128)S(1)} custom-call(f32[256,512]{1,0:T(8,128)} %matrix.3), custom_call_target="tpu_custom_call" | custom-call | flops 100663296 | bytes 819200 | tf_op jit(solution)/shard_map/pallas_call | solution.py:274
  2.1 13.0 %all_to_all.35 = f32[8,72,128]{2,1,0:T(8,128)S(1)} all-to-all(f32[8,72,128]{2,1,0:T(8,128)S(1)} %bitcast.20), channel_id=1, replica_groups=mesh['col'=8,'zl'=2,'y'=8,'x'=4] {'zl','x'}, dimensions={0} | all-to-all | bytes 589824 | tf_op jit(solution)/shard_map/all_to_all | solution.py:305
  15.1 16.5 %all_to_all.36 = f32[8,72,128]{2,1,0:T(8,128)S(1)} all-to-all(f32[8,72,128]{2,1,0:T(8,128)S(1)} %bitcast.22), channel_id=1, replica_groups=mesh['col'=8,'zl'=2,'y'=8,'x'=4] {'y'}, dimensions={0} | all-to-all | bytes 589824 | tf_op jit(solution)/shard_map/all_to_all | solution.py:305
  31.6 0.0 copy-start
  31.6 0.1 shard_map.43
  31.7 9.8 %all_to_all.37 = f32[8,64,128]{2,1,0:T(8,128)S(1)} all-to-all(f32[8,64,128]{2,1,0:T(8,128)S(1)} %bitcast.24), channel_id=1, replica_groups=mesh['col'=8,'zl'=2,'y'=8,'x'=4] {'zl','x'}, dimensions={0} | all-to-all | bytes 524288 | tf_op jit(solution)/shard_map/all_to_all | solution.py:305
  41.5 0.0 copy-done
  41.5 0.0 copy-start.1
  41.5 1.3 %shard_map.45 = f32[256,256]{1,0:T(8,128)S(1)} custom-call(f32[256,512]{1,0:T(8,128)S(1)} %copy-done, f32[512,128]{1,0:T(8,128)S(1)} %bitcast.26), custom_call_target="tpu_custom_call" | custom-call | flops 503316480 | bytes 1048576 | tf_op jit(solution)/shard_map/pallas_call | solution.py:274
  42.8 5.8 %collective-permute-start = (f32[256,256]{1,0:T(8,128)S(1)}, f32[256,256]{1,0:T(8,128)S(1)}, u32[]{:S(2)}, u32[]{:S(2)}) collective-permute-start(f32[256,256]{1,0:T(8,128)S(1)} %shard_map.45), channel_id=1, source_target_pairs={{0,384},{64,192},{128,0},{192,320},{256,128},{320,448},{384,256},{... | collective-permute-start | bytes 786440 | tf_op jit(solution)/shard_map/ppermute | solution.py:289
  48.6 0.0 copy-done.1
  48.7 2.3 %shard_map.44 = (f32[256,256]{1,0:T(8,128)S(1)}, f32[256,256]{1,0:T(8,128)S(1)}, f32[32,128]{1,0:T(8,128)S(1)}) custom-call(f32[256,512]{1,0:T(8,128)S(1)} %copy-done, f32[512,128]{1,0:T(8,128)S(1)} %bitcast.27, s32[16]{0:T(128)S(1)} %copy-done.1), custom_call_target="tpu_custom_call" | custom-call | flops 603979776 | bytes 1327168 | tf_op jit(solution)/shard_map/pallas_call | solution.py:274
  50.9 8.3 %collective-permute-done.guest = f32[256,256]{1,0:T(8,128)S(1)} collective-permute-done((f32[256,256]{1,0:T(8,128)S(1)}, f32[256,256]{1,0:T(8,128)S(1)}, u32[]{:S(2)}, u32[]{:S(2)}) %collective-permute-start) | collective-permute-done | bytes 262176 | tf_op jit(solution)/shard_map/ppermute | solution.py:289
  59.2 0.4 shard_map.46
  59.6 10.3 %all_to_all.38 = f32[8,136,128]{2,1,0:T(8,128)S(1)} all-to-all(f32[8,136,128]{2,1,0:T(8,128)S(1)} %bitcast.15), channel_id=1, replica_groups=mesh['col'=8,'zl'=2,'y'=8,'x'=4] {'zl','x'}, dimensions={0} | all-to-all | bytes 1114112 | tf_op jit(solution)/shard_map/all_to_all | solution.py:305
  70.0 15.4 %all_to_all.39 = f32[8,136,128]{2,1,0:T(8,128)S(1)} all-to-all(f32[8,136,128]{2,1,0:T(8,128)S(1)} %bitcast.17), channel_id=1, replica_groups=mesh['col'=8,'zl'=2,'y'=8,'x'=4] {'y'}, dimensions={0} | all-to-all | bytes 1114112 | tf_op jit(solution)/shard_map/all_to_all | solution.py:305
  85.5 10.3 %all_to_all.40 = f32[8,136,128]{2,1,0:T(8,128)S(1)} all-to-all(f32[8,136,128]{2,1,0:T(8,128)S(1)} %bitcast.19), channel_id=1, replica_groups=mesh['col'=8,'zl'=2,'y'=8,'x'=4] {'zl','x'}, dimensions={0} | all-to-all | bytes 1114112 | tf_op jit(solution)/shard_map/all_to_all | solution.py:305
  95.8 3.0 %shard_map.49 = (f32[256,256]{1,0:T(8,128)S(1)}, f32[32,128]{1,0:T(8,128)}, f32[256,256]{1,0:T(8,128)S(1)}, f32[256,256]{1,0:T(8,128)S(1)}) custom-call(f32[256,256]{1,0:T(8,128)S(1)} %get-tuple-element.12.keep, f32[256,256]{1,0:T(8,128)S(1)} %collective-permute-done.guest, f32[1088,128]{1,0:T(8,128)S(1)} %bitcast.25), custom_call_target="tpu_custom_call" | custom-call | flops 1610612736 | bytes 1884160 | tf_op jit(solution)/shard_map/pallas_call | solution.py:274
  98.8 4.5 %collective-permute-start.1 = (f32[256,256]{1,0:T(8,128)S(1)}, f32[256,256]{1,0:T(8,128)S(1)}, u32[]{:S(2)}, u32[]{:S(2)}) collective-permute-start(f32[256,256]{1,0:T(8,128)S(1)} %get-tuple-element.14), channel_id=1, source_target_pairs={{0,128},{64,448},{128,256},{192,64},{256,384},{320,192},{384,0},{4... | collective-permute-start | bytes 786440 | tf_op jit(solution)/shard_map/ppermute | solution.py:295
  103.2 14.3 %all-to-all-start.6 = ((f32[8,4,128]{2,1,0:T(4,128)}), f32[8,4,128]{2,1,0:T(4,128)S(1)}, u32[]{:S(2)}, u32[]{:S(2)}) async-start(f32[8,4,128]{2,1,0:T(4,128)} %bitcast.12), calls=%async_computation.6 | async-start | bytes 32768 | tf_op jit(solution)/shard_map/all_to_all | solution.py:305
  117.6 1.4 %shard_map.50.begun = f32[256,512]{1,0:T(8,128)} custom-call(f32[256,256]{1,0:T(8,128)S(1)} %get-tuple-element.12.keep, f32[256,256]{1,0:T(8,128)S(1)} %collective-permute-done.guest, f32[256,256]{1,0:T(8,128)S(1)} %get-tuple-element.16.x_in, f32[256,256]{1,0:T(8,128)S(1)} %get-tuple-element.17.z_in), custom_call_target="tpu_custom_call" | custom-call | flops 201326592 | bytes 1572864 | tf_op jit(solution)/shard_map/pallas_call | solution.py:274
  118.9 5.7 %all-to-all-done.6 = f32[8,4,128]{2,1,0:T(4,128)S(1)} async-done(((f32[8,4,128]{2,1,0:T(4,128)}), f32[8,4,128]{2,1,0:T(4,128)S(1)}, u32[]{:S(2)}, u32[]{:S(2)}) %all-to-all-start.6) | async-done | bytes 16416 | tf_op jit(solution)/shard_map/all_to_all | solution.py:305
  124.7 0.0 collective-permute-done.1.back
  124.7 0.7 shard_map.51
  (3 shorter events, 0.1 us)
Async XLA Ops:
  31.6 10.0 %copy-start = (f32[256,512]{1,0:T(8,128)S(1)}, f32[256,512]{1,0:T(8,128)}, u32[]{:S(2)}) copy-start(f32[256,512]{1,0:T(8,128)} %matrix.3) | copy-start | bytes 1572868
  41.5 7.1 %copy-start.1 = (s32[16]{0:T(128)S(1)}, s32[16]{0:T(128)}, u32[]{:S(2)}) copy-start(s32[16]{0:T(128)} %seats.1) | copy-start | bytes 196
  42.8 16.4 %collective-permute-start = (f32[256,256]{1,0:T(8,128)S(1)}, f32[256,256]{1,0:T(8,128)S(1)}, u32[]{:S(2)}, u32[]{:S(2)}) collective-permute-start(f32[256,256]{1,0:T(8,128)S(1)} %shard_map.45), channel_id=1, source_target_pairs={{0,384},{64,192},{128,0},{192,320},{256,128},{320,448},{384,256},{... | collective-permute-start | bytes 786440 | tf_op jit(solution)/shard_map/ppermute | solution.py:289
  98.8 25.9 %collective-permute-start.1 = (f32[256,256]{1,0:T(8,128)S(1)}, f32[256,256]{1,0:T(8,128)S(1)}, u32[]{:S(2)}, u32[]{:S(2)}) collective-permute-start(f32[256,256]{1,0:T(8,128)S(1)} %get-tuple-element.14), channel_id=1, source_target_pairs={{0,128},{64,448},{128,256},{192,64},{256,384},{320,192},{384,0},{4... | collective-permute-start | bytes 786440 | tf_op jit(solution)/shard_map/ppermute | solution.py:295
  103.2 21.4 %all-to-all-start.6 = ((f32[8,4,128]{2,1,0:T(4,128)}), f32[8,4,128]{2,1,0:T(4,128)S(1)}, u32[]{:S(2)}, u32[]{:S(2)}) async-start(f32[8,4,128]{2,1,0:T(4,128)} %bitcast.12), calls=%async_computation.6 | async-start | bytes 32768 | tf_op jit(solution)/shard_map/all_to_all | solution.py:305

commit v14 on v13

--- a/solution.py
+++ b/solution.py
@@ -185,7 +185,7 @@
     return ref.at[:, pl.ds(pl.multiple_of(odd * W, W), W)]
 
 
-def second(total_rows, keep, guest, got, new_guest, sums, x_out, z_out):
+def second(total_rows, keep, guest, got, new_guest, sums_out, x_out, z_out, sums, done):
     crosses = from_wide(got, 0)
     grams = from_wide(got, 64)
     rows, cols = square_index()
@@ -203,7 +203,6 @@
     z_guest, z = roots(s_guest, s_keep)
     zs, zs_guest = split(z), split(z_guest)
     z_out[...] = z
-    new_guest[...] = product(split(mixed_guest), zs_guest)
     cross = split(crosses)
     flipped = grams.T
     of_keep = split(jnp.where(rows <= cols, grams, flipped))
@@ -227,6 +226,10 @@
     tile = jnp.maximum(jnp.concatenate(four + four, axis=0) / total_rows, 0.0)
     for r in range(4 * N_COL // 8):
         sums[8 * r : 8 * r + 8, :] = tile
+    copy = pltpu.make_async_copy(sums, sums_out, done)
+    copy.start()
+    new_guest[...] = product(split(mixed_guest), zs_guest)
+    copy.wait()
 
 
 def second_keep(keep, guest, x_in, z_in, final, kept, done):
@@ -340,6 +343,8 @@
         (4 * N_COL, 128),
         (W, W),
         (W, W),
+        outs=[VMEM, HBM, VMEM, VMEM],
+        scratch=[pltpu.VMEM((4 * N_COL, 128), jnp.float32), pltpu.SemaphoreType.DMA],
     )(keep, guest, got)
     begun = local(
         second_keep,

time: 126 us -> 126 us (level)
  no operation moved by 1% of the time
where the time goes in v14:
time: 126 us; the launch traced here: 125 us
  blocking collectives  75.3 us (60%)
  starting transfers between devices  24.6 us (20%)
  waiting for transfers between devices  14 us (11%)
  Pallas kernels  10.8 us (9%)
    all_to_all x6, blocking collectives, exchange(): lax.all_to_all(split_up, axis, 0, 0, tiled=True).reshape(pieces.shape)  75.3 us
    all_to_all x1, starting transfers between devices, exchange(): lax.all_to_all(split_up, axis, 0, 0, tiled=True).reshape(pieces.shape)  14.3 us
    pallas_call x11, Pallas kernels, call(): pl.pallas_call(body, out_shape=out[0] if one else out, in_specs=ins or [V...  10.8 us
    ppermute x1, waiting for transfers between devices, swapped(): lax.ppermute(block, 'col', [(c, (c + (2 if c % 2 else -2)) % N_COL) for c...  8.27 us
    ppermute x1, starting transfers between devices, swapped(): lax.ppermute(block, 'col', [(c, (c + (2 if c % 2 else -2)) % N_COL) for c...  5.81 us
    all_to_all x1, waiting for transfers between devices, exchange(): lax.all_to_all(split_up, axis, 0, 0, tiled=True).reshape(pieces.shape)  5.7 us
    ppermute x1, starting transfers between devices, swapped_back(): lax.ppermute(block, 'col', [(c, (c + (-2 if c % 2 else 2)) % N_COL) for c...  4.48 us
  transfers between devices with their start and end apart: 3, of which 2 were waited for; matrix products, arithmetic and copies ran while one was open for 0% of the time, Pallas kernels for 3%

profile of v14, /device:TPU:1, one launch (start us, length us, event | category | flops | bytes accessed | tf_op | source)
XLA Modules:
  0.0 125.4 jit_solution(4504632287174067954)
XLA Ops:
  0.6 1.5 %shard_map.41 = f32[576,128]{1,0:T(8,128)S(1)} custom-call(f32[256,512]{1,0:T(8,128)} %matrix.3), custom_call_target="tpu_custom_call" | custom-call | flops 100663296 | bytes 819200 | tf_op jit(solution)/shard_map/pallas_call | solution.py:277
  2.1 13.0 %all_to_all.35 = f32[8,72,128]{2,1,0:T(8,128)S(1)} all-to-all(f32[8,72,128]{2,1,0:T(8,128)S(1)} %bitcast.20), channel_id=1, replica_groups=mesh['col'=8,'zl'=2,'y'=8,'x'=4] {'zl','x'}, dimensions={0} | all-to-all | bytes 589824 | tf_op jit(solution)/shard_map/all_to_all | solution.py:308
  15.1 16.5 %all_to_all.36 = f32[8,72,128]{2,1,0:T(8,128)S(1)} all-to-all(f32[8,72,128]{2,1,0:T(8,128)S(1)} %bitcast.22), channel_id=1, replica_groups=mesh['col'=8,'zl'=2,'y'=8,'x'=4] {'y'}, dimensions={0} | all-to-all | bytes 589824 | tf_op jit(solution)/shard_map/all_to_all | solution.py:308
  31.6 0.0 copy-start
  31.6 0.1 shard_map.43
  31.7 9.8 %all_to_all.37 = f32[8,64,128]{2,1,0:T(8,128)S(1)} all-to-all(f32[8,64,128]{2,1,0:T(8,128)S(1)} %bitcast.24), channel_id=1, replica_groups=mesh['col'=8,'zl'=2,'y'=8,'x'=4] {'zl','x'}, dimensions={0} | all-to-all | bytes 524288 | tf_op jit(solution)/shard_map/all_to_all | solution.py:308
  41.5 0.0 copy-done
  41.5 0.0 copy-start.1
  41.5 1.3 %shard_map.45 = f32[256,256]{1,0:T(8,128)S(1)} custom-call(f32[256,512]{1,0:T(8,128)S(1)} %copy-done, f32[512,128]{1,0:T(8,128)S(1)} %bitcast.26), custom_call_target="tpu_custom_call" | custom-call | flops 503316480 | bytes 1048576 | tf_op jit(solution)/shard_map/pallas_call | solution.py:277
  42.8 5.8 %collective-permute-start = (f32[256,256]{1,0:T(8,128)S(1)}, f32[256,256]{1,0:T(8,128)S(1)}, u32[]{:S(2)}, u32[]{:S(2)}) collective-permute-start(f32[256,256]{1,0:T(8,128)S(1)} %shard_map.45), channel_id=1, source_target_pairs={{0,384},{64,192},{128,0},{192,320},{256,128},{320,448},{384,256},{... | collective-permute-start | bytes 786440 | tf_op jit(solution)/shard_map/ppermute | solution.py:292
  48.6 0.0 copy-done.1
  48.7 2.3 %shard_map.44 = (f32[256,256]{1,0:T(8,128)S(1)}, f32[256,256]{1,0:T(8,128)S(1)}, f32[32,128]{1,0:T(8,128)S(1)}) custom-call(f32[256,512]{1,0:T(8,128)S(1)} %copy-done, f32[512,128]{1,0:T(8,128)S(1)} %bitcast.27, s32[16]{0:T(128)S(1)} %copy-done.1), custom_call_target="tpu_custom_call" | custom-call | flops 603979776 | bytes 1327168 | tf_op jit(solution)/shard_map/pallas_call | solution.py:277
  50.9 8.3 %collective-permute-done.guest = f32[256,256]{1,0:T(8,128)S(1)} collective-permute-done((f32[256,256]{1,0:T(8,128)S(1)}, f32[256,256]{1,0:T(8,128)S(1)}, u32[]{:S(2)}, u32[]{:S(2)}) %collective-permute-start) | collective-permute-done | bytes 262176 | tf_op jit(solution)/shard_map/ppermute | solution.py:292
  59.2 0.4 shard_map.46
  59.6 10.3 %all_to_all.38 = f32[8,136,128]{2,1,0:T(8,128)S(1)} all-to-all(f32[8,136,128]{2,1,0:T(8,128)S(1)} %bitcast.15), channel_id=1, replica_groups=mesh['col'=8,'zl'=2,'y'=8,'x'=4] {'zl','x'}, dimensions={0} | all-to-all | bytes 1114112 | tf_op jit(solution)/shard_map/all_to_all | solution.py:308
  70.0 15.4 %all_to_all.39 = f32[8,136,128]{2,1,0:T(8,128)S(1)} all-to-all(f32[8,136,128]{2,1,0:T(8,128)S(1)} %bitcast.17), channel_id=1, replica_groups=mesh['col'=8,'zl'=2,'y'=8,'x'=4] {'y'}, dimensions={0} | all-to-all | bytes 1114112 | tf_op jit(solution)/shard_map/all_to_all | solution.py:308
  85.5 10.3 %all_to_all.40 = f32[8,136,128]{2,1,0:T(8,128)S(1)} all-to-all(f32[8,136,128]{2,1,0:T(8,128)S(1)} %bitcast.19), channel_id=1, replica_groups=mesh['col'=8,'zl'=2,'y'=8,'x'=4] {'zl','x'}, dimensions={0} | all-to-all | bytes 1114112 | tf_op jit(solution)/shard_map/all_to_all | solution.py:308
  95.8 3.0 %shard_map.49 = (f32[256,256]{1,0:T(8,128)S(1)}, f32[32,128]{1,0:T(8,128)}, f32[256,256]{1,0:T(8,128)S(1)}, f32[256,256]{1,0:T(8,128)S(1)}) custom-call(f32[256,256]{1,0:T(8,128)S(1)} %get-tuple-element.12.keep, f32[256,256]{1,0:T(8,128)S(1)} %collective-permute-done.guest, f32[1088,128]{1,0:T(8,128)S(1)} %bitcast.25), custom_call_target="tpu_custom_call" | custom-call | flops 1610612736 | bytes 1884160 | tf_op jit(solution)/shard_map/pallas_call | solution.py:277
  98.8 4.5 %collective-permute-start.1 = (f32[256,256]{1,0:T(8,128)S(1)}, f32[256,256]{1,0:T(8,128)S(1)}, u32[]{:S(2)}, u32[]{:S(2)}) collective-permute-start(f32[256,256]{1,0:T(8,128)S(1)} %get-tuple-element.14), channel_id=1, source_target_pairs={{0,128},{64,448},{128,256},{192,64},{256,384},{320,192},{384,0},{4... | collective-permute-start | bytes 786440 | tf_op jit(solution)/shard_map/ppermute | solution.py:298
  103.3 14.3 %all-to-all-start.6 = ((f32[8,4,128]{2,1,0:T(4,128)}), f32[8,4,128]{2,1,0:T(4,128)S(1)}, u32[]{:S(2)}, u32[]{:S(2)}) async-start(f32[8,4,128]{2,1,0:T(4,128)} %bitcast.12), calls=%async_computation.6 | async-start | bytes 32768 | tf_op jit(solution)/shard_map/all_to_all | solution.py:308
  117.6 1.4 %shard_map.50.begun = f32[256,512]{1,0:T(8,128)} custom-call(f32[256,256]{1,0:T(8,128)S(1)} %get-tuple-element.12.keep, f32[256,256]{1,0:T(8,128)S(1)} %collective-permute-done.guest, f32[256,256]{1,0:T(8,128)S(1)} %get-tuple-element.16.x_in, f32[256,256]{1,0:T(8,128)S(1)} %get-tuple-element.17.z_in), custom_call_target="tpu_custom_call" | custom-call | flops 201326592 | bytes 1572864 | tf_op jit(solution)/shard_map/pallas_call | solution.py:277
  118.9 5.7 %all-to-all-done.6 = f32[8,4,128]{2,1,0:T(4,128)S(1)} async-done(((f32[8,4,128]{2,1,0:T(4,128)}), f32[8,4,128]{2,1,0:T(4,128)S(1)}, u32[]{:S(2)}, u32[]{:S(2)}) %all-to-all-start.6) | async-done | bytes 16416 | tf_op jit(solution)/shard_map/all_to_all | solution.py:308
  124.7 0.0 collective-permute-done.1.back
  124.7 0.7 shard_map.51
  (3 shorter events, 0.1 us)
Async XLA Ops:
  31.6 10.0 %copy-start = (f32[256,512]{1,0:T(8,128)S(1)}, f32[256,512]{1,0:T(8,128)}, u32[]{:S(2)}) copy-start(f32[256,512]{1,0:T(8,128)} %matrix.3) | copy-start | bytes 1572868
  41.5 7.1 %copy-start.1 = (s32[16]{0:T(128)S(1)}, s32[16]{0:T(128)}, u32[]{:S(2)}) copy-start(s32[16]{0:T(128)} %seats.1) | copy-start | bytes 196
  42.8 16.4 %collective-permute-start = (f32[256,256]{1,0:T(8,128)S(1)}, f32[256,256]{1,0:T(8,128)S(1)}, u32[]{:S(2)}, u32[]{:S(2)}) collective-permute-start(f32[256,256]{1,0:T(8,128)S(1)} %shard_map.45), channel_id=1, source_target_pairs={{0,384},{64,192},{128,0},{192,320},{256,128},{320,448},{384,256},{... | collective-permute-start | bytes 786440 | tf_op jit(solution)/shard_map/ppermute | solution.py:292
  98.8 25.9 %collective-permute-start.1 = (f32[256,256]{1,0:T(8,128)S(1)}, f32[256,256]{1,0:T(8,128)S(1)}, u32[]{:S(2)}, u32[]{:S(2)}) collective-permute-start(f32[256,256]{1,0:T(8,128)S(1)} %get-tuple-element.14), channel_id=1, source_target_pairs={{0,128},{64,448},{128,256},{192,64},{256,384},{320,192},{384,0},{4... | collective-permute-start | bytes 786440 | tf_op jit(solution)/shard_map/ppermute | solution.py:298
  103.3 21.4 %all-to-all-start.6 = ((f32[8,4,128]{2,1,0:T(4,128)}), f32[8,4,128]{2,1,0:T(4,128)S(1)}, u32[]{:S(2)}, u32[]{:S(2)}) async-start(f32[8,4,128]{2,1,0:T(4,128)} %bitcast.12), calls=%async_computation.6 | async-start | bytes 32768 | tf_op jit(solution)/shard_map/all_to_all | solution.py:308

commit v15 on v13

--- a/solution.py
+++ b/solution.py
@@ -13,8 +13,8 @@
 N_COL = 8
 ZL, Y, X = 2, 8, 4
 EIGHT = 8
-NARROW = 72
-WIDE = 136
+NARROW = 66
+WIDE = 129
 LOADS = 8
 LIMIT = 32 * 1024 * 1024
 LOAD_LIMIT = 56000000
@@ -90,9 +90,8 @@
         at = NARROW * r
         out[at : at + 64, :] = cross[64 * r : 64 * r + 64]
         half = (r % 4) // 2
-        pair = [norm_keep[:, 128 * half : 128 * half + 128]]
-        pair.append(norm_move[:, 128 * (r // 4) : 128 * (r // 4) + 128])
-        out[at + 64 : at + 72, :] = jnp.concatenate(pair * 4, axis=0)
+        out[at + 64 : at + 65, :] = norm_keep[:, 128 * half : 128 * half + 128]
+        out[at + 65 : at + 66, :] = norm_move[:, 128 * (r // 4) : 128 * (r // 4) + 128]
 
 
 def square_index():
@@ -110,12 +109,11 @@
     rows, cols = square_index()
     grams = stacked(jnp.where(rows <= cols, gram_keep[...], product(parts, parts, 0, 0)))
     norms = column_squares(guest[...])
-    norms = jnp.concatenate([norms[:, :128], norms[:, 128:]] * 4, axis=0)
     for r in range(EIGHT):
         at = WIDE * r
         out[at : at + 64, :] = cross[64 * r : 64 * r + 64]
         out[at + 64 : at + 128, :] = grams[64 * r : 64 * r + 64]
-        out[at + 128 : at + 136, :] = norms
+        out[at + 128 : at + 129, :] = norms[:, 128 * (r // 4) : 128 * (r // 4) + 128]
 
 
 def added(got, size):
@@ -178,7 +176,8 @@
 
 
 def guest_squares(got):
-    return jnp.concatenate([got[128:129, :], got[129:130, :]], axis=1)
+    at = 4 * WIDE + 128
+    return jnp.concatenate([got[128:129, :], got[at : at + 1, :]], axis=1)
 
 
 def half_of(ref, odd):
@@ -301,7 +300,10 @@
 
 
 def exchange(pieces, axis):
-    split_up = pieces.reshape(lax.axis_size(axis), -1, 128)
+    n = lax.axis_size(axis)
+    rows = pieces.shape[0] // n
+    shape = (n, rows, 128) if rows % 4 == 0 else (n, 1, rows * 128)
+    split_up = pieces.reshape(shape)
     return lax.all_to_all(split_up, axis, 0, 0, tiled=True).reshape(pieces.shape)
 
 

time: 126 us -> 126 us (level)
  starting transfers between devices: 24.6 us -> 27.3 us
  blocking collectives: 75.3 us -> 72.8 us
    all_to_all x1, starting transfers between devices: 14.3 us -> 17.1 us  [exchange(): lax.all_to_all(split_up, axis, 0, 0, tiled=True).reshape(pieces.shape)]
    all_to_all x6, blocking collectives: 75.3 us -> 72.8 us  [exchange(): lax.all_to_all(split_up, axis, 0, 0, tiled=True).reshape(pieces.shape)]
where the time goes in v15:
time: 126 us
  blocking collectives  72.8 us (58%)
  starting transfers between devices  27.3 us (22%)
  waiting for transfers between devices  14 us (11%)
  Pallas kernels  10.8 us (9%)
    all_to_all x6, blocking collectives, exchange(): lax.all_to_all(split_up, axis, 0, 0, tiled=True).reshape(pieces.shape)  72.8 us
    all_to_all x1, starting transfers between devices, exchange(): lax.all_to_all(split_up, axis, 0, 0, tiled=True).reshape(pieces.shape)  17.1 us
    pallas_call x11, Pallas kernels, call(): pl.pallas_call(body, out_shape=out[0] if one else out, in_specs=ins or [V...  10.8 us
    ppermute x1, waiting for transfers between devices, swapped(): lax.ppermute(block, 'col', [(c, (c + (2 if c % 2 else -2)) % N_COL) for c...  8.28 us
    ppermute x1, starting transfers between devices, swapped(): lax.ppermute(block, 'col', [(c, (c + (2 if c % 2 else -2)) % N_COL) for c...  5.81 us
    all_to_all x1, waiting for transfers between devices, exchange(): lax.all_to_all(split_up, axis, 0, 0, tiled=True).reshape(pieces.shape)  5.7 us
    ppermute x1, starting transfers between devices, swapped_back(): lax.ppermute(block, 'col', [(c, (c + (-2 if c % 2 else 2)) % N_COL) for c...  4.41 us
  transfers between devices with their start and end apart: 3, of which 2 were waited for; matrix products, arithmetic and copies ran while one was open for 0% of the time, Pallas kernels for 3%

profile of v15, /device:TPU:1, one launch (start us, length us, event | category | flops | bytes accessed | tf_op | source)
XLA Modules:
  0.0 125.6 jit_solution(914963599909278082)
XLA Ops:
  0.6 1.5 %shard_map.41 = f32[528,128]{1,0:T(8,128)S(1)} custom-call(f32[256,512]{1,0:T(8,128)} %matrix.3), custom_call_target="tpu_custom_call" | custom-call | flops 100663296 | bytes 794624 | tf_op jit(solution)/shard_map/pallas_call | solution.py:273
  2.1 12.9 %all_to_all.35 = f32[8,1,8448]{2,1,0:T(1,128)S(1)} all-to-all(f32[8,1,8448]{2,1,0:T(1,128)S(1)} %bitcast.20), channel_id=1, replica_groups=mesh['col'=8,'zl'=2,'y'=8,'x'=4] {'zl','x'}, dimensions={0} | all-to-all | bytes 540672 | tf_op jit(solution)/shard_map/all_to_all | solution.py:307
  15.0 16.1 %all_to_all.36 = f32[8,1,8448]{2,1,0:T(1,128)S(1)} all-to-all(f32[8,1,8448]{2,1,0:T(1,128)S(1)} %bitcast.22), channel_id=1, replica_groups=mesh['col'=8,'zl'=2,'y'=8,'x'=4] {'y'}, dimensions={0} | all-to-all | bytes 540672 | tf_op jit(solution)/shard_map/all_to_all | solution.py:307
  31.1 0.0 copy-start
  31.1 0.1 shard_map.43
  31.3 8.6 %all_to_all.37 = f32[8,64,128]{2,1,0:T(8,128)S(1)} all-to-all(f32[8,64,128]{2,1,0:T(8,128)S(1)} %bitcast.24), channel_id=1, replica_groups=mesh['col'=8,'zl'=2,'y'=8,'x'=4] {'zl','x'}, dimensions={0} | all-to-all | bytes 524288 | tf_op jit(solution)/shard_map/all_to_all | solution.py:307
  39.9 0.0 copy-done
  39.9 0.0 copy-start.1
  39.9 1.3 %shard_map.45 = f32[256,256]{1,0:T(8,128)S(1)} custom-call(f32[256,512]{1,0:T(8,128)S(1)} %copy-done, f32[512,128]{1,0:T(8,128)S(1)} %bitcast.26), custom_call_target="tpu_custom_call" | custom-call | flops 503316480 | bytes 1048576 | tf_op jit(solution)/shard_map/pallas_call | solution.py:273
  41.2 5.8 %collective-permute-start = (f32[256,256]{1,0:T(8,128)S(1)}, f32[256,256]{1,0:T(8,128)S(1)}, u32[]{:S(2)}, u32[]{:S(2)}) collective-permute-start(f32[256,256]{1,0:T(8,128)S(1)} %shard_map.45), channel_id=1, source_target_pairs={{0,384},{64,192},{128,0},{192,320},{256,128},{320,448},{384,256},{... | collective-permute-start | bytes 786440 | tf_op jit(solution)/shard_map/ppermute | solution.py:288
  47.0 0.0 copy-done.1
  47.0 2.3 %shard_map.44 = (f32[256,256]{1,0:T(8,128)S(1)}, f32[256,256]{1,0:T(8,128)S(1)}, f32[32,128]{1,0:T(8,128)S(1)}) custom-call(f32[256,512]{1,0:T(8,128)S(1)} %copy-done, f32[512,128]{1,0:T(8,128)S(1)} %bitcast.27, s32[16]{0:T(128)S(1)} %copy-done.1), custom_call_target="tpu_custom_call" | custom-call | flops 603979776 | bytes 1327168 | tf_op jit(solution)/shard_map/pallas_call | solution.py:273
  49.3 8.3 %collective-permute-done.guest = f32[256,256]{1,0:T(8,128)S(1)} collective-permute-done((f32[256,256]{1,0:T(8,128)S(1)}, f32[256,256]{1,0:T(8,128)S(1)}, u32[]{:S(2)}, u32[]{:S(2)}) %collective-permute-start) | collective-permute-done | bytes 262176 | tf_op jit(solution)/shard_map/ppermute | solution.py:288
  57.6 0.4 shard_map.46
  58.0 10.2 %all_to_all.38 = f32[8,1,16512]{2,1,0:T(1,128)S(1)} all-to-all(f32[8,1,16512]{2,1,0:T(1,128)S(1)} %bitcast.15), channel_id=1, replica_groups=mesh['col'=8,'zl'=2,'y'=8,'x'=4] {'zl','x'}, dimensions={0} | all-to-all | bytes 1056768 | tf_op jit(solution)/shard_map/all_to_all | solution.py:307
  68.2 0.1 shard_map.47
  68.3 14.7 %all_to_all.39 = f32[8,1,16512]{2,1,0:T(1,128)S(1)} all-to-all(f32[8,1,16512]{2,1,0:T(1,128)S(1)} %bitcast.17), channel_id=1, replica_groups=mesh['col'=8,'zl'=2,'y'=8,'x'=4] {'y'}, dimensions={0} | all-to-all | bytes 1056768 | tf_op jit(solution)/shard_map/all_to_all | solution.py:307
  83.0 0.1 shard_map.48
  83.1 10.2 %all_to_all.40 = f32[8,1,16512]{2,1,0:T(1,128)S(1)} all-to-all(f32[8,1,16512]{2,1,0:T(1,128)S(1)} %bitcast.19), channel_id=1, replica_groups=mesh['col'=8,'zl'=2,'y'=8,'x'=4] {'zl','x'}, dimensions={0} | all-to-all | bytes 1056768 | tf_op jit(solution)/shard_map/all_to_all | solution.py:307
  93.3 3.0 %shard_map.49 = (f32[256,256]{1,0:T(8,128)S(1)}, f32[32,128]{1,0:T(8,128)}, f32[256,256]{1,0:T(8,128)S(1)}, f32[256,256]{1,0:T(8,128)S(1)}) custom-call(f32[256,256]{1,0:T(8,128)S(1)} %get-tuple-element.12.keep, f32[256,256]{1,0:T(8,128)S(1)} %collective-permute-done.guest, f32[1032,128]{1,0:T(8,128)S(1)} %bitcast.25), custom_call_target="tpu_custom_call" | custom-call | flops 1610612736 | bytes 1855488 | tf_op jit(solution)/shard_map/pallas_call | solution.py:273
  96.3 4.4 %collective-permute-start.1 = (f32[256,256]{1,0:T(8,128)S(1)}, f32[256,256]{1,0:T(8,128)S(1)}, u32[]{:S(2)}, u32[]{:S(2)}) collective-permute-start(f32[256,256]{1,0:T(8,128)S(1)} %get-tuple-element.14), channel_id=1, source_target_pairs={{0,128},{64,448},{128,256},{192,64},{256,384},{320,192},{384,0},{4... | collective-permute-start | bytes 786440 | tf_op jit(solution)/shard_map/ppermute | solution.py:294
  100.7 17.1 %all-to-all-start.6 = ((f32[8,4,128]{2,1,0:T(4,128)}), f32[8,4,128]{2,1,0:T(4,128)S(1)}, u32[]{:S(2)}, u32[]{:S(2)}) async-start(f32[8,4,128]{2,1,0:T(4,128)} %bitcast.12), calls=%async_computation.6 | async-start | bytes 32768 | tf_op jit(solution)/shard_map/all_to_all | solution.py:307
  117.8 1.4 %shard_map.50.begun = f32[256,512]{1,0:T(8,128)} custom-call(f32[256,256]{1,0:T(8,128)S(1)} %get-tuple-element.12.keep, f32[256,256]{1,0:T(8,128)S(1)} %collective-permute-done.guest, f32[256,256]{1,0:T(8,128)S(1)} %get-tuple-element.16.x_in, f32[256,256]{1,0:T(8,128)S(1)} %get-tuple-element.17.z_in), custom_call_target="tpu_custom_call" | custom-call | flops 201326592 | bytes 1572864 | tf_op jit(solution)/shard_map/pallas_call | solution.py:273
  119.1 5.7 %all-to-all-done.6 = f32[8,4,128]{2,1,0:T(4,128)S(1)} async-done(((f32[8,4,128]{2,1,0:T(4,128)}), f32[8,4,128]{2,1,0:T(4,128)S(1)}, u32[]{:S(2)}, u32[]{:S(2)}) %all-to-all-start.6) | async-done | bytes 16416 | tf_op jit(solution)/shard_map/all_to_all | solution.py:307
  124.8 0.0 collective-permute-done.1.back
  124.9 0.7 shard_map.51
  (1 shorter events, 0.0 us)
Async XLA Ops:
  31.1 8.7 %copy-start = (f32[256,512]{1,0:T(8,128)S(1)}, f32[256,512]{1,0:T(8,128)}, u32[]{:S(2)}) copy-start(f32[256,512]{1,0:T(8,128)} %matrix.3) | copy-start | bytes 1572868
  39.9 7.1 %copy-start.1 = (s32[16]{0:T(128)S(1)}, s32[16]{0:T(128)}, u32[]{:S(2)}) copy-start(s32[16]{0:T(128)} %seats.1) | copy-start | bytes 196
  41.2 16.4 %collective-permute-start = (f32[256,256]{1,0:T(8,128)S(1)}, f32[256,256]{1,0:T(8,128)S(1)}, u32[]{:S(2)}, u32[]{:S(2)}) collective-permute-start(f32[256,256]{1,0:T(8,128)S(1)} %shard_map.45), channel_id=1, source_target_pairs={{0,384},{64,192},{128,0},{192,320},{256,128},{320,448},{384,256},{... | collective-permute-start | bytes 786440 | tf_op jit(solution)/shard_map/ppermute | solution.py:288
  96.3 28.6 %collective-permute-start.1 = (f32[256,256]{1,0:T(8,128)S(1)}, f32[256,256]{1,0:T(8,128)S(1)}, u32[]{:S(2)}, u32[]{:S(2)}) collective-permute-start(f32[256,256]{1,0:T(8,128)S(1)} %get-tuple-element.14), channel_id=1, source_target_pairs={{0,128},{64,448},{128,256},{192,64},{256,384},{320,192},{384,0},{4... | collective-permute-start | bytes 786440 | tf_op jit(solution)/shard_map/ppermute | solution.py:294
  100.7 24.1 %all-to-all-start.6 = ((f32[8,4,128]{2,1,0:T(4,128)}), f32[8,4,128]{2,1,0:T(4,128)S(1)}, u32[]{:S(2)}, u32[]{:S(2)}) async-start(f32[8,4,128]{2,1,0:T(4,128)} %bitcast.12), calls=%async_computation.6 | async-start | bytes 32768 | tf_op jit(solution)/shard_map/all_to_all | solution.py:307
